TPU v7x, 128 devices: a whole 4x4x4 slice. The times are simulated.
128 devices in a mesh: section: 2 (over core), dev: 64 (over y, z, x).
Axes of the slice: x: 4, y: 4, z: 4, core: 2. Of those that a mesh axis runs over, the one named last changes fastest.
Arguments:
- inputs: bfloat16 [2, 8192, 1024], P(None, 'dev'), may hold values from -6 to 6
- lengths: int32 [2, 64, 4], P(None, 'dev'), may hold values from 1 to 64, 128 in all within a row
- expand_weight: bfloat16 [1024, 4, 1024], P(None, None, 'section'), may hold values from -0.1875 to 0.1875
- mixing_weight: bfloat16 [1024, 1024], P('section'), may hold values from -0.1875 to 0.1875
- projection: bfloat16 [1024, 256], replicated, may hold values from -0.375 to 0.375
- saved_rows: bfloat16 [2, 8192, 256], P(None, 'dev'), may hold values from -103 to 103
- cluster_ids: int32 [2, 8192], P(None, 'dev'), may hold values from 0 to 4095, as said below
- item_ids: int32 [2, 8192], P(None, 'dev'), may hold values from 0 to 511
- top_table: bfloat16 [4096, 256], P('section'), may hold values from -4 to 4
- codebook: bfloat16 [4096, 512, 256], P('dev', 'section'), may hold values from -4 to 4
Outputs:
- grad_inputs: bfloat16 [2, 8192, 1024], P(None, 'dev')
- grad_expand: float32 [1024, 4, 1024], P('dev', None, 'section')
- grad_mixing: float32 [1024, 1024], P('section', 'dev')
- grad_table: float32 [4096, 256], P(('section', 'dev'))
- grad_codebook: bfloat16 [4096, 512, 256], P('dev', 'section')
Inputs may be any that keep to these rules, and one draw needn't show every extreme that they name: `cluster_ids`: cluster k belongs to owner k // 64. The 128 rows of one device of dev name clusters of one owner at most 4 times, and in each micro-batch one owner is named exactly 4 times by the rows of every device. The 4 lengths of one device sum to 128.
All inputs are finite; a program needn't handle non-finite values.
Results may differ from a plain program's by a relative error of at most 0.014.
Values may be sent and summed in bfloat16 or wider, within the bound.
No kernel may reach another device: no remote copies, remote signals or barrier semaphores. Data moves between devices by JAX's collectives and lax.ppermute only.
A program may use at most 192 MiB of HBM per device.

v0:
```python
import jax
import jax.numpy as jnp
from jax import lax
from jax.sharding import PartitionSpec as P

HEAD_DIM = 128
ITEMS = 512
SEQ_MOST = 64


eps = 1e-05


def combined_all(part, axis, combine):
    gathered = jax.tree.map(lambda a: lax.all_gather(a, axis), part)

    def take(source):
        return jax.tree.map(lambda a: lax.dynamic_index_in_dim(a, source, 0, False), gathered)

    return lax.fori_loop(
        1, lax.axis_size(axis), lambda source, state: combine(state, take(source)), take(0)
    )


def as_sent(shard):
    return jax.tree.map(lambda a: a.astype(jnp.bfloat16) if a.dtype == jnp.float32 else a, shard)


def silu_grad(argument):
    logistic = jax.nn.sigmoid(argument)
    return logistic * (1.0 + argument * (1.0 - logistic))


def seg_mask(lengths_row, count):
    seg_ends = jnp.cumsum(lengths_row, dtype=jnp.int32)
    positions = jnp.arange(count, dtype=jnp.int32)
    segment = jnp.sum(
        (positions[:, None] >= seg_ends[None, :]).astype(jnp.int32), axis=1, dtype=jnp.int32
    )
    same_seq = segment[:, None] == segment[None, :]
    causal = positions[None, :] <= positions[:, None]
    return jnp.where(same_seq & causal, 1.0, 0.0).astype(jnp.float32)


def layer_norm(argument):
    row_mean = jnp.mean(argument, axis=-1, keepdims=True)
    centered = argument - row_mean
    variance = jnp.mean(centered * centered, axis=-1, keepdims=True)
    inverse = lax.rsqrt(variance + eps)
    return (centered * inverse, inverse)


def norm_back(incoming, normed, inverse):
    mean_in = jnp.mean(incoming, axis=-1, keepdims=True)
    mean_dot = jnp.mean(incoming * normed, axis=-1, keepdims=True)
    return (incoming - mean_in - normed * mean_dot) * inverse


def contract_rows(left, right):
    return lax.dot_general(
        left, right, (((0,), (0,)), ((), ())), preferred_element_type=jnp.float32
    )


def contract_cols(left, right):
    return lax.dot_general(
        left, right, (((1,), (1,)), ((), ())), preferred_element_type=jnp.float32
    )


def merge_totals(first, second):
    row_peak = jnp.maximum(first[0], second[0])
    row_total = first[1] * jnp.exp(first[0] - row_peak) + second[1] * jnp.exp(second[0] - row_peak)
    return (row_peak, row_total)


def split_softmax(logits):
    row_peak = jnp.max(logits, axis=1, keepdims=True)
    row_total = jnp.sum(jnp.exp(logits - row_peak), axis=1, keepdims=True)
    row_peak, row_total = combined_all((row_peak, row_total), "section", merge_totals)
    return jnp.exp(logits - row_peak) / row_total


def section_total(partial_sum):
    return lax.psum(partial_sum, "section")


def trunk_part(inputs, seq_mask, expand_weight, mixing_weight, out_grad):
    row_count, model_width = inputs.shape
    col_count = expand_weight.shape[2]
    head_count = col_count // HEAD_DIM
    normed, inverse = layer_norm(inputs.astype(jnp.float32))
    normed_b = normed.astype(jnp.bfloat16)
    flat_in = expand_weight.reshape(model_width, 4 * col_count)
    pre_act = jnp.dot(normed_b, flat_in, preferred_element_type=jnp.float32)
    activated = jax.nn.silu(pre_act).astype(jnp.bfloat16)
    gate_part = activated[:, :col_count].astype(jnp.float32)
    value_heads = activated[:, col_count : 2 * col_count].reshape(row_count, head_count, HEAD_DIM)
    query_heads = activated[:, 2 * col_count : 3 * col_count].reshape(
        row_count, head_count, HEAD_DIM
    )
    key_heads = activated[:, 3 * col_count :].reshape(row_count, head_count, HEAD_DIM)
    scores = jnp.einsum("ihk,jhk->hij", query_heads, key_heads, preferred_element_type=jnp.float32)
    attention = (jax.nn.silu(scores) * seq_mask / SEQ_MOST).astype(jnp.bfloat16)
    mixed_out = jnp.einsum(
        "hij,jhk->ihk", attention, value_heads, preferred_element_type=jnp.float32
    )
    out_normed, inverse_mid = layer_norm(mixed_out)
    normed_flat = out_normed.reshape(row_count, col_count)
    product = (normed_flat * gate_part).astype(jnp.bfloat16)
    grad_product = contract_cols(out_grad, mixing_weight)
    grad_mix = contract_rows(product, out_grad)
    grad_gate = grad_product * normed_flat
    grad_onorm = (grad_product * gate_part).reshape(row_count, head_count, HEAD_DIM)
    grad_mixed = norm_back(grad_onorm, out_normed, inverse_mid).astype(jnp.bfloat16)
    grad_attention = jnp.einsum(
        "ihk,jhk->hij", grad_mixed, value_heads, preferred_element_type=jnp.float32
    )
    grad_values = jnp.einsum(
        "hij,ihk->jhk", attention, grad_mixed, preferred_element_type=jnp.float32
    )
    grad_scores = (grad_attention * silu_grad(scores) * seq_mask / SEQ_MOST).astype(jnp.bfloat16)
    grad_query = jnp.einsum(
        "hij,jhk->ihk", grad_scores, key_heads, preferred_element_type=jnp.float32
    )
    grad_keys = jnp.einsum(
        "hij,ihk->jhk", grad_scores, query_heads, preferred_element_type=jnp.float32
    )
    grad_acts = jnp.concatenate(
        [
            grad_gate,
            grad_values.reshape(row_count, col_count),
            grad_query.reshape(row_count, col_count),
            grad_keys.reshape(row_count, col_count),
        ],
        axis=1,
    )
    grad_pre = (grad_acts * silu_grad(pre_act)).astype(jnp.bfloat16)
    grad_exp = contract_rows(normed_b, grad_pre).reshape(model_width, 4, col_count)
    grad_part = contract_cols(grad_pre, flat_in)
    return (grad_part, grad_exp, grad_mix, normed, inverse)


def body(
    inputs,
    lengths,
    expand_weight,
    mixing_weight,
    projection,
    saved_rows,
    cluster_ids,
    item_ids,
    top_table,
    codebook,
):
    micro_count, row_count, model_width = inputs.shape
    owners = lax.axis_size("dev")
    section_index = lax.axis_index("section")
    half_clusters, head_width = top_table.shape
    local_books, half_items = (codebook.shape[0], codebook.shape[1])
    capacity = 2 * row_count // owners
    slot_count = owners * capacity
    block_rows = 128
    block_count = slot_count // block_rows
    col_count = expand_weight.shape[2]
    cluster_base = section_index * half_clusters
    item_base = section_index * half_items
    grad_expand = jnp.zeros((model_width, 4, col_count), jnp.float32)
    grad_mixing = jnp.zeros((col_count, model_width), jnp.float32)
    grad_table = jnp.zeros((half_clusters, head_width), jnp.float32)
    grad_books = jnp.zeros((local_books * half_items, head_width), jnp.float32)
    input_grads = []
    for micro_index in range(micro_count):
        saved = saved_rows[micro_index]
        targets = cluster_ids[micro_index]
        chosen = item_ids[micro_index]
        top_probs = split_softmax(contract_cols(saved, top_table))
        top_hits = jnp.where(
            jnp.arange(half_clusters, dtype=jnp.int32)[None, :] + cluster_base == targets[:, None],
            1.0,
            0.0,
        )
        top_grad = (top_probs - top_hits).astype(jnp.bfloat16)
        row_top = jnp.dot(top_grad, top_table, preferred_element_type=jnp.float32)
        step_table = contract_rows(top_grad, saved)
        owner_ids = targets // local_books
        owner_marks = (owner_ids[:, None] == jnp.arange(owners, dtype=jnp.int32)[None, :]).astype(
            jnp.int32
        )
        earlier = jnp.cumsum(owner_marks, axis=0, dtype=jnp.int32) - owner_marks
        slot_ids = owner_ids * capacity + jnp.sum(earlier * owner_marks, axis=1, dtype=jnp.int32)
        send_rows = jnp.zeros((slot_count, head_width), jnp.bfloat16).at[slot_ids].set(saved)
        send_codes = (
            jnp.full((slot_count,), -1, jnp.int32)
            .at[slot_ids]
            .set(targets % local_books * ITEMS + chosen)
        )
        got_rows, got_codes = (
            lax.all_to_all(send_rows, "dev", split_axis=0, concat_axis=0, tiled=True),
            lax.all_to_all(send_codes, "dev", split_axis=0, concat_axis=0, tiled=True),
        )
        filled = got_codes >= 0
        local_ids = jnp.where(filled, got_codes // ITEMS, 0)
        item_local = jnp.where(filled, got_codes % ITEMS, -1) - item_base
        id_blocks = local_ids.reshape(block_count, block_rows)

        def leaf_scores(pair):
            book_rows = codebook[pair[1]]
            return jnp.einsum("bid,bd->bi", book_rows, pair[0], preferred_element_type=jnp.float32)

        scores = lax.map(
            leaf_scores, (got_rows.reshape(block_count, block_rows, head_width), id_blocks)
        ).reshape(slot_count, half_items)
        leaf_probs = split_softmax(scores)
        leaf_hits = jnp.where(
            jnp.arange(half_items, dtype=jnp.int32)[None, :] == item_local[:, None], 1.0, 0.0
        )
        leaf_grad = jnp.where(filled[:, None], leaf_probs - leaf_hits, 0.0).astype(jnp.bfloat16)

        def leaf_back(pair):
            book_rows = codebook[pair[1]]
            return jnp.einsum(
                "bi,bid->bd", pair[0], book_rows, preferred_element_type=jnp.float32
            ).astype(jnp.bfloat16)

        back_rows = lax.map(
            leaf_back, (leaf_grad.reshape(block_count, block_rows, half_items), id_blocks)
        ).reshape(slot_count, head_width)
        book_marks = (
            local_ids[:, None] == jnp.arange(local_books, dtype=jnp.int32)[None, :]
        ).astype(jnp.bfloat16)
        weighted = (book_marks[:, :, None] * leaf_grad[:, None, :]).reshape(
            slot_count, local_books * half_items
        )
        grad_books = grad_books + contract_rows(weighted, got_rows)
        returned = lax.all_to_all(
            as_sent(back_rows), "dev", split_axis=0, concat_axis=0, tiled=True
        ).astype(back_rows.dtype)
        row_grad = section_total(row_top + returned[slot_ids].astype(jnp.float32)).astype(
            jnp.bfloat16
        )
        out_grad = contract_cols(row_grad, projection).astype(jnp.bfloat16)
        seq_mask = seg_mask(lengths[micro_index, 0], row_count)
        grad_part, step_expand, step_mixing, normed, inverse = trunk_part(
            inputs[micro_index], seq_mask, expand_weight, mixing_weight, out_grad
        )
        grad_expand = grad_expand + step_expand
        grad_mixing = grad_mixing + step_mixing
        grad_table = grad_table + step_table
        grad_normed = section_total(grad_part)
        input_grads.append(
            (out_grad.astype(jnp.float32) + norm_back(grad_normed, normed, inverse)).astype(
                jnp.bfloat16
            )
        )
    share_expand, share_mixing, share_table = (
        lax.psum_scatter(grad_expand, "dev", scatter_dimension=0, tiled=True),
        lax.psum_scatter(grad_mixing, "dev", scatter_dimension=1, tiled=True),
        lax.psum_scatter(grad_table, "dev", scatter_dimension=0, tiled=True),
    )
    book_grads = grad_books.reshape(local_books, half_items, head_width).astype(jnp.bfloat16)
    return (jnp.stack(input_grads), share_expand, share_mixing, share_table, book_grads)


def solution(mesh):
    return jax.shard_map(
        body,
        mesh=mesh,
        in_specs=(
            P(None, "dev", None),
            P(None, "dev", None),
            P(None, None, "section"),
            P("section", None),
            P(),
            P(None, "dev", None),
            P(None, "dev"),
            P(None, "dev"),
            P("section", None),
            P("dev", "section", None),
        ),
        out_specs=(
            P(None, "dev", None),
            P("dev", None, "section"),
            P("section", "dev"),
            P(("section", "dev"), None),
            P("dev", "section", None),
        ),
        check_vma=False,
    )
```

profile of v0, /device:TPU:0, one launch (start us, length us, event | category | flops | bytes accessed | tf_op | source)
XLA Modules:
  0.0 1472.6 jit_solution(9512386170763901277)
XLA Ops:
  12.2 11.5 all-to-all-start.3
  28.7 4.0 copy.218
  55.0 10.3 all-to-all-start
  70.9 3.8 all-to-all-done
  74.8 6.5 all-to-all-start.1
  83.3 7.9 all-to-all-done.1
  91.2 5.7 all-to-all-start.4
  97.1 39.1 %while.8 = (s32[]{:T(128)}, f32[2,128,256]{2,1,0:T(8,128)S(1)}, s32[2,128]{1,0:T(2,128)S(1)}, bf16[64,256,256]{2,1,0:T(8,128)(2,1)}, bf16[2,128,256]{2,1,0:T(8,128)(2,1)S(1)}, /*index=5*/s32[]{:T(128)}) while((s32[]{:T(128)}, f32[2,128,256]{2,1,0:T(8,128)S(1)}, s32[2,128]{1,0:T(2,128)S(1)}, bf16[64,256,256]{2,1,0:T(8,128)(2,1)}, ...), condition=%wide.region_7.8_spmd, body=%wide.region_6.7_spmd.sunk | while | flops 16778624 | bytes 50927704 | solution.py:211
  97.1 11.4 gather_fusion
  108.5 8.0 fusion.244
  116.6 11.5 gather_fusion
  128.1 8.0 fusion.244
  140.6 39.1 %while.9 = (s32[]{:T(128)}, bf16[2,128,256]{2,1,0:T(8,128)(2,1)S(1)}, bf16[2,128,256]{2,1,0:T(8,128)(2,1)S(1)}, s32[2,128]{1,0:T(2,128)S(1)}, bf16[64,256,256]{2,1,0:T(8,128)(2,1)}, /*index=5*/s32[]{:T(128)}) while((s32[]{:T(128)}, bf16[2,128,256]{2,1,0:T(8,128)(2,1)S(1)}, bf16[2,128,256]{2,1,0:T(8,128)(2,1)S(1)}, s32[2,128]{1,0:T(2,128)S(1)}, ...), condition=%wide.region_11.12_spmd, body=%wide.region_10.11_spmd.sunk | while | flops 16778624 | bytes 50796632 | solution.py:226
  140.7 11.4 gather_fusion.1
  152.1 8.0 fusion.248
  160.2 11.5 gather_fusion.1
  171.6 8.0 fusion.248
  180.4 11.0 all-to-all-start.2
  192.4 39.2 %while.10 = (s32[]{:T(128)}, f32[2,128,256]{2,1,0:T(8,128)S(1)}, s32[2,128]{1,0:T(2,128)S(1)}, bf16[64,256,256]{2,1,0:T(8,128)(2,1)}, bf16[2,128,256]{2,1,0:T(8,128)(2,1)S(1)}, /*index=5*/s32[]{:T(128)}) while((s32[]{:T(128)}, f32[2,128,256]{2,1,0:T(8,128)S(1)}, s32[2,128]{1,0:T(2,128)S(1)}, bf16[64,256,256]{2,1,0:T(8,128)(2,1)}, ...), condition=%wide.region_31.32_spmd, body=%wide.region_30.31_spmd.sunk | while | flops 16778624 | bytes 50927704 | solution.py:211
  192.4 11.5 gather_fusion.2
  204.0 8.0 fusion.253
  212.1 11.4 gather_fusion.2
  223.5 8.0 fusion.253
  236.4 39.2 %while.11 = (s32[]{:T(128)}, bf16[2,128,256]{2,1,0:T(8,128)(2,1)S(1)}, bf16[2,128,256]{2,1,0:T(8,128)(2,1)S(1)}, s32[2,128]{1,0:T(2,128)S(1)}, bf16[64,256,256]{2,1,0:T(8,128)(2,1)}, /*index=5*/s32[]{:T(128)}) while((s32[]{:T(128)}, bf16[2,128,256]{2,1,0:T(8,128)(2,1)S(1)}, bf16[2,128,256]{2,1,0:T(8,128)(2,1)S(1)}, ...), condition=%wide.region_35.36_spmd, body=%wide.region_34.35_spmd.sunk | while | flops 16778624 | bytes 50796632 | solution.py:226
  236.5 11.5 gather_fusion.3
  248.0 8.0 fusion.257
  256.1 11.4 gather_fusion.3
  267.5 8.0 fusion.257
  276.3 10.1 all-to-all-start.5
  290.2 6.1 all-to-all-done.5
  297.9 4.8 all-reduce.8
  315.3 4.5 fusion.167
  322.4 5.8 fusion.60
  328.3 11.9 all-reduce.5.cloned.1.call-done
  342.1 4.0 multiply_convert_fusion
  363.2 4.5 fusion.171
  368.8 8.2 convolution_add_fusion.1
  379.7 3.2 convolution_add_fusion.2
  384.0 4.6 broadcast_multiply_fusion.1
  388.6 15.5 %copy.219 = bf16[32,8,64,256]{3,1,2,0:T(8,128)(2,1)} copy(bf16[32,8,64,256]{3,2,1,0:T(8,128)(2,1)} %bitcast.481) | data formatting | bytes 16777216
  404.3 4.8 broadcast_multiply_fusion
  409.1 15.3 %copy.220 = bf16[32,8,64,256]{3,1,2,0:T(8,128)(2,1)} copy(bf16[32,8,64,256]{3,2,1,0:T(8,128)(2,1)} %bitcast.482) | data formatting | bytes 16777216
  426.7 2.7 convolution_add_fusion.3
  429.5 11.9 fusion.172
  441.4 14.1 fusion.20
  459.2 305.4 %reduce-scatter.4.cloned.1.call-done = f32[16,4,512]{2,0,1:T(8,128)} async-done(((f32[1024,4,512]{2,0,1:T(8,128)}), f32[16,4,512]{2,0,1:T(8,128)}) %reduce-scatter.4.cloned.1.call-update) | async-done | bytes 131088 | tf_op jit(solution)/shard_map/reduce_scatter | solution.py:257
  766.3 348.7 %reduce-scatter.8.cloned.1.call-done = f32[32,256]{1,0:T(8,128)} async-done(((f32[2048,256]{1,0:T(8,128)}), f32[32,256]{1,0:T(8,128)}) %reduce-scatter.8.cloned.1.call-update) | async-done | bytes 32784 | tf_op jit(solution)/shard_map/reduce_scatter | solution.py:259
  1115.0 350.6 %reduce-scatter.6.cloned.1.call-done = f32[512,16]{0,1:T(8,128)} async-done(((f32[512,1024]{0,1:T(8,128)}), f32[512,16]{0,1:T(8,128)}) %reduce-scatter.6.cloned.1.call-update) | async-done | bytes 32784 | tf_op jit(solution)/shard_map/reduce_scatter | solution.py:258
  (361 shorter events, 103.3 us)
Async XLA Ops:
  7.2 17.8 %copy-start = (bf16[2048,256]{1,0:T(8,128)(2,1)S(1)}, bf16[2048,256]{1,0:T(8,128)(2,1)}, u32[]{:S(2)}) copy-start(bf16[2048,256]{1,0:T(8,128)(2,1)} %param.26) | copy-start | bytes 3145732
  7.2 25.4 %copy-start.2 = (bf16[2,128,1024]{2,1,0:T(8,128)(2,1)S(1)}, bf16[2,128,1024]{2,1,0:T(8,128)(2,1)}, u32[]{:S(2)}) copy-start(bf16[2,128,1024]{2,1,0:T(8,128)(2,1)} %param.18) | copy-start | bytes 1572868
  12.2 42.8 %all-to-all-start.3 = ((s32[64,4,1]{1,2,0:T(1,128)}), s32[64,4,1]{1,2,0:T(1,128)S(1)}, u32[]{:S(2)}, u32[]{:S(2)}) async-start(s32[64,4,1]{1,2,0:T(1,128)} %bitcast.68), calls=%async_computation.3 | async-start | bytes 65536 | tf_op jit(solution)/shard_map/all_to_all | solution.py:200
  28.6 14.4 copy-start.6
  32.6 14.2 copy-start.58
  32.7 33.3 %copy-start.17 = (bf16[2,128,256]{2,1,0:T(8,128)(2,1)S(1)}, bf16[2,128,256]{2,1,0:T(8,128)(2,1)}, u32[]{:S(2)}) copy-start(bf16[2,128,256]{2,1,0:T(8,128)(2,1)} %param.23) | copy-start | bytes 393220
  37.2 59.8 %copy-start.23 = (bf16[16,4,8,128]{3,2,1,0:T(8,128)(2,1)}, bf16[16,4,8,128]{3,2,1,0:T(8,128)(2,1)S(1)}, u32[]{:S(2)}) copy-start(bf16[16,4,8,128]{3,2,1,0:T(8,128)(2,1)S(1)} %get-tuple-element.287) | copy-start | bytes 393220
  37.4 28.5 %copy-start.19 = (bf16[128,512]{0,1:T(8,128)(2,1)}, bf16[128,512]{0,1:T(8,128)(2,1)S(1)}, u32[]{:S(2)}) copy-start(bf16[128,512]{0,1:T(8,128)(2,1)S(1)} %copy.212) | copy-start | bytes 393220
  47.4 49.6 %copy-start.21 = (bf16[128,512]{0,1:T(8,128)(2,1)}, bf16[128,512]{0,1:T(8,128)(2,1)S(1)}, u32[]{:S(2)}) copy-start(bf16[128,512]{0,1:T(8,128)(2,1)S(1)} %copy.213) | copy-start | bytes 393220
  48.3 42.9 %copy-start.25 = (bf16[4,128,128]{2,1,0:T(8,128)(2,1)}, bf16[4,128,128]{2,1,0:T(8,128)(2,1)S(1)}, u32[]{:S(2)}) copy-start(bf16[4,128,128]{2,1,0:T(8,128)(2,1)S(1)} %get-tuple-element.324) | copy-start | bytes 393220
  48.6 48.4 %copy-start.32 = (f32[128,4]{0,1:T(4,128)}, f32[128,4]{0,1:T(4,128)S(1)}, u32[]{:S(2)}) copy-start(f32[128,4]{0,1:T(4,128)S(1)} %broadcast_multiply_fusion.7) | copy-start | bytes 6148
  54.9 42.1 %copy-start.26 = (s32[64,4,1]{1,2,0:T(1,128)}, s32[64,4,1]{1,2,0:T(1,128)S(1)}, u32[]{:S(2)}) copy-start(s32[64,4,1]{1,2,0:T(1,128)S(1)} %all-to-all-done.3) | copy-start | bytes 3076
  55.0 19.8 %all-to-all-start = ((s32[64,4,1]{1,2,0:T(1,128)}), s32[64,4,1]{1,2,0:T(1,128)S(1)}, u32[]{:S(2)}, u32[]{:S(2)}) async-start(s32[64,4,1]{1,2,0:T(1,128)} %bitcast.36), calls=%async_computation | async-start | bytes 65536 | tf_op jit(solution)/shard_map/all_to_all | solution.py:200
  74.8 22.3 %copy-start.28 = (s32[64,4,1]{1,2,0:T(1,128)}, s32[64,4,1]{1,2,0:T(1,128)S(1)}, u32[]{:S(2)}) copy-start(s32[64,4,1]{1,2,0:T(1,128)S(1)} %all-to-all-done) | copy-start | bytes 3076
  74.8 16.5 %all-to-all-start.1 = ((bf16[64,4,256]{2,1,0:T(4,128)(2,1)}), bf16[64,4,256]{2,1,0:T(4,128)(2,1)S(1)}, u32[]{:S(2)}, u32[]{:S(2)}) async-start(bf16[64,4,256]{2,1,0:T(4,128)(2,1)} %all_to_all.55), calls=%async_computation.1 | async-start | bytes 262144 | tf_op jit(solution)/shard_map/all_to_all | solution.py:199
  91.2 89.2 %all-to-all-start.4 = ((bf16[64,4,256]{2,1,0:T(4,128)(2,1)}), bf16[64,4,256]{2,1,0:T(4,128)(2,1)}, u32[]{:S(2)}, u32[]{:S(2)}) async-start(bf16[64,4,256]{2,1,0:T(4,128)(2,1)} %all_to_all.63), calls=%async_computation.4 | async-start | bytes 262144 | tf_op jit(solution)/shard_map/all_to_all | solution.py:199
  140.6 51.7 %copy-start.59 = (s32[2,128]{1,0:T(2,128)S(1)}, s32[2,128]{1,0:T(2,128)}, u32[]{:S(2)}) copy-start(s32[2,128]{1,0:T(2,128)} %get-tuple-element.521) | copy-start | bytes 3076
  180.4 95.9 %all-to-all-start.2 = ((bf16[64,4,256]{2,1,0:T(4,128)(2,1)}), bf16[64,4,256]{2,1,0:T(4,128)(2,1)}, u32[]{:S(2)}, u32[]{:S(2)}) async-start(bf16[64,4,256]{2,1,0:T(4,128)(2,1)} %all_to_all.57), calls=%async_computation.2 | async-start | bytes 262144 | tf_op jit(solution)/shard_map/all_to_all | solution.py:236
  192.4 43.5 %copy-start.57 = (s32[2,128]{1,0:T(2,128)S(1)}, s32[2,128]{1,0:T(2,128)}, u32[]{:S(2)}) copy-start(s32[2,128]{1,0:T(2,128)} %get-tuple-element.308) | copy-start | bytes 3076
  192.4 43.5 %copy-start.62 = (pred[2,128]{1,0:T(4,128)(4,1)S(1)}, pred[2,128]{1,0:T(4,128)(4,1)}, u32[]{:S(2)}) copy-start(pred[2,128]{1,0:T(4,128)(4,1)} %broadcast_compare_fusion.8) | copy-start | bytes 772
  236.1 52.3 %copy-start.47 = (s32[2048]{0:T(1024)S(1)}, s32[2048]{0:T(1024)}, u32[]{:S(2)}) copy-start(s32[2048]{0:T(1024)} %iota_add_fusion) | copy-start | bytes 24580
  236.1 52.3 %copy-start.65 = (s32[128]{0:T(128)S(1)}, s32[128]{0:T(128)}, u32[]{:S(2)}) copy-start(s32[128]{0:T(128)} %get-tuple-element.307) | copy-start | bytes 1540
  236.1 52.3 %copy-start.71 = (f32[128]{0:T(128)S(1)}, f32[128]{0:T(128)}, u32[]{:S(2)}) copy-start(f32[128]{0:T(128)} %get-tuple-element.277) | copy-start | bytes 1540
  236.1 52.3 %copy-start.73 = (f32[128]{0:T(128)S(1)}, f32[128]{0:T(128)}, u32[]{:S(2)}) copy-start(f32[128]{0:T(128)} %get-tuple-element.278) | copy-start | bytes 1540
  275.6 21.8 %copy-start.7 = (f32[128,2048]{1,0:T(8,128)S(1)}, f32[128,2048]{1,0:T(8,128)}, u32[]{:S(2)}) copy-start(f32[128,2048]{1,0:T(8,128)} %copy-done.6) | copy-start | bytes 3145732
  275.6 21.8 %copy-start.63 = (s32[128]{0:T(128)S(1)}, s32[128]{0:T(128)}, u32[]{:S(2)}) copy-start(s32[128]{0:T(128)} %get-tuple-element.306) | copy-start | bytes 1540
  275.6 21.8 %copy-start.67 = (f32[128]{0:T(128)S(1)}, f32[128]{0:T(128)}, u32[]{:S(2)}) copy-start(f32[128]{0:T(128)} %get-tuple-element.271) | copy-start | bytes 1540
  275.6 21.8 %copy-start.69 = (f32[128]{0:T(128)S(1)}, f32[128]{0:T(128)}, u32[]{:S(2)}) copy-start(f32[128]{0:T(128)} %get-tuple-element.272) | copy-start | bytes 1540
  276.3 20.0 %all-to-all-start.5 = ((bf16[64,4,256]{2,1,0:T(4,128)(2,1)}), bf16[64,4,256]{2,1,0:T(4,128)(2,1)S(1)}, u32[]{:S(2)}, u32[]{:S(2)}) async-start(bf16[64,4,256]{2,1,0:T(4,128)(2,1)} %all_to_all.65), calls=%async_computation.5 | async-start | bytes 262144 | tf_op jit(solution)/shard_map/all_to_all | solution.py:236
  286.5 53.7 %all-reduce.5.cloned.1.call-start = ((), (), s32[]{:S(2)}) async-start(), calls=%async_computation.9 | async-start | bytes 1048576 | tf_op jit(solution)/shard_map/psum | solution.py:85
  288.5 17.5 %copy-start.9 = (f32[128,4,128]{0,2,1:T(8,128)S(1)}, f32[128,4,128]{0,2,1:T(8,128)}, u32[]{:S(2)}) copy-start(f32[128,4,128]{0,2,1:T(8,128)} %copy-done.8) | copy-start | bytes 786436
  288.5 17.5 %copy-start.31 = (f32[128,4]{0,1:T(4,128)S(1)}, f32[128,4]{0,1:T(4,128)}, u32[]{:S(2)}) copy-start(f32[128,4]{0,1:T(4,128)} %add_rsqrt_fusion.1) | copy-start | bytes 6148
  288.5 17.5 %copy-start.33 = (f32[128,4]{0,1:T(4,128)S(1)}, f32[128,4]{0,1:T(4,128)}, u32[]{:S(2)}) copy-start(f32[128,4]{0,1:T(4,128)} %copy-done.32) | copy-start | bytes 6148
  288.5 18.0 %copy-start.24 = (bf16[16,4,8,128]{3,2,1,0:T(8,128)(2,1)S(1)}, bf16[16,4,8,128]{3,2,1,0:T(8,128)(2,1)}, u32[]{:S(2)}) copy-start(bf16[16,4,8,128]{3,2,1,0:T(8,128)(2,1)} %copy-done.23) | copy-start | bytes 393220
  290.2 17.5 %copy-start.20 = (bf16[128,512]{0,1:T(8,128)(2,1)S(1)}, bf16[128,512]{0,1:T(8,128)(2,1)}, u32[]{:S(2)}) copy-start(bf16[128,512]{0,1:T(8,128)(2,1)} %copy-done.19) | copy-start | bytes 393220
  290.2 17.7 %copy-start.22 = (bf16[128,512]{0,1:T(8,128)(2,1)S(1)}, bf16[128,512]{0,1:T(8,128)(2,1)}, u32[]{:S(2)}) copy-start(bf16[128,512]{0,1:T(8,128)(2,1)} %copy-done.21) | copy-start | bytes 393220
  306.4 16.0 %copy-start.3 = (bf16[2,128,1024]{2,1,0:T(8,128)(2,1)S(1)}, bf16[2,128,1024]{2,1,0:T(8,128)(2,1)}, u32[]{:S(2)}) copy-start(bf16[2,128,1024]{2,1,0:T(8,128)(2,1)} %param.18) | copy-start | bytes 1572868
  306.4 16.0 %copy-start.50 = (f32[128]{0:T(128)S(1)}, f32[128]{0:T(128)}, u32[]{:S(2)}) copy-start(f32[128]{0:T(128)} %copy-done.49) | copy-start | bytes 1540
  315.3 24.9 %copy-start.46 = (f32[128]{0:T(128)S(1)}, f32[128]{0:T(128)}, u32[]{:S(2)}) copy-start(f32[128]{0:T(128)} %broadcast_multiply_fusion.10) | copy-start | bytes 1540
  315.3 24.9 %copy-start.53 = (f32[128]{0:T(128)S(1)}, f32[128]{0:T(128)}, u32[]{:S(2)}) copy-start(f32[128]{0:T(128)} %copy-done.52) | copy-start | bytes 1540
  319.8 135.7 %all-reduce.7.cloned.1.call-start = ((), (), s32[]{:S(2)}) async-start(), calls=%async_computation.10 | async-start | bytes 1048576 | tf_op jit(solution)/shard_map/psum | solution.py:85
  367.7 396.9 %reduce-scatter.4.cloned.1.call-start = ((), (), s32[]{:S(2)}) async-start(), calls=%async_computation.11 | async-start | bytes 8519680 | tf_op jit(solution)/shard_map/reduce_scatter | solution.py:257
  377.1 737.9 %reduce-scatter.8.cloned.1.call-start = ((), (), s32[]{:S(2)}) async-start(), calls=%async_computation.13 | async-start | bytes 2129920 | tf_op jit(solution)/shard_map/reduce_scatter | solution.py:259
  383.0 1082.6 %reduce-scatter.6.cloned.1.call-start = ((), (), s32[]{:S(2)}) async-start(), calls=%async_computation.12 | async-start | bytes 2129920 | tf_op jit(solution)/shard_map/reduce_scatter | solution.py:258
  388.6 15.5 %copy-start.43 = (f32[1,256,1]{1,2,0:T(1,128)S(1)}, f32[1,256,1]{1,2,0:T(1,128)}, u32[]{:S(2)}) copy-start(f32[1,256,1]{1,2,0:T(1,128)} %copy-done.42) | copy-start | bytes 3076
  388.6 15.5 %copy-start.45 = (f32[1,256,1]{1,2,0:T(1,128)S(1)}, f32[1,256,1]{1,2,0:T(1,128)}, u32[]{:S(2)}) copy-start(f32[1,256,1]{1,2,0:T(1,128)} %copy-done.44) | copy-start | bytes 3076
  409.1 15.3 %copy-start.14 = (bf16[64,4,256]{2,1,0:T(4,128)(2,1)S(1)}, bf16[64,4,256]{2,1,0:T(4,128)(2,1)}, u32[]{:S(2)}) copy-start(bf16[64,4,256]{2,1,0:T(4,128)(2,1)} %copy-done.13) | copy-start | bytes 393220
  409.1 16.3 %copy-start.11 = (f32[128,512]{1,0:T(8,128)S(1)}, f32[128,512]{1,0:T(8,128)}, u32[]{:S(2)}) copy-start(f32[128,512]{1,0:T(8,128)} %copy-done.10) | copy-start | bytes 786436
  (38 other events, 188.8 us)
Sparse Core Ops, SparseCore 0:
  319.9 20.1 all-reduce.4
  367.8 25.6 all-reduce.6
  395.9 368.6 reduce-scatter.3
  767.4 347.5 reduce-scatter.7
  1117.9 347.6 reduce-scatter.5
where the time goes:
time: 1480 us; the launch traced here: 1470 us
  waiting for transfers between devices  1030 us (70%)
  local copies, waits for them, and re-layouts  159 us (11%)
  matrix products  150 us (10%)
  starting transfers between devices  55.7 us (4%)
  other arithmetic  37.6 us (3%)
  blocking collectives  19.3 us (1%)
  between operations  15.7 us (1%)
    reduce_scatter x1, waiting for transfers between devices, body(): lax.psum_scatter(grad_mixing, 'dev', scatter_dimension=1, tiled=True)  351 us
    reduce_scatter x1, waiting for transfers between devices, body(): lax.psum_scatter(grad_table, 'dev', scatter_dimension=0, tiled=True)  349 us
    reduce_scatter x1, waiting for transfers between devices, body(): lax.psum_scatter(grad_expand, 'dev', scatter_dimension=0, tiled=True)  305 us
    dot_general x8, matrix products, contract_rows(): lax.dot_general(left, right, (((0,), (0,)), ((), ())), preferred_element_...  49.2 us
    gather x4, local copies, waits for them, and re-layouts, leaf_scores(): book_rows = codebook[pair[1]]  45.8 us
    gather x4, local copies, waits for them, and re-layouts, leaf_back(): book_rows = codebook[pair[1]]  45.8 us
    unnamed x156, local copies, waits for them, and re-layouts  42.4 us
    dot_general x4, matrix products, leaf_back(): jnp.einsum('bi,bid->bd', pair[0], book_rows, preferred_element_type=jnp.f...  32.2 us
  transfers between devices with their start and end apart: 11, of which 7 were waited for; matrix products, arithmetic and copies ran while one was open for 19% of the time, Pallas kernels for 0%

commit v1 on v0

v1 whole, which is shorter than its diff:
```python
import functools

import jax
import jax.numpy as jnp
from jax import lax
from jax.experimental import pallas as pl
from jax.experimental.pallas import tpu as pltpu
from jax.sharding import Mesh
from jax.sharding import PartitionSpec as P

HEAD_DIM = 128
SEQ_MOST = 64
CAP = 4
eps = 1e-05
DEV = ("y", "z", "x")
f32 = jnp.float32
bf16 = jnp.bfloat16


def swap(part):
    return lax.ppermute(part, "section", [(0, 1), (1, 0)])


def shifted(part, step):
    count = lax.axis_size("x")
    return lax.ppermute(part, "x", [(i, (i + step) % count) for i in range(count)])


def silu_grad(argument):
    logistic = jax.nn.sigmoid(argument)
    return logistic * (1.0 + argument * (1.0 - logistic))


def seg_mask(lengths_row, count):
    seg_ends = jnp.cumsum(lengths_row, dtype=jnp.int32)
    positions = jnp.arange(count, dtype=jnp.int32)
    segment = jnp.sum(
        (positions[:, None] >= seg_ends[None, :]).astype(jnp.int32), axis=1, dtype=jnp.int32
    )
    same_seq = segment[:, None] == segment[None, :]
    causal = positions[None, :] <= positions[:, None]
    return jnp.where(same_seq & causal, 1.0, 0.0).astype(f32)


def layer_norm(argument):
    row_mean = jnp.mean(argument, axis=-1, keepdims=True)
    centered = argument - row_mean
    variance = jnp.mean(centered * centered, axis=-1, keepdims=True)
    inverse = lax.rsqrt(variance + eps)
    return (centered * inverse, inverse)


def norm_back(incoming, normed, inverse):
    mean_in = jnp.mean(incoming, axis=-1, keepdims=True)
    mean_dot = jnp.mean(incoming * normed, axis=-1, keepdims=True)
    return (incoming - mean_in - normed * mean_dot) * inverse


def dot(left, right, dims):
    return lax.dot_general(left, right, (dims, ((), ())), preferred_element_type=f32)


NN = ((1,), (0,))
NT = ((1,), (1,))
TN = ((0,), (0,))


def leaf_scores_kernel(group, got_ref, book_ref, out_ref, stat_ref):
    step = pl.program_id(0)
    width = book_ref.shape[2]

    @pl.when(step == 0)
    def _():
        out_ref[...] = jnp.zeros_like(out_ref)

    rows = got_ref[:, :width]
    codes = got_ref[:, width : width + 1].astype(f32)
    total = out_ref[...]
    for k in range(group):
        mine = codes == (step * group + k + 1).astype(f32)
        total += dot(jnp.where(mine, rows, jnp.zeros_like(rows)), book_ref[k], NT)
    out_ref[...] = total

    @pl.when(step == pl.num_programs(0) - 1)
    def _():
        peak = jnp.max(total, axis=1, keepdims=True)
        mass = jnp.sum(jnp.exp(total - peak), axis=1, keepdims=True)
        lane = lax.broadcasted_iota(jnp.int32, stat_ref.shape, 1)
        stat_ref[...] = jnp.where(lane == 0, peak, mass)


def leaf_back_kernel(group, sec_ref, got_ref, score_ref, mine_ref, other_ref, book_ref, back_ref, grad_ref, total_ref):
    step = pl.program_id(0)
    width = book_ref.shape[2]
    codes = got_ref[:, width : width + 1].astype(f32)

    @pl.when(step == 0)
    def _():
        high = got_ref[:, width + 1 : width + 2].astype(f32)
        low = got_ref[:, width + 2 : width + 3].astype(jnp.int32)
        peak_a, mass_a = mine_ref[:, 0:1], mine_ref[:, 1:2]
        peak_b, mass_b = other_ref[:, 0:1], other_ref[:, 1:2]
        peak = jnp.maximum(peak_a, peak_b)
        mass = mass_a * jnp.exp(peak_a - peak) + mass_b * jnp.exp(peak_b - peak)
        probs = jnp.exp(score_ref[...] - peak) / mass
        item = lax.broadcasted_iota(jnp.int32, probs.shape, 1)
        hit = (item == low) & (high == sec_ref[0].astype(f32))
        grad = jnp.where(codes > 0, probs - jnp.where(hit, 1.0, 0.0), 0.0)
        grad_ref[...] = grad.astype(bf16)
        total_ref[...] = jnp.zeros_like(total_ref)

    grads = grad_ref[...]
    total = total_ref[...]
    for k in range(group):
        mine = codes == (step * group + k + 1).astype(f32)
        total += dot(jnp.where(mine, grads, jnp.zeros_like(grads)), book_ref[k], NN)
    total_ref[...] = total

    @pl.when(step == pl.num_programs(0) - 1)
    def _():
        back_ref[...] = total.astype(bf16)


def leaf_book_kernel(group, got_ref, grad_ref, out_ref, turned_ref):
    step = pl.program_id(0)
    width = out_ref.shape[2]

    @pl.when(step == 0)
    def _():
        turned_ref[...] = grad_ref[...].astype(f32).T.astype(bf16)

    rows = got_ref[:, :width]
    codes = got_ref[:, width : width + 1].astype(f32)
    for k in range(group):
        mine = codes == (step * group + k + 1).astype(f32)
        out_ref[k] = dot(turned_ref[...], jnp.where(mine, rows, jnp.zeros_like(rows)), NN).astype(bf16)


def whole(shape):
    return pl.BlockSpec(shape, lambda i: (0,) * len(shape))


def params():
    return pltpu.CompilerParams(dimension_semantics=("arbitrary",), vmem_limit_bytes=40 * 2**20)


def leaf_scores(got, book):
    books, items, width = book.shape
    slots = got.shape[0]
    group = 8
    return pl.pallas_call(
        functools.partial(leaf_scores_kernel, group),
        grid=(books // group,),
        in_specs=[whole(got.shape), pl.BlockSpec((group, items, width), lambda i: (i, 0, 0))],
        out_specs=[whole((slots, items)), whole((slots, 128))],
        out_shape=[jax.ShapeDtypeStruct((slots, items), f32), jax.ShapeDtypeStruct((slots, 128), f32)],
        compiler_params=params(),
        cost_estimate=pl.CostEstimate(flops=2 * slots * books * items * width, bytes_accessed=books * items * width * 2, transcendentals=0),
        name="leaf_scores",
    )(got, book)


def leaf_back(section, got, scores, mine, other, book):
    books, items, width = book.shape
    slots = got.shape[0]
    group = 8
    return pl.pallas_call(
        functools.partial(leaf_back_kernel, group),
        grid=(books // group,),
        in_specs=[
            pl.BlockSpec(memory_space=pltpu.SMEM),
            whole(got.shape),
            whole(scores.shape),
            whole(mine.shape),
            whole(other.shape),
            pl.BlockSpec((group, items, width), lambda i: (i, 0, 0)),
        ],
        out_specs=[whole((slots, width)), whole((slots, items))],
        out_shape=[jax.ShapeDtypeStruct((slots, width), bf16), jax.ShapeDtypeStruct((slots, items), bf16)],
        scratch_shapes=[pltpu.VMEM((slots, width), f32)],
        compiler_params=params(),
        cost_estimate=pl.CostEstimate(flops=2 * slots * books * items * width, bytes_accessed=books * items * width * 2, transcendentals=0),
        name="leaf_back",
    )(section, got, scores, mine, other, book)


def leaf_book(got, grads, books, width):
    slots, items = grads.shape
    group = 8
    return pl.pallas_call(
        functools.partial(leaf_book_kernel, group),
        grid=(books // group,),
        in_specs=[whole(got.shape), whole(grads.shape)],
        out_specs=pl.BlockSpec((group, items, width), lambda i: (i, 0, 0)),
        out_shape=jax.ShapeDtypeStruct((books, items, width), bf16),
        scratch_shapes=[pltpu.VMEM((items, slots), bf16)],
        compiler_params=params(),
        cost_estimate=pl.CostEstimate(flops=2 * slots * books * items * width, bytes_accessed=books * items * width * 2, transcendentals=0),
        name="leaf_book",
    )(got, grads)


def body(
    inputs,
    lengths,
    expand_weight,
    mixing_weight,
    projection,
    saved_rows,
    cluster_ids,
    item_ids,
    top_table,
    codebook,
):
    micro_count, row_count, model_width = inputs.shape
    total_rows = micro_count * row_count
    owners = lax.axis_size(DEV)
    group = lax.axis_size("x")
    section = lax.axis_index("section")
    my_x = lax.axis_index("x")
    half_clusters, head_width = top_table.shape
    local_books, half_items, _ = codebook.shape
    col_count = expand_weight.shape[2]
    head_count = col_count // HEAD_DIM
    slot_each = micro_count * CAP
    slot_count = owners * slot_each

    owner_ids = cluster_ids // local_books
    marks = (owner_ids[:, :, None] == jnp.arange(owners, dtype=jnp.int32)).astype(bf16)
    place = jnp.arange(row_count, dtype=jnp.int32)
    before = (place[None, :] < place[:, None]).astype(bf16)
    earlier = jnp.einsum("ij,mjo->mio", before, marks, preferred_element_type=f32)
    rank = jnp.sum(earlier * marks.astype(f32), axis=2).astype(jnp.int32)
    slot_ids = owner_ids * slot_each + jnp.arange(micro_count, dtype=jnp.int32)[:, None] * CAP + rank
    slot_ids = slot_ids.reshape(total_rows)
    saved = saved_rows.reshape(total_rows, head_width)
    targets = cluster_ids.reshape(total_rows)
    chosen = item_ids.reshape(total_rows)
    lane = jnp.arange(128, dtype=jnp.int32)[None, :]
    codes = jnp.where(
        lane == 0,
        (targets % local_books + 1)[:, None],
        jnp.where(lane == 1, (chosen // half_items)[:, None], jnp.where(lane == 2, (chosen % half_items)[:, None], 0)),
    )
    extended = jnp.concatenate([saved, codes.astype(bf16)], axis=1)
    pick = (slot_ids[:, None] == jnp.arange(slot_count, dtype=jnp.int32)[None, :]).astype(bf16)
    sent = dot(pick, extended, TN).astype(bf16)
    got = lax.all_to_all(sent.reshape(owners, slot_each, -1), DEV, 0, 0, tiled=True).reshape(slot_count, -1)

    logits = dot(saved, top_table, NT)
    peak = jnp.max(logits, axis=1, keepdims=True)
    mass = jnp.sum(jnp.exp(logits - peak), axis=1, keepdims=True)
    peak_b, mass_b = swap((peak, mass))
    both = jnp.maximum(peak, peak_b)
    mass = mass * jnp.exp(peak - both) + mass_b * jnp.exp(peak_b - both)
    hits = jnp.arange(half_clusters, dtype=jnp.int32)[None, :] + section * half_clusters == targets[:, None]
    top_grad = (jnp.exp(logits - both) / mass - jnp.where(hits, 1.0, 0.0)).astype(bf16)
    row_top = dot(top_grad, top_table, NN)
    table_part = dot(top_grad, saved, TN).astype(bf16)

    flat_inputs = inputs.reshape(total_rows, model_width)
    normed, inverse = layer_norm(flat_inputs.astype(f32))
    normed_b = normed.astype(bf16)
    normed_all = [normed_b] + [shifted(normed_b, s) for s in range(1, group)]
    flat_in = expand_weight.reshape(model_width, 4 * col_count)
    pre_act = dot(normed_b, flat_in, NN)
    activated = jax.nn.silu(pre_act).astype(bf16)
    gate_part = activated[:, :col_count].astype(f32)

    def heads(part):
        return part.reshape(micro_count, row_count, head_count, HEAD_DIM)

    value_heads = heads(activated[:, col_count : 2 * col_count])
    query_heads = heads(activated[:, 2 * col_count : 3 * col_count])
    key_heads = heads(activated[:, 3 * col_count :])
    seq_mask = jax.vmap(lambda one: seg_mask(one, row_count))(lengths[:, 0])[:, None]

    def ein(spec, left, right):
        return jnp.einsum(spec, left, right, preferred_element_type=f32)

    scores = ein("mihk,mjhk->mhij", query_heads, key_heads)
    attention = (jax.nn.silu(scores) * seq_mask / SEQ_MOST).astype(bf16)
    mixed_out = ein("mhij,mjhk->mihk", attention, value_heads)
    out_normed, inverse_mid = layer_norm(mixed_out)
    normed_flat = out_normed.reshape(total_rows, col_count)
    product = (normed_flat * gate_part).astype(bf16)
    product_all = [product] + [shifted(product, s) for s in range(1, group)]

    leaf, stats = leaf_scores(got, codebook)
    back, leaf_grad = leaf_back(section.reshape(1), got, leaf, stats, swap(stats), codebook)
    returned = lax.all_to_all(back.reshape(owners, slot_each, head_width), DEV, 0, 0, tiled=True)
    book_grads = leaf_book(got, leaf_grad, local_books, head_width)

    row_part = row_top + dot(pick, returned.reshape(slot_count, head_width), NN)
    row_grad = (row_part + swap(row_part)).astype(bf16)
    out_grad = dot(row_grad, projection, NT).astype(bf16)
    turned = projection.reshape(owners, group, -1, head_width).swapaxes(0, 1).reshape(group, -1, head_width)
    out_turned = jnp.einsum("rd,gcd->grc", row_grad, turned, preferred_element_type=f32).astype(bf16)

    def exchange(parts):
        pieces = [lax.dynamic_index_in_dim(parts, my_x, 0, False)]
        for s in range(1, group):
            piece = lax.dynamic_index_in_dim(parts, (my_x + s) % group, 0, False)
            pieces.append(shifted(piece, s))
        return pieces

    out_pieces = exchange(out_turned)

    grad_product = dot(out_grad, mixing_weight, NT)
    grad_gate = grad_product * normed_flat
    grad_onorm = heads(grad_product * gate_part)
    grad_mixed = norm_back(grad_onorm, out_normed, inverse_mid).astype(bf16)
    grad_attention = ein("mihk,mjhk->mhij", grad_mixed, value_heads)
    grad_values = ein("mhij,mihk->mjhk", attention, grad_mixed)
    grad_scores = (grad_attention * silu_grad(scores) * seq_mask / SEQ_MOST).astype(bf16)
    grad_query = ein("mhij,mjhk->mihk", grad_scores, key_heads)
    grad_keys = ein("mhij,mihk->mjhk", grad_scores, query_heads)
    acts = [grad_gate, grad_values, grad_query, grad_keys]
    slope = silu_grad(pre_act)
    grad_pre = jnp.stack(
        [
            (part.reshape(total_rows, col_count) * slope[:, i * col_count : (i + 1) * col_count]).astype(bf16)
            for i, part in enumerate(acts)
        ]
    )
    pre_pieces = exchange(grad_pre)
    grad_part = sum(dot(grad_pre[i], expand_weight[:, i], NT) for i in range(4))
    grad_normed = grad_part + swap(grad_part)
    grad_inputs = (out_grad.astype(f32) + norm_back(grad_normed, normed, inverse)).astype(bf16)

    expand_part = sum(dot(a, b, TN) for a, b in zip(normed_all, pre_pieces)).astype(bf16)
    mixing_part = sum(dot(b, a, TN) for a, b in zip(product_all, out_pieces)).astype(bf16)
    sizes = [model_width // owners, mixing_part.shape[0] // owners, half_clusters * head_width // col_count // owners]
    packed = jnp.concatenate(
        [part.reshape(owners, size, col_count) for part, size in zip((expand_part, mixing_part, table_part), sizes)], axis=1
    )
    arrived = lax.all_to_all(packed, DEV, 0, 0, tiled=True)
    arrived = arrived.astype(f32).reshape(owners // group, group, -1, col_count)
    first, second = sizes[0], sizes[0] + sizes[1]
    weights = jnp.sum(arrived[:, :, :second], axis=0)
    share_expand = weights[:, :first].swapaxes(0, 1)
    share_mixing = weights[:, first:].reshape(-1, col_count).T
    share_table = jnp.sum(arrived[:, :, second:], axis=(0, 1)).reshape(-1, head_width)
    return (
        grad_inputs.reshape(inputs.shape),
        share_expand,
        share_mixing,
        share_table,
        book_grads,
    )


def solution(mesh):
    grid = Mesh(mesh.devices.reshape(2, 4, 4, 4), ("section",) + DEV)
    return jax.shard_map(
        body,
        mesh=grid,
        in_specs=(
            P(None, DEV, None),
            P(None, DEV, None),
            P(None, None, "section"),
            P("section", None),
            P(),
            P(None, DEV, None),
            P(None, DEV),
            P(None, DEV),
            P("section", None),
            P(DEV, "section", None),
        ),
        out_specs=(
            P(None, DEV, None),
            P(DEV, None, "section"),
            P("section", DEV),
            P(("section",) + DEV, None),
            P(DEV, "section", None),
        ),
        check_vma=False,
    )
```

time: 1480 us -> 233 us (0.16)
  waiting for transfers between devices: 1030 us -> 74.1 us
  local copies, waits for them, and re-layouts: 159 us -> 37.8 us
  matrix products: 150 us -> 28.9 us
  Pallas kernels: 0 us -> 25 us
  blocking collectives: 19.3 us -> 0 us
  starting transfers between devices: 55.7 us -> 40.8 us
    reduce_scatter x3 -> x0, waiting for transfers between devices: 1000 us -> none  [the longest x1 351 us: body(): lax.psum_scatter(grad_mixing, 'dev', scatter_dimension=1, tiled=True)]
    dot_general x40 -> x28, matrix products: 150 us -> 28.9 us  [the longest x20 22.9 us: dot(): lax.dot_general(left, right, (dims, ((), ())), preferred_element_type=f32)]
    gather x10 -> x0, local copies, waits for them, and re-layouts: 93.6 us -> none  [the longest x4 45.8 us: leaf_scores(): book_rows = codebook[pair[1]]]
    ppermute x0 -> x17, waiting for transfers between devices: none -> 36.5 us  [the longest x12 36.4 us: shifted(): lax.ppermute(part, 'x', [(i, (i + step) % count) for i in range(count)])]
    unnamed x156 -> x70, local copies, waits for them, and re-layouts: 42.4 us -> 14 us
    all_to_all x6 -> x3, starting transfers between devices: 55.1 us -> 27.7 us  [the longest x1 11.5 us: body(): lax.all_to_all(sent.reshape(owners, slot_each, -1), DEV, 0, 0, tiled=True)]
    pallas_call x0 -> x3, Pallas kernels: none -> 25 us  [the longest x1 8.97 us: leaf_back(): pl.pallas_call(functools.partial(leaf_back_kernel, group), grid=(books //...]
    all_to_all x6 -> x3, waiting for transfers between devices: 17.9 us -> 37.6 us  [the longest x1 28.8 us: body(): arrived = lax.all_to_all(packed, DEV, 0, 0, tiled=True)]
  transfers between devices with their start and end apart: 11 -> 20, of which waited for: 7 -> 8; matrix products, arithmetic and copies ran while one was open for 19% -> 18% of each run, Pallas kernels for 0% -> 7%
where the time goes in v1:
time: 233 us; the launch traced here: 231 us
  waiting for transfers between devices  74.1 us (32%)
  starting transfers between devices  40.8 us (18%)
  local copies, waits for them, and re-layouts  37.8 us (16%)
  matrix products  28.9 us (12%)
  Pallas kernels  25 us (11%)
  other arithmetic  23.3 us (10%)
    ppermute x12, waiting for transfers between devices, shifted(): lax.ppermute(part, 'x', [(i, (i + step) % count) for i in range(count)])  36.4 us
    all_to_all x1, waiting for transfers between devices, body(): arrived = lax.all_to_all(packed, DEV, 0, 0, tiled=True)  28.8 us
    dot_general x20, matrix products, dot(): lax.dot_general(left, right, (dims, ((), ())), preferred_element_type=f32)  22.9 us
    unnamed x70, local copies, waits for them, and re-layouts  14 us
    ppermute x12, starting transfers between devices, shifted(): lax.ppermute(part, 'x', [(i, (i + step) % count) for i in range(count)])  12 us
    all_to_all x1, starting transfers between devices, body(): lax.all_to_all(sent.reshape(owners, slot_each, -1), DEV, 0, 0, tiled=True)  11.5 us
    all_to_all x1, starting transfers between devices, body(): lax.all_to_all(back.reshape(owners, slot_each, head_width), DEV, 0, 0, ti...  10.6 us
    pallas_call x1, Pallas kernels, leaf_back(): pl.pallas_call(functools.partial(leaf_back_kernel, group), grid=(books //...  8.97 us
  transfers between devices with their start and end apart: 20, of which 8 were waited for; matrix products, arithmetic and copies ran while one was open for 18% of the time, Pallas kernels for 7%

profile of v1, /device:TPU:0, one launch (start us, length us, event | category | flops | bytes accessed | tf_op | source)
XLA Modules:
  0.0 231.4 jit_solution(4150934166972308544)
XLA Ops:
  3.3 2.1 fusion.5
  5.4 11.5 %all-to-all-start = ((bf16[64,8,384]{2,1,0:T(8,128)(2,1)}), bf16[64,8,384]{2,1,0:T(8,128)(2,1)S(1)}, u32[]{:S(2)}, u32[]{:S(2)}) async-start(bf16[64,8,384]{2,1,0:T(8,128)(2,1)} %fusion.5), calls=%async_computation | async-start | bytes 786432 | tf_op jit(solution)/shard_map/all_to_all | solution.py:248
  16.9 2.1 fusion.47
  18.9 1.4 copy-done.5
  20.3 1.7 exponential_reduce_fusion
  24.4 7.8 %fusion.45 = (bf16[1024,1,512]{2,1,0:T(2,128)(2,1)}, bf16[1024,1,512]{2,1,0:T(2,128)(2,1)}, bf16[1024,1,512]{2,1,0:T(2,128)(2,1)}, bf16[1024,1,512]{2,1,0:T(2,128)(2,1)}) fusion(bf16[1024,4,512]{2,1,0:T(4,128)(2,1)S(1)} %copy-done.4), kind=kLoop, calls=%fused_computation.139 | loop fusion | bytes 8388608 | tf_op jit(solution)/shard_map/slice | solution.py:327
  32.2 1.4 copy.117
  33.6 3.1 %multiply_convert_fusion = (bf16[256,2048]{1,0:T(8,128)(2,1)S(1)}, f32[256,2048]{1,0:T(8,128)}) fusion(bf16[256,1024]{1,0:T(8,128)(2,1)S(1)} %bitcast.199, bf16[1024,2048]{1,0:T(8,128)(2,1)S(1)} %bitcast.188), kind=kOutput, calls=%fused_computation.6 | convolution fusion | flops 1078460416 | bytes 7864320 | tf_op jit(solution)/shard_map/dot_general | solution.py:60
  40.2 3.4 %copy-done.2 = bf16[64,256,256]{2,1,0:T(8,128)(2,1)S(1)} copy-done((bf16[64,256,256]{2,1,0:T(8,128)(2,1)S(1)}, bf16[64,256,256]{2,1,0:T(8,128)(2,1)}, u32[]{:S(2)}) %copy-start.2) | copy-done | bytes 8388632
  43.6 7.8 %leaf_scores.1 = (f32[512,256]{1,0:T(8,128)S(1)}, f32[512,128]{1,0:T(8,128)S(1)}) custom-call(bf16[512,384]{1,0:T(8,128)(2,1)S(1)} %bitcast.184, bf16[64,256,256]{2,1,0:T(8,128)(2,1)S(1)} %copy-done.2), custom_call_target="tpu_custom_call" | custom-call | flops 4294967296 | bytes 8388608 | tf_op jit(solution)/shard_map/leaf_scores/pallas_call | solution.py:151
  51.7 2.0 reshape.320
  53.7 2.0 copy.110
  55.7 2.0 reshape.321
  57.7 1.3 multiply_add_fusion
  59.0 3.4 %copy-done.3 = bf16[64,256,256]{2,1,0:T(8,128)(2,1)S(1)} copy-done((bf16[64,256,256]{2,1,0:T(8,128)(2,1)S(1)}, bf16[64,256,256]{2,1,0:T(8,128)(2,1)}, u32[]{:S(2)}) %copy-start.3) | copy-done | bytes 8388632
  62.4 9.0 %leaf_back.1 = (bf16[512,256]{1,0:T(8,128)(2,1)}, bf16[512,256]{1,0:T(8,128)(2,1)S(1)}) custom-call(s32[1]{0:T(128)} %bitcast.9.sec_ref, bf16[512,384]{1,0:T(8,128)(2,1)S(1)} %bitcast.185, f32[512,256]{1,0:T(8,128)S(1)} %get-tuple-element.9.score_ref, f32[512,128]{1,0:T(8,128)S(1)} %get-tuple-element.10.mine_ref, ...), custom_call_target="tpu_custom_call" | custom-call | flops 4294967296 | bytes 8388608 | tf_op jit(solution)/shard_map/leaf_back/pallas_call | solution.py:167
  71.4 10.6 %all-to-all-start.1 = ((bf16[64,8,256]{2,1,0:T(8,128)(2,1)}), bf16[64,8,256]{2,1,0:T(8,128)(2,1)}, u32[]{:S(2)}, u32[]{:S(2)}) async-start(bf16[64,8,256]{2,1,0:T(8,128)(2,1)} %bitcast.13), calls=%async_computation.1 | async-start | bytes 524288 | tf_op jit(solution)/shard_map/all_to_all | solution.py:291
  82.0 2.2 subtract_convert_fusion
  84.2 8.8 %all-to-all-done.1 = bf16[64,8,256]{2,1,0:T(8,128)(2,1)} async-done(((bf16[64,8,256]{2,1,0:T(8,128)(2,1)}), bf16[64,8,256]{2,1,0:T(8,128)(2,1)}, u32[]{:S(2)}, u32[]{:S(2)}) %all-to-all-start.1) | async-done | bytes 262176 | tf_op jit(solution)/shard_map/all_to_all | solution.py:291
  93.0 1.3 fusion.17
  94.3 1.1 convolution_add_fusion.5
  96.0 1.2 reshape.323
  99.0 1.4 convolution_convert_fusion.2
  100.4 2.2 convert_multiply_fusion.1
  103.0 1.1 multiply_reduce_fusion.2
  106.3 1.6 fusion.3
  110.1 1.2 convolution_bitcast_fusion.2
  111.5 1.3 copy.108
  112.8 2.0 copy.105
  115.9 2.8 %fusion.12 = (bf16[256,512]{1,0:T(8,128)(2,1)S(1)}, bf16[256,512]{1,0:T(8,128)(2,1)S(1)}, bf16[256,512]{1,0:T(8,128)(2,1)S(1)}, bf16[256,512]{1,0:T(8,128)(2,1)S(1)}, bf16[256,512]{1,0:T(8,128)(2,1)S(1)}) fusion(f32[32,8,4,128]{3,2,1,0:T(4,128)S(1)} %bitcast.195, f32[256,2048]{1,0:T(8,128)} %get-tuple-element.44, f32[32,8,4,128]{3,2,1,0:T(4,128)} %bitcast.196, ...), kind=kLoop, calls=%fused_computation.51 | loop fusion | flops 1572864 | bytes 6291456 | tf_op jit(solution)/shard_map/convert_element_type | solution.py:322
  126.1 2.2 collective-permute-start.15
  129.5 1.8 fusion.18
  131.8 1.2 fusion.10
  133.0 5.1 %collective-permute-done.11 = bf16[256,256]{1,0:T(8,128)(2,1)S(1)} collective-permute-done((bf16[256,256]{1,0:T(8,128)(2,1)S(1)}, bf16[256,256]{1,0:T(8,128)(2,1)S(1)}, u32[]{:S(2)}, u32[]{:S(2)}) %collective-permute-start.11) | collective-permute-done | bytes 131104 | tf_op jit(solution)/shard_map/ppermute | solution.py:26
  139.1 2.6 %collective-permute-start.7 = (bf16[256,1024]{1,0:T(8,128)(2,1)S(1)}, bf16[256,1024]{1,0:T(8,128)(2,1)S(1)}, u32[]{:S(2)}, u32[]{:S(2)}) collective-permute-start(bf16[256,1024]{1,0:T(8,128)(2,1)S(1)} %get-tuple-element.51), channel_id=1, source_target_pairs={{0,2},{1,3},{2,0},{3,1},{4,6},{5,7},{6,4},{7,5},{8,10},{9,11},{10,... | collective-permute-start | bytes 1572872 | tf_op jit(solution)/shard_map/ppermute | solution.py:26
  143.2 2.9 %collective-permute-done.13 = bf16[256,256]{1,0:T(8,128)(2,1)S(1)} collective-permute-done((bf16[256,256]{1,0:T(8,128)(2,1)S(1)}, bf16[256,256]{1,0:T(8,128)(2,1)S(1)}, u32[]{:S(2)}, u32[]{:S(2)}) %collective-permute-start.13) | collective-permute-done | bytes 131104 | tf_op jit(solution)/shard_map/ppermute | solution.py:26
  146.5 1.6 collective-permute-start.5
  148.5 14.6 %collective-permute-done.8 = bf16[256,512]{1,0:T(8,128)(2,1)} collective-permute-done((bf16[256,512]{1,0:T(8,128)(2,1)}, bf16[256,512]{1,0:T(8,128)(2,1)}, u32[]{:S(2)}, u32[]{:S(2)}) %collective-permute-start.8) | collective-permute-done | bytes 262176 | tf_op jit(solution)/shard_map/ppermute | solution.py:26
  163.1 1.4 fusion.51
  164.5 2.4 %collective-permute-done.6 = bf16[256,512]{1,0:T(8,128)(2,1)S(1)} collective-permute-done((bf16[256,512]{1,0:T(8,128)(2,1)}, bf16[256,512]{1,0:T(8,128)(2,1)S(1)}, u32[]{:S(2)}, u32[]{:S(2)}) %collective-permute-start.6) | collective-permute-done | bytes 262176 | tf_op jit(solution)/shard_map/ppermute | solution.py:26
  167.0 11.2 %collective-permute-done.5 = bf16[256,1024]{1,0:T(8,128)(2,1)} collective-permute-done((bf16[256,1024]{1,0:T(8,128)(2,1)S(1)}, bf16[256,1024]{1,0:T(8,128)(2,1)}, u32[]{:S(2)}, u32[]{:S(2)}) %collective-permute-start.5) | collective-permute-done | bytes 524320 | tf_op jit(solution)/shard_map/ppermute | solution.py:26
  178.2 1.5 fusion.50
  179.8 1.5 add_convert_fusion
  181.3 2.3 pad_maximum_fusion
  183.6 5.6 %all-to-all-start.2 = ((bf16[64,36,512]{2,1,0:T(8,128)(2,1)}), bf16[64,36,512]{2,1,0:T(8,128)(2,1)}, u32[]{:S(2)}, u32[]{:S(2)}) async-start(bf16[64,36,512]{2,1,0:T(8,128)(2,1)} %pad_maximum_fusion), calls=%async_computation.2 | async-start | bytes 5242880 | tf_op jit(solution)/shard_map/all_to_all | solution.py:337
  189.2 8.3 %leaf_book.1 = bf16[64,256,256]{2,1,0:T(8,128)(2,1)} custom-call(bf16[512,384]{1,0:T(8,128)(2,1)S(1)} %bitcast.186, bf16[512,256]{1,0:T(8,128)(2,1)S(1)} %get-tuple-element.12.grad_ref), custom_call_target="tpu_custom_call" | custom-call | flops 4294967296 | bytes 8388608 | tf_op jit(solution)/shard_map/leaf_book/pallas_call | solution.py:190
  197.4 28.8 %all-to-all-done.2 = bf16[64,36,512]{2,1,0:T(8,128)(2,1)} async-done(((bf16[64,36,512]{2,1,0:T(8,128)(2,1)}), bf16[64,36,512]{2,1,0:T(8,128)(2,1)}, u32[]{:S(2)}, u32[]{:S(2)}) %all-to-all-start.2) | async-done | bytes 2359328 | tf_op jit(solution)/shard_map/all_to_all | solution.py:337
  226.2 2.5 %bitcast_convert_fusion = f32[16,4,36,512]{3,2,1,0:T(8,128)S(1)} fusion(bf16[64,36,512]{2,1,0:T(8,128)(2,1)} %all-to-all-done.2), kind=kLoop, calls=%fused_computation.135 | loop fusion | flops 1179648 | bytes 7077888 | tf_op jit(solution)/shard_map/reshape | solution.py:338
  (157 shorter events, 31.6 us)
Async XLA Ops:
  0.6 16.2 %copy-start = (bf16[2048,256]{1,0:T(8,128)(2,1)S(1)}, bf16[2048,256]{1,0:T(8,128)(2,1)}, u32[]{:S(2)}) copy-start(bf16[2048,256]{1,0:T(8,128)(2,1)} %param.18) | copy-start | bytes 3145732
  3.1 2.3 copy-start.32
  5.4 34.6 %all-to-all-start = ((bf16[64,8,384]{2,1,0:T(8,128)(2,1)}), bf16[64,8,384]{2,1,0:T(8,128)(2,1)S(1)}, u32[]{:S(2)}, u32[]{:S(2)}) async-start(bf16[64,8,384]{2,1,0:T(8,128)(2,1)} %fusion.5), calls=%async_computation | async-start | bytes 786432 | tf_op jit(solution)/shard_map/all_to_all | solution.py:248
  16.9 5.7 %copy-start.6 = (bf16[2,128,1024]{2,1,0:T(8,128)(2,1)S(1)}, bf16[2,128,1024]{2,1,0:T(8,128)(2,1)}, u32[]{:S(2)}) copy-start(bf16[2,128,1024]{2,1,0:T(8,128)(2,1)} %param.10) | copy-start | bytes 1572868
  18.9 1.4 copy-start.5
  20.3 4.1 %copy-start.4 = (bf16[1024,4,512]{2,1,0:T(4,128)(2,1)S(1)}, bf16[1024,4,512]{2,1,0:T(4,128)(2,1)}, u32[]{:S(2)}) copy-start(bf16[1024,4,512]{2,1,0:T(4,128)(2,1)} %param.12) | copy-start | bytes 12582916
  22.1 35.7 %collective-permute-start.1 = (f32[256,1]{0,1:T(1,128)}, f32[256,1]{0,1:T(1,128)}, u32[]{:S(2)}, u32[]{:S(2)}) collective-permute-start(f32[256,1]{0,1:T(1,128)} %bitcast.3), channel_id=1, source_target_pairs={{0,64},{64,0},{1,65},{65,1},{2,66},{66,2},{3,67},{67,3},{4,68},{68... | collective-permute-start | bytes 3080 | tf_op jit(solution)/shard_map/ppermute | solution.py:21
  22.1 35.7 %collective-permute-start = (f32[256,1]{0,1:T(1,128)}, f32[256,1]{0,1:T(1,128)}, u32[]{:S(2)}, u32[]{:S(2)}) collective-permute-start(f32[256,1]{0,1:T(1,128)} %bitcast.1), channel_id=1, source_target_pairs={{0,64},{64,0},{1,65},{65,1},{2,66},{66,2},{3,67},{67,3},{4,68},{68... | collective-permute-start | bytes 3080 | tf_op jit(solution)/shard_map/ppermute | solution.py:21
  24.4 9.2 %copy-start.17 = (bf16[2,128,1024]{2,1,0:T(8,128)(2,1)}, bf16[2,128,1024]{2,1,0:T(8,128)(2,1)S(1)}, u32[]{:S(2)}) copy-start(bf16[2,128,1024]{2,1,0:T(8,128)(2,1)S(1)} %multiply_convert_fusion.1) | copy-start | bytes 1572868
  36.7 1.6 copy-start.33
  38.3 1.2 copy-start.13
  38.7 1.3 copy-start.27
  40.2 3.4 %copy-start.2 = (bf16[64,256,256]{2,1,0:T(8,128)(2,1)S(1)}, bf16[64,256,256]{2,1,0:T(8,128)(2,1)}, u32[]{:S(2)}) copy-start(bf16[64,256,256]{2,1,0:T(8,128)(2,1)} %book_ref.3) | copy-start | bytes 25165828
  51.4 7.6 %collective-permute-start.2 = (f32[512,128]{1,0:T(8,128)S(1)}, f32[512,128]{1,0:T(8,128)S(1)}, u32[]{:S(2)}, u32[]{:S(2)}) collective-permute-start(f32[512,128]{1,0:T(8,128)S(1)} %get-tuple-element.10.mine_ref), channel_id=1, source_target_pairs={{0,64},{64,0},{1,65},{65,1},{2,66},{66,2},{3,67},{67,3},{4,68},{68... | collective-permute-start | bytes 786440 | tf_op jit(solution)/shard_map/ppermute | solution.py:21
  59.0 3.4 %copy-start.3 = (bf16[64,256,256]{2,1,0:T(8,128)(2,1)S(1)}, bf16[64,256,256]{2,1,0:T(8,128)(2,1)}, u32[]{:S(2)}) copy-start(bf16[64,256,256]{2,1,0:T(8,128)(2,1)} %book_ref.3) | copy-start | bytes 25165828
  71.4 21.7 %all-to-all-start.1 = ((bf16[64,8,256]{2,1,0:T(8,128)(2,1)}), bf16[64,8,256]{2,1,0:T(8,128)(2,1)}, u32[]{:S(2)}, u32[]{:S(2)}) async-start(bf16[64,8,256]{2,1,0:T(8,128)(2,1)} %bitcast.13), calls=%async_computation.1 | async-start | bytes 524288 | tf_op jit(solution)/shard_map/all_to_all | solution.py:291
  93.0 2.4 %copy-start.23 = (bf16[2,128,256]{2,1,0:T(8,128)(2,1)S(1)}, bf16[2,128,256]{2,1,0:T(8,128)(2,1)}, u32[]{:S(2)}) copy-start(bf16[2,128,256]{2,1,0:T(8,128)(2,1)} %param.15) | copy-start | bytes 393220
  95.5 1.9 collective-permute-start.3
  96.0 4.5 %copy-start.22 = (bf16[512,1024]{1,0:T(8,128)(2,1)S(1)}, bf16[512,1024]{1,0:T(8,128)(2,1)}, u32[]{:S(2)}) copy-start(bf16[512,1024]{1,0:T(8,128)(2,1)} %param.13) | copy-start | bytes 3145732
  106.3 2.7 %copy-start.14 = (bf16[2,128,4,128]{1,3,2,0:T(8,128)(2,1)S(1)}, bf16[2,128,4,128]{1,3,2,0:T(8,128)(2,1)}, u32[]{:S(2)}) copy-start(bf16[2,128,4,128]{1,3,2,0:T(8,128)(2,1)} %copy-done.13) | copy-start | bytes 786436
  106.3 3.8 %copy-start.25 = (f32[2,4,128,128]{3,2,1,0:T(8,128)S(1)}, f32[2,4,128,128]{3,2,1,0:T(8,128)}, u32[]{:S(2)}) copy-start(f32[2,4,128,128]{3,2,1,0:T(8,128)} %copy-done.24) | copy-start | bytes 1572868
  106.3 3.8 %copy-start.29 = (f32[2,128,128]{2,1,0:T(8,128)S(1)}, f32[2,128,128]{2,1,0:T(8,128)}, u32[]{:S(2)}) copy-start(f32[2,128,128]{2,1,0:T(8,128)} %copy-done.28) | copy-start | bytes 393220
  111.5 3.4 %copy-start.26 = (f32[2,128,4,128]{1,3,2,0:T(8,128)S(1)}, f32[2,128,4,128]{1,3,2,0:T(8,128)}, u32[]{:S(2)}) copy-start(f32[2,128,4,128]{1,3,2,0:T(8,128)} %convolution_bitcast_fusion.2) | copy-start | bytes 1572868
  115.9 6.1 %copy-start.11 = (bf16[1024,1,512]{2,1,0:T(2,128)(2,1)S(1)}, bf16[1024,1,512]{2,1,0:T(2,128)(2,1)}, u32[]{:S(2)}) copy-start(bf16[1024,1,512]{2,1,0:T(2,128)(2,1)} %get-tuple-element.38) | copy-start | bytes 3145732
  118.7 3.8 %copy-start.10 = (bf16[1024,1,512]{2,1,0:T(2,128)(2,1)S(1)}, bf16[1024,1,512]{2,1,0:T(2,128)(2,1)}, u32[]{:S(2)}) copy-start(bf16[1024,1,512]{2,1,0:T(2,128)(2,1)} %get-tuple-element.37) | copy-start | bytes 3145732
  118.7 24.2 %collective-permute-start.16 = (bf16[256,512]{1,0:T(8,128)(2,1)S(1)}, bf16[256,512]{1,0:T(8,128)(2,1)S(1)}, u32[]{:S(2)}, u32[]{:S(2)}) collective-permute-start(bf16[256,512]{1,0:T(8,128)(2,1)S(1)} %get-tuple-element.53), channel_id=1, source_target_pairs={{0,3},{1,0},{2,1},{3,2},{4,7},{5,4},{6,5},{7,6},{8,11},{9,8},{10,9... | collective-permute-start | bytes 786440 | tf_op jit(solution)/shard_map/ppermute | solution.py:26
  119.7 19.3 %collective-permute-start.12 = (bf16[256,512]{1,0:T(8,128)(2,1)S(1)}, bf16[256,512]{1,0:T(8,128)(2,1)S(1)}, u32[]{:S(2)}, u32[]{:S(2)}) collective-permute-start(bf16[256,512]{1,0:T(8,128)(2,1)S(1)} %get-tuple-element.53), channel_id=1, source_target_pairs={{0,1},{1,2},{2,3},{3,0},{4,5},{5,6},{6,7},{7,4},{8,9},{9,10},{10,1... | collective-permute-start | bytes 786440 | tf_op jit(solution)/shard_map/ppermute | solution.py:26
  120.8 25.7 %collective-permute-start.14 = (bf16[256,512]{1,0:T(8,128)(2,1)S(1)}, bf16[256,512]{1,0:T(8,128)(2,1)S(1)}, u32[]{:S(2)}, u32[]{:S(2)}) collective-permute-start(bf16[256,512]{1,0:T(8,128)(2,1)S(1)} %get-tuple-element.53), channel_id=1, source_target_pairs={{0,2},{1,3},{2,0},{3,1},{4,6},{5,7},{6,4},{7,5},{8,10},{9,11},{10,... | collective-permute-start | bytes 786440 | tf_op jit(solution)/shard_map/ppermute | solution.py:26
  122.5 1.6 copy-start.9
  123.0 1.8 copy-start.8
  124.6 1.1 copy-start.21
  125.3 6.0 %collective-permute-start.4 = (f32[256,1024]{1,0:T(8,128)S(1)}, f32[256,1024]{1,0:T(8,128)S(1)}, u32[]{:S(2)}, u32[]{:S(2)}) collective-permute-start(f32[256,1024]{1,0:T(8,128)S(1)} %convolution_add_fusion), channel_id=1, source_target_pairs={{0,64},{64,0},{1,65},{65,1},{2,66},{66,2},{3,67},{67,3},{4,68},{68... | collective-permute-start | bytes 3145736 | tf_op jit(solution)/shard_map/ppermute | solution.py:21
  126.1 15.9 %collective-permute-start.15 = (bf16[256,256]{1,0:T(8,128)(2,1)S(1)}, bf16[256,256]{1,0:T(8,128)(2,1)S(1)}, u32[]{:S(2)}, u32[]{:S(2)}) collective-permute-start(bf16[256,256]{1,0:T(8,128)(2,1)S(1)} %get-tuple-element.55), channel_id=1, source_target_pairs={{0,3},{1,0},{2,1},{3,2},{4,7},{5,4},{6,5},{7,6},{8,11},{9,8},{10,9... | collective-permute-start | bytes 393224 | tf_op jit(solution)/shard_map/ppermute | solution.py:26
  128.3 1.3 copy-start.18
  129.3 2.1 copy-start.30
  129.3 2.1 copy-start.31
  131.3 6.8 %collective-permute-start.11 = (bf16[256,256]{1,0:T(8,128)(2,1)S(1)}, bf16[256,256]{1,0:T(8,128)(2,1)S(1)}, u32[]{:S(2)}, u32[]{:S(2)}) collective-permute-start(bf16[256,256]{1,0:T(8,128)(2,1)S(1)} %get-tuple-element.56), channel_id=1, source_target_pairs={{0,1},{1,2},{2,3},{3,0},{4,5},{5,6},{6,7},{7,4},{8,9},{9,10},{10,1... | collective-permute-start | bytes 393224 | tf_op jit(solution)/shard_map/ppermute | solution.py:26
  138.1 8.0 %collective-permute-start.13 = (bf16[256,256]{1,0:T(8,128)(2,1)S(1)}, bf16[256,256]{1,0:T(8,128)(2,1)S(1)}, u32[]{:S(2)}, u32[]{:S(2)}) collective-permute-start(bf16[256,256]{1,0:T(8,128)(2,1)S(1)} %get-tuple-element.54), channel_id=1, source_target_pairs={{0,2},{1,3},{2,0},{3,1},{4,6},{5,7},{6,4},{7,5},{8,10},{9,11},{10,... | collective-permute-start | bytes 393224 | tf_op jit(solution)/shard_map/ppermute | solution.py:26
  139.1 24.0 %collective-permute-start.7 = (bf16[256,1024]{1,0:T(8,128)(2,1)S(1)}, bf16[256,1024]{1,0:T(8,128)(2,1)S(1)}, u32[]{:S(2)}, u32[]{:S(2)}) collective-permute-start(bf16[256,1024]{1,0:T(8,128)(2,1)S(1)} %get-tuple-element.51), channel_id=1, source_target_pairs={{0,2},{1,3},{2,0},{3,1},{4,6},{5,7},{6,4},{7,5},{8,10},{9,11},{10,... | collective-permute-start | bytes 1572872 | tf_op jit(solution)/shard_map/ppermute | solution.py:26
  142.0 21.1 %collective-permute-start.8 = (bf16[256,512]{1,0:T(8,128)(2,1)}, bf16[256,512]{1,0:T(8,128)(2,1)}, u32[]{:S(2)}, u32[]{:S(2)}) collective-permute-start(bf16[256,512]{1,0:T(8,128)(2,1)} %get-tuple-element.47), channel_id=1, source_target_pairs={{0,2},{1,3},{2,0},{3,1},{4,6},{5,7},{6,4},{7,5},{8,10},{9,11},{10,... | collective-permute-start | bytes 786440 | tf_op jit(solution)/shard_map/ppermute | solution.py:26
  143.0 24.0 %collective-permute-start.6 = (bf16[256,512]{1,0:T(8,128)(2,1)}, bf16[256,512]{1,0:T(8,128)(2,1)S(1)}, u32[]{:S(2)}, u32[]{:S(2)}) collective-permute-start(bf16[256,512]{1,0:T(8,128)(2,1)} %get-tuple-element.45), channel_id=1, source_target_pairs={{0,1},{1,2},{2,3},{3,0},{4,5},{5,6},{6,7},{7,4},{8,9},{9,10},{10,1... | collective-permute-start | bytes 786440 | tf_op jit(solution)/shard_map/ppermute | solution.py:26
  146.1 33.6 %collective-permute-start.10 = (bf16[256,512]{1,0:T(8,128)(2,1)S(1)}, bf16[256,512]{1,0:T(8,128)(2,1)}, u32[]{:S(2)}, u32[]{:S(2)}) collective-permute-start(bf16[256,512]{1,0:T(8,128)(2,1)S(1)} %get-tuple-element.46), channel_id=1, source_target_pairs={{0,3},{1,0},{2,1},{3,2},{4,7},{5,4},{6,5},{7,6},{8,11},{9,8},{10,9... | collective-permute-start | bytes 786440 | tf_op jit(solution)/shard_map/ppermute | solution.py:26
  146.5 31.7 %collective-permute-start.5 = (bf16[256,1024]{1,0:T(8,128)(2,1)S(1)}, bf16[256,1024]{1,0:T(8,128)(2,1)}, u32[]{:S(2)}, u32[]{:S(2)}) collective-permute-start(bf16[256,1024]{1,0:T(8,128)(2,1)S(1)} %get-tuple-element.51), channel_id=1, source_target_pairs={{0,1},{1,2},{2,3},{3,0},{4,5},{5,6},{6,7},{7,4},{8,9},{9,10},{10,1... | collective-permute-start | bytes 1572872 | tf_op jit(solution)/shard_map/ppermute | solution.py:26
  163.1 16.7 %collective-permute-start.9 = (bf16[256,1024]{1,0:T(8,128)(2,1)S(1)}, bf16[256,1024]{1,0:T(8,128)(2,1)S(1)}, u32[]{:S(2)}, u32[]{:S(2)}) collective-permute-start(bf16[256,1024]{1,0:T(8,128)(2,1)S(1)} %get-tuple-element.51), channel_id=1, source_target_pairs={{0,3},{1,0},{2,1},{3,2},{4,7},{5,4},{6,5},{7,6},{8,11},{9,8},{10,9... | collective-permute-start | bytes 1572872 | tf_op jit(solution)/shard_map/ppermute | solution.py:26
  164.5 15.2 %copy-start.7 = (f32[1024,512]{1,0:T(8,128)S(1)}, f32[1024,512]{1,0:T(8,128)}, u32[]{:S(2)}) copy-start(f32[1024,512]{1,0:T(8,128)} %fusion.18) | copy-start | bytes 6291460
  179.7 1.6 copy-start.12
  183.6 42.6 %all-to-all-start.2 = ((bf16[64,36,512]{2,1,0:T(8,128)(2,1)}), bf16[64,36,512]{2,1,0:T(8,128)(2,1)}, u32[]{:S(2)}, u32[]{:S(2)}) async-start(bf16[64,36,512]{2,1,0:T(8,128)(2,1)} %pad_maximum_fusion), calls=%async_computation.2 | async-start | bytes 5242880 | tf_op jit(solution)/shard_map/all_to_all | solution.py:337
  228.7 2.7 %copy-start.1 = (bf16[2048,256]{1,0:T(8,128)(2,1)S(1)}, bf16[2048,256]{1,0:T(8,128)(2,1)}, u32[]{:S(2)}) copy-start(bf16[2048,256]{1,0:T(8,128)(2,1)} %param.18) | copy-start | bytes 3145732
  (6 other events, 5.2 us)

commit v2 on v0

v2 whole, which is shorter than its diff:
```python
import functools

import jax
import jax.numpy as jnp
from jax import lax
from jax.experimental import pallas as pl
from jax.experimental.pallas import tpu as pltpu
from jax.sharding import Mesh
from jax.sharding import PartitionSpec as P

HEAD_DIM = 128
SEQ_MOST = 64
SEQS = 4
CAP = 4
eps = 1e-05
DEV = ("y", "z", "x")
f32 = jnp.float32
bf16 = jnp.bfloat16
NN = ((1,), (0,))
NT = ((1,), (1,))
TN = ((0,), (0,))


def swap(part):
    return lax.ppermute(part, "section", [(0, 1), (1, 0)])


def shifted(part, axis, step):
    count = lax.axis_size(axis)
    return lax.ppermute(part, axis, [(i, (i + step) % count) for i in range(count)])


def member():
    return lax.rem(lax.axis_index("x"), 2) + 2 * lax.rem(lax.axis_index("y"), 2)


def from_member(part, other):
    count = lax.axis_size("x")
    flip = count * (other // 2) + other % 2
    return lax.ppermute(part, ("y", "x"), [(i, i ^ flip) for i in range(lax.axis_size("y") * count)])


def dot(left, right, dims):
    return lax.dot_general(left, right, (dims, ((), ())), preferred_element_type=f32)


def iota(shape, dim):
    return lax.broadcasted_iota(jnp.int32, shape, dim)


def row_norm(argument):
    row_mean = jnp.mean(argument, axis=-1, keepdims=True)
    centered = argument - row_mean
    variance = jnp.mean(centered * centered, axis=-1, keepdims=True)
    inverse = lax.rsqrt(variance + eps)
    return (centered * inverse, inverse)


def norm_back(incoming, normed, inverse):
    mean_in = jnp.mean(incoming, axis=-1, keepdims=True)
    mean_dot = jnp.mean(incoming * normed, axis=-1, keepdims=True)
    return (incoming - mean_in - normed * mean_dot) * inverse


def call(kernel, name, outs, args, kinds, after=(), scratch=(), limit=56, flops=0, token=False):
    in_kinds, out_kinds = kinds.split()
    if token:
        outs, out_kinds = [*outs, ((8, 128), f32)], out_kinds + "V"
    assert len(in_kinds) == len(args) and len(out_kinds) == len(outs), name
    spaces = {"V": pltpu.VMEM, "S": pltpu.SMEM, "H": pl.ANY, "R": pl.ANY}
    held = [pltpu.VMEM(a.shape, a.dtype) for a, k in zip(args, in_kinds) if k == "H"]
    held += [pltpu.VMEM(s, d) for (s, d), k in zip(outs, out_kinds) if k == "H"]
    sems = [pltpu.SemaphoreType.DMA((len(held),))] if held else []

    def run(*refs):
        ins = list(refs[: len(args)])
        refs = refs[len(args) + len(after) :]
        results = list(refs[: len(outs)])
        buffers = list(refs[len(outs) : len(outs) + len(held)])
        rest = refs[len(outs) + len(held) + len(sems) :]
        sem = refs[len(outs) + len(held)] if held else None
        count = 0
        first, last = [], []
        for i, kind in enumerate(in_kinds):
            if kind == "H":
                first.append(pltpu.make_async_copy(ins[i], buffers[count], sem.at[count]))
                first[-1].start()
                ins[i] = buffers[count]
                count += 1
        for i, kind in enumerate(out_kinds):
            if kind == "H":
                last.append(pltpu.make_async_copy(buffers[count], results[i], sem.at[count]))
                results[i] = buffers[count]
                count += 1
        for copy in first:
            copy.wait()
        if token:
            results.pop()[...] = jnp.zeros((8, 128), f32)
        kernel(*ins, *results, *rest)
        for copy in last:
            copy.start()
        for copy in last:
            copy.wait()

    return pl.pallas_call(
        run,
        in_specs=[pl.BlockSpec(memory_space=spaces[k]) for k in in_kinds] + [pl.BlockSpec(memory_space=pl.ANY)] * len(after),
        out_specs=[pl.BlockSpec(memory_space=spaces[k]) for k in out_kinds],
        out_shape=[jax.ShapeDtypeStruct(s, d) for s, d in outs],
        scratch_shapes=held + sems + list(scratch),
        compiler_params=pltpu.CompilerParams(vmem_limit_bytes=limit * 2**20),
        cost_estimate=pl.CostEstimate(flops=flops, bytes_accessed=0, transcendentals=0),
        name=name,
    )(*args, *after)


def one_hot(slots_row, count):
    return jnp.where(iota((count, slots_row.shape[1]), 0) == slots_row, 1.0, 0.0).astype(bf16)


def dispatch_kernel(owners, books, half, cluster_ref, item_ref, saved_ref, sent_ref, slot_ref, mark_ref):
    micro, rows = cluster_ref.shape
    width = saved_ref.shape[2]
    each = micro * CAP
    before = jnp.where(iota((rows, rows), 0) < iota((rows, rows), 1), 1.0, 0.0).astype(bf16)
    same = jnp.where(iota((rows, rows), 0) == iota((rows, rows), 1), 1.0, 0.0).astype(bf16)
    kind = iota((128, rows), 0)
    rows_out, codes_out = 0.0, 0.0
    for m in range(micro):
        target, item = cluster_ref[m : m + 1], item_ref[m : m + 1]
        owner, local = target // books, target % books
        marks = jnp.where(iota((owners, rows), 0) == owner, 1.0, 0.0)
        earlier = dot(marks.astype(bf16), before, NN)
        rank = jnp.sum(earlier * marks, axis=0, keepdims=True).astype(jnp.int32)
        slot = owner * each + m * CAP + rank
        slot_ref[m : m + 1] = slot
        code = jnp.where(
            kind == 0,
            local + 1,
            jnp.where(kind == 1, item // half, jnp.where(kind == 2, item % half, jnp.where(kind == 3, owner, 0))),
        )
        code = code.astype(f32).astype(bf16)
        pick = one_hot(slot, owners * each)
        rows_out += dot(pick, saved_ref[m], NN)
        codes_out += dot(pick, code, NT)
        turned = dot(same, code, NT)
        mark_ref[m * rows : (m + 1) * rows] = jnp.broadcast_to(
            turned[:, 3:4] * books + turned[:, 0:1] - 1.0, (rows, 128)
        )
    sent_ref[:, :width] = rows_out.astype(bf16)
    sent_ref[:, width:] = codes_out.astype(bf16)


def top_logits_kernel(saved_ref, table_ref, logit_ref, stat_ref):
    logits = dot(saved_ref[...], table_ref[...], NT)
    logit_ref[...] = logits
    peak = jnp.max(logits, axis=1, keepdims=True)
    mass = jnp.sum(jnp.exp(logits - peak), axis=1, keepdims=True)
    stat_ref[...] = jnp.where(iota(stat_ref.shape, 1) == 0, peak, mass)


def joined(mine_ref, other_ref):
    peak_a, mass_a = mine_ref[:, 0:1], mine_ref[:, 1:2]
    peak_b, mass_b = other_ref[:, 0:1], other_ref[:, 1:2]
    peak = jnp.maximum(peak_a, peak_b)
    return peak, mass_a * jnp.exp(peak_a - peak) + mass_b * jnp.exp(peak_b - peak)


def top_grad_kernel(group, own, logit_ref, mine_ref, other_ref, mark_ref, table_ref, saved_ref, *out_refs):
    row_ref, grad_refs = out_refs[0], out_refs[1:]
    half = table_ref.shape[0]
    quarter = half // group
    piece = own // group
    base = lax.axis_index("section") * half
    me = lax.axis_index("z")
    peak, mass = joined(mine_ref, other_ref)
    target = mark_ref[:, 0:1].astype(jnp.int32) - base
    total = 0.0
    column = iota((mark_ref.shape[0], quarter), 1)
    for q in range(group):
        index = (column // piece) * own + q * piece + column % piece
        cols = pl.ds(q * quarter, quarter)
        probs = jnp.exp(logit_ref[:, cols] - peak) / mass
        grad = (probs - jnp.where(index == target, 1.0, 0.0)).astype(bf16)
        total += dot(grad, table_ref[cols, :], NN)
        for s in range(group):

            @pl.when(lax.rem(me + s, group) == q)
            def _(s=s, grad=grad):
                grad_refs[s][:, :quarter] = grad
                grad_refs[s][:, quarter:] = saved_ref[...]

    row_ref[...] = total


def table_kernel(owners, *refs):
    *in_refs, out_ref = refs
    quarter = in_refs[0].shape[1] - 256
    total = sum(dot(r[:, :quarter], r[:, quarter:], TN) for r in in_refs)
    left = total[:, :128].reshape(owners, -1, 128)
    right = total[:, 128:].reshape(owners, -1, 128)
    out_ref[...] = jnp.concatenate([left, right], axis=1).astype(bf16)


def masked_product(code_ref, left_ref, width, book_ref, out_ref, dims, group, ready):
    lines = 256
    out_ref[...] = jnp.zeros_like(out_ref)

    def step(i, carry):
        ready(i)
        books = book_ref[pl.ds(i * group, group)]
        if dims == NT:
            right = jnp.concatenate([books[k] for k in range(group)], axis=1)
        else:
            right = books.reshape(-1, books.shape[2])
        for r in range(0, out_ref.shape[0], lines):
            some = pl.ds(r, lines)
            left, code = left_ref[some, :width], code_ref[some, :]
            parts = []
            for k in range(group):
                here = code == (i * group + k + 1).astype(f32).astype(bf16)
                parts.append(jnp.where(here, left, jnp.zeros_like(left)))
            out_ref[some, :] += dot(jnp.concatenate(parts, axis=1), right, dims)
        return carry

    lax.fori_loop(0, book_ref.shape[0] // group, step, 0)


GROUP_LIMIT = 40
BOOK_GROUP = 16
BOOK_COPIES = 4


def leaf_scores_kernel(got_in, book_in, out_ref, stat_ref, got_ref, book_ref, code_ref, got_sem, sem):
    width = book_ref.shape[2]
    steps = book_ref.shape[0] // BOOK_GROUP
    piece = BOOK_GROUP // BOOK_COPIES

    def copies(i):
        for j in range(BOOK_COPIES):
            some = pl.ds(i * BOOK_GROUP + j * piece, piece)
            yield pltpu.make_async_copy(book_in.at[some], book_ref.at[some], sem.at[i, j])

    got_copy = pltpu.make_async_copy(got_in, got_ref, got_sem)
    got_copy.start()
    for i in range(2):
        for copy in copies(i):
            copy.start()
    got_copy.wait()
    code_ref[...] = jnp.broadcast_to(got_ref[:, width : width + 1], code_ref.shape)

    def ready(i):
        for copy in copies(i):
            copy.wait()

        @pl.when(i + 2 < steps)
        def _():
            for copy in copies(i + 2):
                copy.start()

    masked_product(code_ref, got_ref, width, book_ref, out_ref, NT, BOOK_GROUP, ready)
    scores = out_ref[...]
    peak = jnp.max(scores, axis=1, keepdims=True)
    mass = jnp.sum(jnp.exp(scores - peak), axis=1, keepdims=True)
    stat_ref[...] = jnp.where(iota(stat_ref.shape, 1) == 0, peak, mass)


def leaf_back_kernel(got_ref, score_ref, mine_ref, other_ref, book_ref, back_ref, grad_ref, code_ref, total_ref):
    items, width = book_ref.shape[1:]
    code = got_ref[:, width : width + 1]
    code_ref[...] = jnp.broadcast_to(code, code_ref.shape)
    high = got_ref[:, width + 1 : width + 2].astype(f32).astype(jnp.int32)
    low = got_ref[:, width + 2 : width + 3].astype(f32).astype(jnp.int32)
    peak, mass = joined(mine_ref, other_ref)
    probs = jnp.exp(score_ref[...] - peak) / mass
    hit = (iota(probs.shape, 1) == low) & (high == lax.axis_index("section"))
    grad = jnp.where(code.astype(f32) > 0, probs - jnp.where(hit, 1.0, 0.0), 0.0)
    grad_ref[...] = grad.astype(bf16)
    masked_product(code_ref, grad_ref, items, book_ref, total_ref, NN, 32, lambda i: None)
    back_ref[...] = total_ref[...].astype(bf16)


def leaf_book_kernel(got_ref, grad_ref, out_ref, code_ref, turned_ref, held_ref, sem):
    books, items, width = out_ref.shape
    group = books // sem.shape[0]
    slots = got_ref.shape[0]
    turned_ref[...] = grad_ref[...].astype(f32).T.astype(bf16)
    code_ref[...] = jnp.broadcast_to(got_ref[:, width : width + 1].astype(f32), (slots, items)).T.astype(bf16)
    rows = got_ref[:, :width]
    copies = []
    for i in range(books // group):
        some = pl.ds(i * group, group)
        turned, code = turned_ref[...], code_ref[...]
        parts = []
        for k in range(group):
            here = code == (i * group + k + 1)
            parts.append(jnp.where(here, turned, jnp.zeros_like(turned)))
        grads = dot(jnp.concatenate(parts, axis=0), rows, NN)
        held_ref[some] = grads.reshape(group, items, width).astype(bf16)
        copies.append(pltpu.make_async_copy(held_ref.at[some], out_ref.at[some], sem.at[i]))
        copies[-1].start()
    for copy in copies:
        copy.wait()


def leaf_scores(got, book, after):
    books, items, width = book.shape
    slots = got.shape[0]
    return call(
        leaf_scores_kernel,
        "leaf_scores",
        [((slots, items), f32), ((slots, 128), f32), (got.shape, bf16), (book.shape, bf16)],
        (got, book),
        "RR VVVV", limit=42,
        flops=2 * slots * books * items * width,
        scratch=[
            pltpu.VMEM((slots, width), bf16),
            pltpu.SemaphoreType.DMA,
            pltpu.SemaphoreType.DMA((books // BOOK_GROUP, BOOK_COPIES)),
        ],
        after=after,
    )


def leaf_back(got, scores, mine, other, book, after):
    books, items, width = book.shape
    slots = got.shape[0]
    return call(
        leaf_back_kernel,
        "leaf_back",
        [((slots, width), bf16), ((slots, items), bf16)],
        (got, scores, mine, other, book),
        "VVVVV HH",
        limit=28,
        scratch=[pltpu.VMEM((slots, items), bf16), pltpu.VMEM((slots, width), f32)],
        after=after,
    )


def leaf_book(got, grads, books, width, after):
    slots, items = grads.shape
    group = 4
    return call(
        leaf_book_kernel,
        "leaf_book",
        [((books, items, width), bf16)],
        (got, grads),
        "HH R",
        scratch=[
            pltpu.VMEM((items, slots), bf16),
            pltpu.VMEM((items, slots), bf16),
            pltpu.VMEM((books, items, width), bf16),
            pltpu.SemaphoreType.DMA((books // group,)),
        ],
        after=after,
    )[0]


def slope_of(argument, logistic):
    return logistic * (1.0 + argument * (1.0 - logistic))


def norms_kernel(length_ref, input_ref, out_ref):
    micro, rows, width = input_ref.shape
    for m in range(micro):
        out_ref[m * rows : (m + 1) * rows] = row_norm(input_ref[m].astype(f32))[0].astype(bf16)
    seqs = length_ref.shape[2]
    lane = iota((16, width), 1)
    held = jnp.zeros((16, width), f32)
    for m in range(micro):
        for i in range(seqs):
            held = jnp.where(lane == m * seqs + i, length_ref[m, 0, i].astype(f32), held)
    out_ref[micro * rows :] = held.astype(bf16)


def seq_mask(sizes, rows):
    row, col = iota((rows, rows), 0), iota((rows, rows), 1)
    row_seg, col_seg, end = 0, 0, 0
    for size in sizes:
        end = end + size
        row_seg += jnp.where(row >= end, 1, 0)
        col_seg += jnp.where(col >= end, 1, 0)
    return jnp.where((row_seg == col_seg) & (col <= row), 1.0 / SEQ_MOST, 0.0)


def held_sizes(held, m):
    held = held.astype(f32)[0:1].astype(jnp.int32)
    return [held[:, m * SEQS + i : m * SEQS + i + 1] for i in range(SEQS)]


def attend_all(acts, masks):
    scores = [dot(query, key, NT) for _, _, query, key in acts]
    logistics = [jax.nn.sigmoid(score) for score in scores]
    attention = [(a * b * mask).astype(bf16) for a, b, mask in zip(scores, logistics, masks)]
    mixed = [dot(a, act[1], NN) for a, act in zip(attention, acts)]
    back = [slope_of(a, b) * mask for a, b, mask in zip(scores, logistics, masks)]
    normed = [row_norm(one) for one in mixed]
    return [(a, b, n, jnp.broadcast_to(i, n.shape)) for a, b, (n, i) in zip(attention, back, normed)]


def my_head():
    return pl.ds(pl.multiple_of(member() * HEAD_DIM, HEAD_DIM), HEAD_DIM)


def group_forward_kernel(*refs):
    *norm_ins, weight_in, act_ref, slope_ref, att_ref, back_ref, out_ref, inverse_ref, prod_ref = refs[:-3]
    weight_ref, norm_ref, sem = refs[-3:]
    pairs = [(weight_in.at[:, :, my_head()], weight_ref)] + [(one, norm_ref.at[s]) for s, one in enumerate(norm_ins)]
    copies = [pltpu.make_async_copy(a, b, sem.at[i]) for i, (a, b) in enumerate(pairs)]
    for copy in copies:
        copy.start()
    for copy in copies:
        copy.wait()
    rows = att_ref.shape[1]
    total = out_ref.shape[0] // len(norm_ins)
    weight = jnp.concatenate([weight_ref[t] for t in range(4)], axis=1)
    acts, masks, spans = [], [], []
    for s in range(len(norm_ins)):
        for m in range(total // rows):
            lines = pl.ds(s * total + m * rows, rows)
            pre_act = dot(norm_ref[s, m * rows : (m + 1) * rows, :], weight, NN)
            logistic = jax.nn.sigmoid(pre_act)
            act = (pre_act * logistic).astype(bf16)
            act_ref[lines, :] = act
            slope_ref[lines, :] = slope_of(pre_act, logistic)
            spans.append(lines)
            masks.append(seq_mask(held_sizes(norm_ref[s, total:, :128], m), rows))
            acts.append([act[:, t * HEAD_DIM : (t + 1) * HEAD_DIM] for t in range(4)])
    for lines, act, result in zip(spans, acts, attend_all(acts, masks)):
        att_ref[lines, :], back_ref[lines, :], out_ref[lines, :], inverse_ref[lines, :] = result
        prod_ref[lines, :] = (result[2] * act[0].astype(f32)).astype(bf16)


def attend_back_all(incoming, acts, results):
    mixed = [
        norm_back(a * act[0].astype(f32), normed, inverse).astype(bf16)
        for a, act, (_, _, normed, inverse) in zip(incoming, acts, results)
    ]
    grads = [dot(a, act[1], NT) for a, act in zip(mixed, acts)]
    values = [dot(result[0], a, TN) for result, a in zip(results, mixed)]
    grads = [(a * result[1]).astype(bf16) for a, result in zip(grads, results)]
    queries = [dot(a, act[3], NN) for a, act in zip(grads, acts)]
    keys = [dot(a, act[2], TN) for a, act in zip(grads, acts)]
    gates = [a * result[2] for a, result in zip(incoming, results)]
    return list(zip(gates, values, queries, keys))


def rows_kernel(slot_ref, returned_ref, top_ref, out_ref):
    micro, rows = slot_ref.shape
    for m in range(micro):
        lines = pl.ds(m * rows, rows)
        pick = one_hot(slot_ref[m : m + 1], returned_ref.shape[0])
        out_ref[lines, :] = top_ref[lines, :] + dot(pick, returned_ref[...], TN)


def add_kernel(mine_ref, other_ref, out_ref):
    out_ref[...] = (mine_ref[...] + other_ref[...]).astype(bf16)


def trunk_kernel(length_ref, norm_ref, row_ref, proj_ref, mix_ref, weight_in, og_ref, part_ref, pre_ref, weight_ref, sem):
    copies = [pltpu.make_async_copy(weight_in.at[t], weight_ref.at[t], sem.at[t]) for t in range(4)]
    for copy in copies:
        copy.start()
    rows = HEAD_DIM
    total, cols = row_ref.shape[0], weight_ref.shape[2]
    out_grad = dot(row_ref[...], proj_ref[...], NT).astype(bf16)
    og_ref[...] = out_grad
    grad_product = dot(out_grad, mix_ref[...], NT)
    for copy in copies:
        copy.wait()
    for m in range(total // rows):
        lines = pl.ds(m * rows, rows)
        normed = norm_ref[lines, :]
        acts, slopes = [], []
        for t in range(4):
            pre_act = dot(normed, weight_ref[t], NN)
            logistic = jax.nn.sigmoid(pre_act)
            acts.append((pre_act * logistic).astype(bf16))
            slopes.append(slope_of(pre_act, logistic))
        heads = [slice(h * HEAD_DIM, (h + 1) * HEAD_DIM) for h in range(cols // HEAD_DIM)]
        acts = [[act[:, lanes] for act in acts] for lanes in heads]
        masks = [seq_mask([length_ref[m, 0, i] for i in range(SEQS)], rows)] * len(heads)
        incoming = [grad_product[m * rows : (m + 1) * rows, lanes] for lanes in heads]
        for lanes, grads in zip(heads, attend_back_all(incoming, acts, attend_all(acts, masks))):
            for t, grad in enumerate(grads):
                pre_ref[t, lines, lanes] = (grad * slopes[t][:, lanes]).astype(bf16)
    part_ref[...] = sum(dot(pre_ref[t], weight_ref[t], NT) for t in range(4))


def inputs_kernel(input_ref, og_ref, mine_ref, other_ref, out_ref):
    micro, rows, _ = input_ref.shape
    for m in range(micro):
        lines = pl.ds(m * rows, rows)
        normed, inverse = row_norm(input_ref[m].astype(f32))
        grad = norm_back(mine_ref[lines, :] + other_ref[lines, :], normed, inverse)
        out_ref[m] = (og_ref[lines, :].astype(f32) + grad).astype(bf16)


def weights_kernel(group, owners, *refs):
    row_refs, norm_refs = refs[:group], refs[group : 2 * group]
    act_ref, slope_ref, att_ref, back_ref, out_ref, inverse_ref, prod_ref, proj_ref, mix_ref, table_ref, packed_ref = refs[2 * group :]
    total = row_refs[0].shape[0]
    rows = att_ref.shape[1]
    cols = act_ref.shape[1]
    count = total // rows
    mix = mix_ref[my_head(), :]
    mixing, expand = 0.0, 0.0
    spans, incoming = [], []
    for s in range(group):
        out_grad = dot(row_refs[s][...], proj_ref[...], NT).astype(bf16)
        mixing += dot(out_grad, prod_ref[s * total : (s + 1) * total, :], TN)
        grad_product = dot(out_grad, mix, NT)
        for m in range(count):
            spans.append(pl.ds(s * total + m * rows, rows))
            incoming.append(grad_product[m * rows : (m + 1) * rows])
    packed_ref[:, :, cols : cols + HEAD_DIM] = mixing.reshape(owners, -1, HEAD_DIM).astype(bf16)
    packed_ref[:, :, cols + HEAD_DIM :] = table_ref[...]
    acts = [[act_ref[lines, t * HEAD_DIM : (t + 1) * HEAD_DIM] for t in range(4)] for lines in spans]
    results = [(att_ref[lines, :], back_ref[lines, :], out_ref[lines, :], inverse_ref[lines, :]) for lines in spans]
    grads = attend_back_all(incoming, acts, results)
    pre = [(jnp.concatenate(grad, axis=1) * slope_ref[lines, :]).astype(bf16) for grad, lines in zip(grads, spans)]
    for s in range(group):
        expand += dot(norm_refs[s][:total, :], jnp.concatenate(pre[s * count : (s + 1) * count], axis=0), TN)
    packed_ref[:, :, :cols] = expand.reshape(owners, -1, cols).astype(bf16)


def final_kernel(group, in_ref, expand_ref, mixing_ref, table_ref):
    cols = expand_ref.shape[2]
    side = range(group)
    for g in side:
        sources = [(y * group + z) * group + x for y in side for z in side for x in side if x % 2 + 2 * (y % 2) == g]
        total = sum(in_ref[i, :, : cols + HEAD_DIM].astype(f32) for i in sources)
        head = pl.ds(g * HEAD_DIM, HEAD_DIM)
        for t in range(4):
            expand_ref[:, t, head] = total[:, t * HEAD_DIM : (t + 1) * HEAD_DIM]
        mixing_ref[:, head] = total[:, cols:]
    lanes = pl.ds(cols + HEAD_DIM, HEAD_DIM)
    for z in side:
        total = sum(in_ref[(y * group + z) * group + x, :, lanes].astype(f32) for y in side for x in side)
        half = total.shape[0] // 2
        table_ref[z * half : (z + 1) * half, :HEAD_DIM] = total[:half]
        table_ref[z * half : (z + 1) * half, HEAD_DIM:] = total[half:]


def body(
    inputs,
    lengths,
    expand_weight,
    mixing_weight,
    projection,
    saved_rows,
    cluster_ids,
    item_ids,
    top_table,
    codebook,
):
    micro, rows, model_width = inputs.shape
    total = micro * rows
    owners = lax.axis_size(DEV)
    group = lax.axis_size("x")
    half_clusters, width = top_table.shape
    books, items, _ = codebook.shape
    cols = expand_weight.shape[2]
    slots = owners * micro * CAP
    own = half_clusters // owners
    saved = saved_rows.reshape(total, width)

    sent, slot_ids, marks = call(
        functools.partial(dispatch_kernel, owners, books, items),
        "dispatch",
        [((slots, width + 128), bf16), ((micro, rows), jnp.int32), ((total, 128), f32)],
        (cluster_ids, item_ids, saved_rows),
        "HHH HVH", limit=56,
    )
    got = lax.all_to_all(sent.reshape(owners, slots // owners, -1), DEV, 0, 0, tiled=True).reshape(slots, -1)

    (normed,) = call(
        norms_kernel,
        "norms",
        [((total + 16, model_width), bf16)],
        (lengths, inputs),
        "SV V",
        limit=28,
        after=(slot_ids,),
    )
    normed_all = [normed] + [from_member(normed, s) for s in range(1, group)]
    table = top_table.reshape(owners, group, own // group, width).swapaxes(0, 1).reshape(half_clusters, width)
    logits, stats = call(
        top_logits_kernel,
        "top_logits",
        [((total, half_clusters), f32), ((total, 128), f32)],
        (saved, table),
        "HH VV",
        limit=40,
        after=(slot_ids,),
    )
    row_top, *top_grads, top_token = call(
        functools.partial(top_grad_kernel, group, own),
        "top_grads",
        [((total, width), f32)] + [((total, half_clusters // group + width), bf16)] * group,
        (logits, stats, swap(stats), marks, table, saved),
        "VVVHHH " + "H" * (1 + group),
        limit=40,
        token=True,
    )
    top_all = [top_grads[0]] + [shifted(top_grads[s], "z", s) for s in range(1, group)]

    leaf, leaf_stats, got_held, book_held = leaf_scores(got, codebook, (top_token, normed[:8, :128]))
    back, leaf_grad = leaf_back(
        got_held, leaf, leaf_stats, swap(leaf_stats), book_held, ()
    )
    returned = lax.all_to_all(back.reshape(owners, slots // owners, width), DEV, 0, 0, tiled=True)

    late_weight, _ = lax.optimization_barrier((expand_weight, back))
    weight = lax.optimization_barrier(late_weight.swapaxes(0, 1))
    window_token = sum((a[:8, :128] for a in normed_all[1:]), weight[0, :8, :128])
    table_part, table_token = call(
        functools.partial(table_kernel, owners),
        "table_part",
        [((owners, 16, 128), bf16)],
        top_all,
        "H" * group + " H",
        after=(back, window_token),
        token=True,
    )

    (row_part,) = call(
        rows_kernel,
        "rows",
        [((total, width), f32)],
        (slot_ids, returned.reshape(slots, width), row_top),
        "VHH V", limit=28,
        after=(table_token,),
    )
    (row_grad,) = call(add_kernel, "row_grad", [((total, width), bf16)], (row_part, swap(row_part)), "VV V", limit=28)
    row_all = [row_grad] + [from_member(row_grad, s) for s in range(1, group)]

    group_rows = group * total
    group_forward = call(
        group_forward_kernel,
        "group_forward",
        [
            ((group_rows, 4 * HEAD_DIM), bf16),
            ((group_rows, 4 * HEAD_DIM), f32),
            ((group_rows, rows), bf16),
            ((group_rows, rows), f32),
            ((group_rows, HEAD_DIM), f32),
            ((group_rows, HEAD_DIM), f32),
            ((group_rows, HEAD_DIM), bf16),
        ],
        (*normed_all, weight),
        "R" * (group + 1) + " " + "V" * 7,
        limit=GROUP_LIMIT,
        after=(row_grad,),
        scratch=[
            pltpu.VMEM((4, model_width, HEAD_DIM), bf16),
            pltpu.VMEM((group, total + 16, model_width), bf16),
            pltpu.SemaphoreType.DMA((group + 1,)),
        ],
    )

    (packed,) = call(
        functools.partial(weights_kernel, group, owners),
        "weight_parts",
        [((owners, model_width // owners, cols + 2 * HEAD_DIM), bf16)],
        (*row_all, *normed_all, *group_forward, projection, mixing_weight, table_part),
        "V" * (2 * group + 10) + " H",
        limit=28,
    )
    arrived = lax.all_to_all(packed, DEV, 0, 0, tiled=True)

    out_grad, grad_part = call(
        trunk_kernel,
        "trunk",
        [((total, model_width), bf16), ((total, model_width), f32)],
        (lengths, normed, row_grad, projection, mixing_weight, weight),
        "SHHHHR VV",
        limit=48,
        scratch=[pltpu.VMEM((4, total, cols), bf16), pltpu.VMEM(weight.shape, bf16), pltpu.SemaphoreType.DMA((4,))],
        after=(packed,),
    )
    (grad_inputs,) = call(
        inputs_kernel, "input_grads", [(inputs.shape, bf16)], (inputs, out_grad, grad_part, swap(grad_part)), "HVVV H", limit=48
    )
    book_grads = leaf_book(got, leaf_grad, books, width, (packed,))
    share = model_width // owners
    expand, mixing, table_share = call(
        functools.partial(final_kernel, group),
        "weight_sums",
        [((share, 4, cols), f32), ((share, cols), f32), ((own, width), f32)],
        (arrived,),
        "V HHH",
        limit=28,
    )
    return grad_inputs, expand, mixing.T, table_share, book_grads


def solution(mesh):
    grid = Mesh(mesh.devices.reshape(2, 4, 4, 4), ("section",) + DEV)
    return jax.shard_map(
        body,
        mesh=grid,
        in_specs=(
            P(None, DEV, None),
            P(None, DEV, None),
            P(None, None, "section"),
            P("section", None),
            P(),
            P(None, DEV, None),
            P(None, DEV),
            P(None, DEV),
            P("section", None),
            P(DEV, "section", None),
        ),
        out_specs=(
            P(None, DEV, None),
            P(DEV, None, "section"),
            P("section", DEV),
            P(("section",) + DEV, None),
            P(DEV, "section", None),
        ),
        check_vma=False,
    )
```

time: 1480 us -> 123 us (0.08)
  waiting for transfers between devices: 1030 us -> 7.52 us
  matrix products: 150 us -> 0 us
  local copies, waits for them, and re-layouts: 159 us -> 19.3 us
  Pallas kernels: 0 us -> 50.2 us
  other arithmetic: 37.6 us -> 0.59 us
  blocking collectives: 19.3 us -> 0 us
    reduce_scatter x3 -> x0, waiting for transfers between devices: 1000 us -> none  [the longest x1 351 us: body(): lax.psum_scatter(grad_mixing, 'dev', scatter_dimension=1, tiled=True)]
    dot_general x40 -> x0, matrix products: 150 us -> none  [the longest x8 49.2 us: contract_rows(): lax.dot_general(left, right, (((0,), (0,)), ((), ())), preferred_element_...]
    gather x10 -> x0, local copies, waits for them, and re-layouts: 93.6 us -> none  [the longest x4 45.8 us: leaf_scores(): book_rows = codebook[pair[1]]]
    pallas_call x0 -> x15, Pallas kernels: none -> 50.2 us  [call(): pl.pallas_call(run, in_specs=[pl.BlockSpec(memory_space=spaces[k]) for k...]
    unnamed x156 -> x46, local copies, waits for them, and re-layouts: 42.4 us -> 15 us
    all_to_all x6 -> x3, starting transfers between devices: 55.1 us -> 30.3 us  [the longest x1 11.6 us: body(): lax.all_to_all(sent.reshape(owners, slots // owners, -1), DEV, 0, 0, tile...]
  transfers between devices with their start and end apart: 11 -> 16, of which waited for: 7 -> 2; matrix products, arithmetic and copies ran while one was open for 19% -> 4% of each run, Pallas kernels for 0% -> 34%
where the time goes in v2:
time: 123 us; the launch traced here: 122 us
  Pallas kernels  50.2 us (41%)
  starting transfers between devices  43.5 us (35%)
  local copies, waits for them, and re-layouts  19.3 us (16%)
  waiting for transfers between devices  7.52 us (6%)
    pallas_call x15, Pallas kernels, call(): pl.pallas_call(run, in_specs=[pl.BlockSpec(memory_space=spaces[k]) for k...  50.2 us
    unnamed x46, local copies, waits for them, and re-layouts  15 us
    all_to_all x1, starting transfers between devices, body(): lax.all_to_all(sent.reshape(owners, slots // owners, -1), DEV, 0, 0, tile...  11.6 us
    all_to_all x1, starting transfers between devices, body(): arrived = lax.all_to_all(packed, DEV, 0, 0, tiled=True)  10.4 us
    all_to_all x1, starting transfers between devices, body(): lax.all_to_all(back.reshape(owners, slots // owners, width), DEV, 0, 0, t...  8.24 us
    ppermute x6, starting transfers between devices, from_member(): lax.ppermute(part, ('y', 'x'), [(i, i ^ flip) for i in range(lax.axis_siz...  7.14 us
    all_to_all x1, waiting for transfers between devices, body(): arrived = lax.all_to_all(packed, DEV, 0, 0, tiled=True)  5.94 us
    ppermute x3, starting transfers between devices, shifted(): lax.ppermute(part, axis, [(i, (i + step) % count) for i in range(count)])  5.77 us
  transfers between devices with their start and end apart: 16, of which 2 were waited for; matrix products, arithmetic and copies ran while one was open for 4% of the time, Pallas kernels for 34%

profile of v2, /device:TPU:0, one launch (start us, length us, event | category | flops | bytes accessed | tf_op | source)
XLA Modules:
  0.0 122.3 jit_solution(3558643834178870148)
XLA Ops:
  0.7 2.9 %dispatch.1 = (bf16[512,384]{1,0:T(8,128)(2,1)}, s32[2,128]{1,0:T(2,128)}, f32[256,128]{1,0:T(8,128)}) custom-call(s32[2,128]{1,0:T(2,128)} %refs_0_.4, s32[2,128]{1,0:T(2,128)} %refs_1_.3, bf16[2,128,256]{2,1,0:T(8,128)(2,1)} %refs_2_.1), custom_call_target="tpu_custom_call" | custom-call | tf_op jit(solution)/shard_map/dispatch/pallas_call | solution.py:105
  3.6 11.6 %all-to-all-start = ((bf16[64,8,384]{2,1,0:T(8,128)(2,1)}), bf16[64,8,384]{2,1,0:T(8,128)(2,1)S(1)}, u32[]{:S(2)}, u32[]{:S(2)}) async-start(bf16[64,8,384]{2,1,0:T(8,128)(2,1)} %bitcast.28), calls=%async_computation | async-start | bytes 786432 | tf_op jit(solution)/shard_map/all_to_all | solution.py:575
  15.3 1.3 %copy.15 = bf16[64,4,8,256]{3,2,0,1:T(8,128)(2,1)S(1)} copy(bf16[64,4,8,256]{3,2,1,0:T(8,128)(2,1)} %bitcast.27) | data formatting | bytes 2097152 | tf_op jit(solution)/shard_map/reshape | solution.py:587
  16.6 0.9 copy-done.10
  17.5 0.7 copy-done.17
  18.1 1.1 top_logits.1
  19.2 0.1 collective-permute-start
  19.3 0.7 copy-done.18
  20.0 0.9 norms.1.refs_0_.refs_4_.refs_1_
  20.9 2.6 %collective-permute-start.7 = (bf16[272,1024]{1,0:T(8,128)(2,1)S(1)}, bf16[272,1024]{1,0:T(8,128)(2,1)S(1)}, u32[]{:S(2)}, u32[]{:S(2)}) collective-permute-start(bf16[272,1024]{1,0:T(8,128)(2,1)S(1)} %norms.1.refs_0_.refs_4_.refs_1_), channel_id=1, source_target_pairs={{0,17},{1,16},{2,19},{3,18},{16,1},{17,0},{18,3},{19,2},{32,49},{3... | collective-permute-start | bytes 1671176 | tf_op jit(solution)/shard_map/ppermute | solution.py:40
  23.4 0.6 collective-permute-start.6
  24.0 0.5 collective-permute-start.5
  24.4 2.9 %top_grads.1 = (f32[256,256]{1,0:T(8,128)S(1)}, bf16[256,768]{1,0:T(8,128)(2,1)S(1)}, bf16[256,768]{1,0:T(8,128)(2,1)}, bf16[256,768]{1,0:T(8,128)(2,1)}, bf16[2...) custom-call(f32[256,2048]{1,0:T(8,128)S(1)} %get-tuple-element.39.refs_0_, f32[256,128]{1,0:T(8,128)S(1)} %get-tuple-element.40.refs_1_, ...), custom_call_target="tpu_custom_call" | custom-call | tf_op jit(solution)/shard_map/top_grads/pallas_call | solution.py:105
  27.4 0.7 copy-done.11
  28.1 0.7 copy-done.13
  28.8 7.5 %leaf_scores.1 = (f32[512,256]{1,0:T(8,128)S(1)}, f32[512,128]{1,0:T(8,128)S(1)}, bf16[512,384]{1,0:T(8,128)(2,1)S(1)}, bf16[64,256,256]{2,1,0:T(8,128)(2,1)S(1)}) custom-call(bf16[512,384]{1,0:T(8,128)(2,1)S(1)} %bitcast.22, bf16[64,256,256]{2,1,0:T(8,128)(2,1)} %refs_1_.5, f32[8,128]{1,0:T(8,128)S(1)} %get-tuple-element.42.refs_2_, ...), custom_call_target="tpu_custom_call" | custom-call | flops 4294967296 | tf_op jit(solution)/shard_map/leaf_scores/pallas_call | solution.py:105
  36.4 0.1 collective-permute-start.1
  36.5 1.6 %collective-permute-start.2 = (bf16[256,768]{1,0:T(8,128)(2,1)}, bf16[256,768]{1,0:T(8,128)(2,1)S(1)}, u32[]{:S(2)}, u32[]{:S(2)}) collective-permute-start(bf16[256,768]{1,0:T(8,128)(2,1)} %get-tuple-element.50), channel_id=1, source_target_pairs={{0,4},{4,8},{8,12},{12,0},{1,5},{5,9},{9,13},{13,1},{2,6},{6,10},{... | collective-permute-start | bytes 1179656 | tf_op jit(solution)/shard_map/ppermute | solution.py:30
  38.1 2.7 %collective-permute-start.3 = (bf16[256,768]{1,0:T(8,128)(2,1)}, bf16[256,768]{1,0:T(8,128)(2,1)}, u32[]{:S(2)}, u32[]{:S(2)}) collective-permute-start(bf16[256,768]{1,0:T(8,128)(2,1)} %get-tuple-element.51), channel_id=1, source_target_pairs={{0,8},{4,12},{8,0},{12,4},{1,9},{5,13},{9,1},{13,5},{2,10},{6,14},... | collective-permute-start | bytes 1179656 | tf_op jit(solution)/shard_map/ppermute | solution.py:30
  40.8 1.5 %collective-permute-start.4 = (bf16[256,768]{1,0:T(8,128)(2,1)S(1)}, bf16[256,768]{1,0:T(8,128)(2,1)}, u32[]{:S(2)}, u32[]{:S(2)}) collective-permute-start(bf16[256,768]{1,0:T(8,128)(2,1)S(1)} %get-tuple-element.52), channel_id=1, source_target_pairs={{0,12},{4,0},{8,4},{12,8},{1,13},{5,1},{9,5},{13,9},{2,14},{6,2},{... | collective-permute-start | bytes 1179656 | tf_op jit(solution)/shard_map/ppermute | solution.py:30
  42.3 6.4 %leaf_back.1 = (bf16[512,256]{1,0:T(8,128)(2,1)}, bf16[512,256]{1,0:T(8,128)(2,1)S(1)}) custom-call(bf16[512,384]{1,0:T(8,128)(2,1)S(1)} %get-tuple-element.43.refs_0_, f32[512,256]{1,0:T(8,128)S(1)} %get-tuple-element.44.refs_1_, f32[512,128]{1,0:T(8,128)S(1)} %get-tuple-element.45.refs_2_, f32[512,128]{1,0:T(8,128)S(1)} %collective-permute-done.1.refs_3_, ...), custom_call_target="tpu_custom_call" | custom-call | tf_op jit(solution)/shard_map/leaf_back/pallas_call | solution.py:105
  48.6 0.7 copy-done.15
  49.3 8.2 %all-to-all-start.1 = ((bf16[64,8,256]{2,1,0:T(8,128)(2,1)}), bf16[64,8,256]{2,1,0:T(8,128)(2,1)S(1)}, u32[]{:S(2)}, u32[]{:S(2)}) async-start(bf16[64,8,256]{2,1,0:T(8,128)(2,1)} %bitcast.6), calls=%async_computation.1 | async-start | bytes 524288 | tf_op jit(solution)/shard_map/all_to_all | solution.py:612
  57.6 3.0 %copy.18 = bf16[1024,4,512]{2,0,1:T(8,128)(2,1)S(1)} copy(bf16[1024,4,512]{2,1,0:T(4,128)(2,1)} %param.12) | data formatting | bytes 8388608 | tf_op jit(solution)/shard_map/optimization_barrier | solution.py:614
  60.6 0.6 slice_add_fusion.refs_5_
  61.2 2.0 %copy-done = bf16[1024,4,512]{2,0,1:T(8,128)(2,1)} copy-done((bf16[1024,4,512]{2,0,1:T(8,128)(2,1)}, bf16[1024,4,512]{2,0,1:T(8,128)(2,1)S(1)}, u32[]{:S(2)}) %copy-start) | copy-done | bytes 4194328
  63.2 0.8 copy-done.3
  64.1 0.7 copy-done.22
  64.8 3.2 %table_part.1 = (bf16[64,16,128]{2,1,0:T(8,128)(2,1)}, f32[8,128]{1,0:T(8,128)}) custom-call(bf16[256,768]{1,0:T(8,128)(2,1)} %copy-done.11, bf16[256,768]{1,0:T(8,128)(2,1)} %copy-done.22, bf16[256,768]{1,0:T(8,128)(2,1)} %collective-permute-done.3.refs_2_, bf16[256,768]{1,0:T(8,128)(2,1)} %collective-permute-done.4.refs_3_, ...), custom_call_target="tpu_custom_call" | custom-call | tf_op jit(solution)/shard_map/table_part/pallas_call | solution.py:105
  68.0 1.0 copy-done.14
  69.1 0.7 copy-done.20
  69.7 0.3 rows.1.refs_0_
  70.2 1.5 %collective-permute-done.8.refs_1_ = f32[256,256]{1,0:T(8,128)S(1)} collective-permute-done((f32[256,256]{1,0:T(8,128)S(1)}, f32[256,256]{1,0:T(8,128)S(1)}, u32[]{:S(2)}, u32[]{:S(2)}) %collective-permute-start.8) | collective-permute-done | bytes 262176 | tf_op jit(solution)/shard_map/ppermute | solution.py:25
  71.7 1.5 %collective-permute-start.9 = (bf16[256,256]{1,0:T(8,128)(2,1)S(1)}, bf16[256,256]{1,0:T(8,128)(2,1)S(1)}, u32[]{:S(2)}, u32[]{:S(2)}) collective-permute-start(bf16[256,256]{1,0:T(8,128)(2,1)S(1)} %row_grad.1.refs_5_.refs_0_.refs_2_), channel_id=1, source_target_pairs={{0,1},{1,0},{2,3},{3,2},{16,17},{17,16},{18,19},{19,18},{32,33},{3... | collective-permute-start | bytes 393224 | tf_op jit(solution)/shard_map/ppermute | solution.py:40
  73.2 1.5 %collective-permute-start.10 = (bf16[256,256]{1,0:T(8,128)(2,1)S(1)}, bf16[256,256]{1,0:T(8,128)(2,1)S(1)}, u32[]{:S(2)}, u32[]{:S(2)}) collective-permute-start(bf16[256,256]{1,0:T(8,128)(2,1)S(1)} %row_grad.1.refs_5_.refs_0_.refs_2_), channel_id=1, source_target_pairs={{0,16},{1,17},{2,18},{3,19},{16,0},{17,1},{18,2},{19,3},{32,48},{3... | collective-permute-start | bytes 393224 | tf_op jit(solution)/shard_map/ppermute | solution.py:40
  74.7 0.6 collective-permute-start.11
  75.3 2.2 %copy-done.1 = bf16[1024,4,512]{2,0,1:T(8,128)(2,1)S(1)} copy-done((bf16[1024,4,512]{2,0,1:T(8,128)(2,1)S(1)}, bf16[1024,4,512]{2,0,1:T(8,128)(2,1)}, u32[]{:S(2)}) %copy-start.1) | copy-done | bytes 4194328
  77.5 1.1 copy-done.4
  78.5 2.7 %group_forward.1 = (bf16[1024,512]{1,0:T(8,128)(2,1)S(1)}, f32[1024,512]{1,0:T(8,128)S(1)}, bf16[1024,128]{1,0:T(8,128)(2,1)S(1)}, f32[1024,128]{1,0:T(8,128)S(1...) custom-call(bf16[272,1024]{1,0:T(8,128)(2,1)S(1)} %norms.1.refs_0_.refs_4_.refs_1_, ...), custom_call_target="tpu_custom_call" | custom-call | tf_op jit(solution)/shard_map/group_forward/pallas_call | solution.py:105
  81.3 1.0 copy-done.5
  82.4 4.7 %weight_parts.1.refs_6_.refs_2_ = bf16[64,16,768]{2,1,0:T(8,128)(2,1)} custom-call(bf16[256,256]{1,0:T(8,128)(2,1)S(1)} %row_grad.1.refs_5_.refs_0_.refs_2_, bf16[256,256]{1,0:T(8,128)(2,1)S(1)} %collective-permute-done.9.refs_1_, bf16[256,256]{1,0:T(8,128)(2,1)S(1)} %collective-permute-done.10.refs_2_, ...), custom_call_target="tpu_custom_call" | custom-call | tf_op jit(solution)/shard_map/weight_parts/pallas_call | solution.py:105
  87.0 10.4 %all-to-all-start.2 = ((bf16[64,16,768]{2,1,0:T(8,128)(2,1)}), bf16[64,16,768]{2,1,0:T(8,128)(2,1)S(1)}, u32[]{:S(2)}, u32[]{:S(2)}) async-start(bf16[64,16,768]{2,1,0:T(8,128)(2,1)} %weight_parts.1.refs_6_.refs_2_), calls=%async_computation.2 | async-start | bytes 3145728 | tf_op jit(solution)/shard_map/all_to_all | solution.py:670
  97.5 1.0 copy-done.6
  98.5 7.8 %trunk.1 = (bf16[256,1024]{1,0:T(8,128)(2,1)S(1)}, f32[256,1024]{1,0:T(8,128)S(1)}) custom-call(s32[2,1,4]{2,1,0:T(1,128)S(1)} %copy-done.21, bf16[272,1024]{1,0:T(8,128)(2,1)S(1)} %norms.1.refs_0_.refs_4_.refs_1_, bf16[256,256]{1,0:T(8,128)(2,1)S(1)} %row_grad.1.refs_5_.refs_0_.refs_2_, bf16[1024,256]{1,0:T(8,128)(2,1)S(1)} %copy-done.6, ...), custom_call_target="tpu_custom_call" | custom-call | tf_op jit(solution)/shard_map/trunk/pallas_call | solution.py:105
  106.4 7.3 %leaf_book.1 = bf16[64,256,256]{2,1,0:T(8,128)(2,1)} custom-call(bf16[512,384]{1,0:T(8,128)(2,1)} %bitcast.23, bf16[512,256]{1,0:T(8,128)(2,1)} %copy-done.15, bf16[64,16,768]{2,1,0:T(8,128)(2,1)} %weight_parts.1.refs_6_.refs_2_), custom_call_target="tpu_custom_call" | custom-call | tf_op jit(solution)/shard_map/leaf_book/pallas_call | solution.py:105
  113.7 1.5 %input_grads.1 = bf16[2,128,1024]{2,1,0:T(8,128)(2,1)} custom-call(bf16[2,128,1024]{2,1,0:T(8,128)(2,1)S(1)} %copy-done.8, bf16[256,1024]{1,0:T(8,128)(2,1)S(1)} %get-tuple-element.63.refs_1_, f32[256,1024]{1,0:T(8,128)S(1)} %get-tuple-element.64.refs_2_, f32[256,1024]{1,0:T(8,128)S(1)} %collective-permute-done.12.refs_3_), custom_call_target="tpu_custom_call" | custom-call | tf_op jit(solution)/shard_map/input_grads/pallas_call | solution.py:105
  115.3 5.9 %all-to-all-done.2.refs_0_ = bf16[64,16,768]{2,1,0:T(8,128)(2,1)S(1)} async-done(((bf16[64,16,768]{2,1,0:T(8,128)(2,1)}), bf16[64,16,768]{2,1,0:T(8,128)(2,1)S(1)}, u32[]{:S(2)}, u32[]{:S(2)}) %all-to-all-start.2) | async-done | bytes 1572896 | tf_op jit(solution)/shard_map/all_to_all | solution.py:670
  121.2 0.9 weight_sums.1
  (49 shorter events, 0.3 us)
Async XLA Ops:
  0.6 18.7 %copy-start.7 = (bf16[2,128,1024]{2,1,0:T(8,128)(2,1)S(1)}, bf16[2,128,1024]{2,1,0:T(8,128)(2,1)}, u32[]{:S(2)}) copy-start(bf16[2,128,1024]{2,1,0:T(8,128)(2,1)} %refs_0_.7) | copy-start | bytes 1572868
  0.6 18.7 %copy-start.21 = (s32[2,1,4]{2,1,0:T(1,128)S(1)}, s32[2,1,4]{2,1,0:T(1,128)}, u32[]{:S(2)}) copy-start(s32[2,1,4]{2,1,0:T(1,128)} %refs_0_.6) | copy-start | bytes 100
  3.6 20.8 %copy-start.16 = (f32[256,128]{1,0:T(8,128)S(1)}, f32[256,128]{1,0:T(8,128)}, u32[]{:S(2)}) copy-start(f32[256,128]{1,0:T(8,128)} %get-tuple-element.41.refs_3_) | copy-start | bytes 393220
  3.6 25.2 %all-to-all-start = ((bf16[64,8,384]{2,1,0:T(8,128)(2,1)}), bf16[64,8,384]{2,1,0:T(8,128)(2,1)S(1)}, u32[]{:S(2)}, u32[]{:S(2)}) async-start(bf16[64,8,384]{2,1,0:T(8,128)(2,1)} %bitcast.28), calls=%async_computation | async-start | bytes 786432 | tf_op jit(solution)/shard_map/all_to_all | solution.py:575
  16.6 0.9 copy-start.10
  17.5 0.7 copy-start.17
  19.2 5.2 %collective-permute-start = (f32[256,128]{1,0:T(8,128)S(1)}, f32[256,128]{1,0:T(8,128)S(1)}, u32[]{:S(2)}, u32[]{:S(2)}) collective-permute-start(f32[256,128]{1,0:T(8,128)S(1)} %get-tuple-element.40.refs_1_), channel_id=1, source_target_pairs={{0,64},{64,0},{1,65},{65,1},{2,66},{66,2},{3,67},{67,3},{4,68},{68... | collective-permute-start | bytes 393224 | tf_op jit(solution)/shard_map/ppermute | solution.py:25
  19.3 0.7 copy-start.18
  20.9 17.3 %collective-permute-start.7 = (bf16[272,1024]{1,0:T(8,128)(2,1)S(1)}, bf16[272,1024]{1,0:T(8,128)(2,1)S(1)}, u32[]{:S(2)}, u32[]{:S(2)}) collective-permute-start(bf16[272,1024]{1,0:T(8,128)(2,1)S(1)} %norms.1.refs_0_.refs_4_.refs_1_), channel_id=1, source_target_pairs={{0,17},{1,16},{2,19},{3,18},{16,1},{17,0},{18,3},{19,2},{32,49},{3... | collective-permute-start | bytes 1671176 | tf_op jit(solution)/shard_map/ppermute | solution.py:40
  23.4 37.2 %collective-permute-start.6 = (bf16[272,1024]{1,0:T(8,128)(2,1)S(1)}, bf16[272,1024]{1,0:T(8,128)(2,1)S(1)}, u32[]{:S(2)}, u32[]{:S(2)}) collective-permute-start(bf16[272,1024]{1,0:T(8,128)(2,1)S(1)} %norms.1.refs_0_.refs_4_.refs_1_), channel_id=1, source_target_pairs={{0,16},{1,17},{2,18},{3,19},{16,0},{17,1},{18,2},{19,3},{32,48},{3... | collective-permute-start | bytes 1671176 | tf_op jit(solution)/shard_map/ppermute | solution.py:40
  24.0 36.6 %collective-permute-start.5 = (bf16[272,1024]{1,0:T(8,128)(2,1)S(1)}, bf16[272,1024]{1,0:T(8,128)(2,1)S(1)}, u32[]{:S(2)}, u32[]{:S(2)}) collective-permute-start(bf16[272,1024]{1,0:T(8,128)(2,1)S(1)} %norms.1.refs_0_.refs_4_.refs_1_), channel_id=1, source_target_pairs={{0,1},{1,0},{2,3},{3,2},{16,17},{17,16},{18,19},{19,18},{32,33},{3... | collective-permute-start | bytes 1671176 | tf_op jit(solution)/shard_map/ppermute | solution.py:40
  27.4 0.7 copy-start.11
  28.1 0.7 copy-start.13
  28.8 7.5 %copy-start.9 = (bf16[64,8,384]{2,1,0:T(8,128)(2,1)}, bf16[64,8,384]{2,1,0:T(8,128)(2,1)S(1)}, u32[]{:S(2)}) copy-start(bf16[64,8,384]{2,1,0:T(8,128)(2,1)S(1)} %all-to-all-done) | copy-start | bytes 1179652
  36.4 4.4 %collective-permute-start.1 = (f32[512,128]{1,0:T(8,128)S(1)}, f32[512,128]{1,0:T(8,128)S(1)}, u32[]{:S(2)}, u32[]{:S(2)}) collective-permute-start(f32[512,128]{1,0:T(8,128)S(1)} %get-tuple-element.45.refs_2_), channel_id=1, source_target_pairs={{0,64},{64,0},{1,65},{65,1},{2,66},{66,2},{3,67},{67,3},{4,68},{68... | collective-permute-start | bytes 786440 | tf_op jit(solution)/shard_map/ppermute | solution.py:25
  36.5 27.6 %collective-permute-start.2 = (bf16[256,768]{1,0:T(8,128)(2,1)}, bf16[256,768]{1,0:T(8,128)(2,1)S(1)}, u32[]{:S(2)}, u32[]{:S(2)}) collective-permute-start(bf16[256,768]{1,0:T(8,128)(2,1)} %get-tuple-element.50), channel_id=1, source_target_pairs={{0,4},{4,8},{8,12},{12,0},{1,5},{5,9},{9,13},{13,1},{2,6},{6,10},{... | collective-permute-start | bytes 1179656 | tf_op jit(solution)/shard_map/ppermute | solution.py:30
  38.1 25.9 %collective-permute-start.3 = (bf16[256,768]{1,0:T(8,128)(2,1)}, bf16[256,768]{1,0:T(8,128)(2,1)}, u32[]{:S(2)}, u32[]{:S(2)}) collective-permute-start(bf16[256,768]{1,0:T(8,128)(2,1)} %get-tuple-element.51), channel_id=1, source_target_pairs={{0,8},{4,12},{8,0},{12,4},{1,9},{5,13},{9,1},{13,5},{2,10},{6,14},... | collective-permute-start | bytes 1179656 | tf_op jit(solution)/shard_map/ppermute | solution.py:30
  40.8 23.2 %collective-permute-start.4 = (bf16[256,768]{1,0:T(8,128)(2,1)S(1)}, bf16[256,768]{1,0:T(8,128)(2,1)}, u32[]{:S(2)}, u32[]{:S(2)}) collective-permute-start(bf16[256,768]{1,0:T(8,128)(2,1)S(1)} %get-tuple-element.52), channel_id=1, source_target_pairs={{0,12},{4,0},{8,4},{12,8},{1,13},{5,1},{9,5},{13,9},{2,14},{6,2},{... | collective-permute-start | bytes 1179656 | tf_op jit(solution)/shard_map/ppermute | solution.py:30
  48.6 0.7 copy-start.15
  49.3 18.7 %all-to-all-start.1 = ((bf16[64,8,256]{2,1,0:T(8,128)(2,1)}), bf16[64,8,256]{2,1,0:T(8,128)(2,1)S(1)}, u32[]{:S(2)}, u32[]{:S(2)}) async-start(bf16[64,8,256]{2,1,0:T(8,128)(2,1)} %bitcast.6), calls=%async_computation.1 | async-start | bytes 524288 | tf_op jit(solution)/shard_map/all_to_all | solution.py:612
  57.6 10.4 %copy-start.19 = (s32[2,128]{1,0:T(2,128)S(1)}, s32[2,128]{1,0:T(2,128)}, u32[]{:S(2)}) copy-start(s32[2,128]{1,0:T(2,128)} %get-tuple-element.37.refs_2_.refs_0_) | copy-start | bytes 3076
  61.2 2.0 %copy-start = (bf16[1024,4,512]{2,0,1:T(8,128)(2,1)}, bf16[1024,4,512]{2,0,1:T(8,128)(2,1)S(1)}, u32[]{:S(2)}) copy-start(bf16[1024,4,512]{2,0,1:T(8,128)(2,1)S(1)} %copy.18) | copy-start | bytes 12582916
  63.2 0.8 copy-start.3
  64.0 0.7 copy-start.22
  68.0 13.3 %copy-start.2 = (bf16[512,1024]{1,0:T(8,128)(2,1)S(1)}, bf16[512,1024]{1,0:T(8,128)(2,1)}, u32[]{:S(2)}) copy-start(bf16[512,1024]{1,0:T(8,128)(2,1)} %refs_4_.1) | copy-start | bytes 3145732
  68.0 13.3 %copy-start.12 = (bf16[64,16,128]{2,1,0:T(8,128)(2,1)S(1)}, bf16[64,16,128]{2,1,0:T(8,128)(2,1)}, u32[]{:S(2)}) copy-start(bf16[64,16,128]{2,1,0:T(8,128)(2,1)} %get-tuple-element.62.refs_17_) | copy-start | bytes 786436
  68.0 1.0 copy-start.14
  69.1 0.7 copy-start.20
  70.1 1.6 %collective-permute-start.8 = (f32[256,256]{1,0:T(8,128)S(1)}, f32[256,256]{1,0:T(8,128)S(1)}, u32[]{:S(2)}, u32[]{:S(2)}) collective-permute-start(f32[256,256]{1,0:T(8,128)S(1)} %rows.1.refs_0_), channel_id=1, source_target_pairs={{0,64},{64,0},{1,65},{65,1},{2,66},{66,2},{3,67},{67,3},{4,68},{68... | collective-permute-start | bytes 786440 | tf_op jit(solution)/shard_map/ppermute | solution.py:25
  71.7 9.5 %collective-permute-start.9 = (bf16[256,256]{1,0:T(8,128)(2,1)S(1)}, bf16[256,256]{1,0:T(8,128)(2,1)S(1)}, u32[]{:S(2)}, u32[]{:S(2)}) collective-permute-start(bf16[256,256]{1,0:T(8,128)(2,1)S(1)} %row_grad.1.refs_5_.refs_0_.refs_2_), channel_id=1, source_target_pairs={{0,1},{1,0},{2,3},{3,2},{16,17},{17,16},{18,19},{19,18},{32,33},{3... | collective-permute-start | bytes 393224 | tf_op jit(solution)/shard_map/ppermute | solution.py:40
  73.2 8.1 %collective-permute-start.10 = (bf16[256,256]{1,0:T(8,128)(2,1)S(1)}, bf16[256,256]{1,0:T(8,128)(2,1)S(1)}, u32[]{:S(2)}, u32[]{:S(2)}) collective-permute-start(bf16[256,256]{1,0:T(8,128)(2,1)S(1)} %row_grad.1.refs_5_.refs_0_.refs_2_), channel_id=1, source_target_pairs={{0,16},{1,17},{2,18},{3,19},{16,0},{17,1},{18,2},{19,3},{32,48},{3... | collective-permute-start | bytes 393224 | tf_op jit(solution)/shard_map/ppermute | solution.py:40
  74.7 6.6 %collective-permute-start.11 = (bf16[256,256]{1,0:T(8,128)(2,1)S(1)}, bf16[256,256]{1,0:T(8,128)(2,1)S(1)}, u32[]{:S(2)}, u32[]{:S(2)}) collective-permute-start(bf16[256,256]{1,0:T(8,128)(2,1)S(1)} %row_grad.1.refs_5_.refs_0_.refs_2_), channel_id=1, source_target_pairs={{0,17},{1,16},{2,19},{3,18},{16,1},{17,0},{18,3},{19,2},{32,49},{3... | collective-permute-start | bytes 393224 | tf_op jit(solution)/shard_map/ppermute | solution.py:40
  75.3 2.2 %copy-start.1 = (bf16[1024,4,512]{2,0,1:T(8,128)(2,1)S(1)}, bf16[1024,4,512]{2,0,1:T(8,128)(2,1)}, u32[]{:S(2)}) copy-start(bf16[1024,4,512]{2,0,1:T(8,128)(2,1)} %copy-done) | copy-start | bytes 12582916
  77.5 1.1 copy-start.4
  81.3 1.0 copy-start.5
  87.0 34.2 %all-to-all-start.2 = ((bf16[64,16,768]{2,1,0:T(8,128)(2,1)}), bf16[64,16,768]{2,1,0:T(8,128)(2,1)S(1)}, u32[]{:S(2)}, u32[]{:S(2)}) async-start(bf16[64,16,768]{2,1,0:T(8,128)(2,1)} %weight_parts.1.refs_6_.refs_2_), calls=%async_computation.2 | async-start | bytes 3145728 | tf_op jit(solution)/shard_map/all_to_all | solution.py:670
  97.4 1.0 copy-start.6
  106.3 7.4 %collective-permute-start.12 = (f32[256,1024]{1,0:T(8,128)S(1)}, f32[256,1024]{1,0:T(8,128)S(1)}, u32[]{:S(2)}, u32[]{:S(2)}) collective-permute-start(f32[256,1024]{1,0:T(8,128)S(1)} %get-tuple-element.64.refs_2_), channel_id=1, source_target_pairs={{0,64},{64,0},{1,65},{65,1},{2,66},{66,2},{3,67},{67,3},{4,68},{68... | collective-permute-start | bytes 3145736 | tf_op jit(solution)/shard_map/ppermute | solution.py:25
  106.4 7.4 %copy-start.8 = (bf16[2,128,1024]{2,1,0:T(8,128)(2,1)S(1)}, bf16[2,128,1024]{2,1,0:T(8,128)(2,1)}, u32[]{:S(2)}) copy-start(bf16[2,128,1024]{2,1,0:T(8,128)(2,1)} %refs_0_.7) | copy-start | bytes 1572868

commit v3 on v2

--- a/solution.py
+++ b/solution.py
@@ -25,19 +25,14 @@
     return lax.ppermute(part, "section", [(0, 1), (1, 0)])
 
 
-def shifted(part, axis, step):
-    count = lax.axis_size(axis)
-    return lax.ppermute(part, axis, [(i, (i + step) % count) for i in range(count)])
-
-
-def member():
-    return lax.rem(lax.axis_index("x"), 2) + 2 * lax.rem(lax.axis_index("y"), 2)
-
-
-def from_member(part, other):
+def member(axis):
+    return lax.rem(lax.axis_index("x"), 2) + 2 * lax.rem(lax.axis_index(axis), 2)
+
+
+def from_member(part, axis, other):
     count = lax.axis_size("x")
     flip = count * (other // 2) + other % 2
-    return lax.ppermute(part, ("y", "x"), [(i, i ^ flip) for i in range(lax.axis_size("y") * count)])
+    return lax.ppermute(part, (axis, "x"), [(i, i ^ flip) for i in range(lax.axis_size(axis) * count)])
 
 
 def dot(left, right, dims):
@@ -151,8 +146,12 @@
     sent_ref[:, width:] = codes_out.astype(bf16)
 
 
-def top_logits_kernel(saved_ref, table_ref, logit_ref, stat_ref):
-    logits = dot(saved_ref[...], table_ref[...], NT)
+def top_logits_kernel(group, owners, saved_ref, table_ref, logit_ref, stat_ref, turned_ref):
+    half, width = table_ref.shape
+    rows = table_ref[...].astype(f32).reshape(owners, group, half // owners // group, width)
+    turned = jnp.concatenate([rows[:, q].reshape(half // group, width) for q in range(group)], axis=0).astype(bf16)
+    turned_ref[...] = turned
+    logits = dot(saved_ref[...], turned, NT)
     logit_ref[...] = logits
     peak = jnp.max(logits, axis=1, keepdims=True)
     mass = jnp.sum(jnp.exp(logits - peak), axis=1, keepdims=True)
@@ -172,7 +171,7 @@
     quarter = half // group
     piece = own // group
     base = lax.axis_index("section") * half
-    me = lax.axis_index("z")
+    me = member("z")
     peak, mass = joined(mine_ref, other_ref)
     target = mark_ref[:, 0:1].astype(jnp.int32) - base
     total = 0.0
@@ -185,7 +184,7 @@
         total += dot(grad, table_ref[cols, :], NN)
         for s in range(group):
 
-            @pl.when(lax.rem(me + s, group) == q)
+            @pl.when(lax.bitwise_xor(me, s) == q)
             def _(s=s, grad=grad):
                 grad_refs[s][:, :quarter] = grad
                 grad_refs[s][:, quarter:] = saved_ref[...]
@@ -399,13 +398,23 @@
 
 
 def my_head():
-    return pl.ds(pl.multiple_of(member() * HEAD_DIM, HEAD_DIM), HEAD_DIM)
+    return pl.ds(pl.multiple_of(member("y") * HEAD_DIM, HEAD_DIM), HEAD_DIM)
+
+
+def head_weight_kernel(weight_in, out_ref, part_ref, flat_ref, sem):
+    copy = pltpu.make_async_copy(weight_in.at[:, :, my_head()], part_ref, sem)
+    copy.start()
+    copy.wait()
+    flat_ref[...] = part_ref[...].astype(f32).reshape(flat_ref.shape)
+    depth, parts = weight_in.shape[:2]
+    for t in range(parts):
+        out_ref[:, t * HEAD_DIM : (t + 1) * HEAD_DIM] = flat_ref[pl.ds(t, depth, stride=parts), :].astype(bf16)
 
 
 def group_forward_kernel(*refs):
     *norm_ins, weight_in, act_ref, slope_ref, att_ref, back_ref, out_ref, inverse_ref, prod_ref = refs[:-3]
     weight_ref, norm_ref, sem = refs[-3:]
-    pairs = [(weight_in.at[:, :, my_head()], weight_ref)] + [(one, norm_ref.at[s]) for s, one in enumerate(norm_ins)]
+    pairs = [(weight_in, weight_ref)] + [(one, norm_ref.at[s]) for s, one in enumerate(norm_ins)]
     copies = [pltpu.make_async_copy(a, b, sem.at[i]) for i, (a, b) in enumerate(pairs)]
     for copy in copies:
         copy.start()
@@ -413,7 +422,7 @@
         copy.wait()
     rows = att_ref.shape[1]
     total = out_ref.shape[0] // len(norm_ins)
-    weight = jnp.concatenate([weight_ref[t] for t in range(4)], axis=1)
+    weight = weight_ref[...]
     acts, masks, spans = [], [], []
     for s in range(len(norm_ins)):
         for m in range(total // rows):
@@ -535,11 +544,12 @@
             expand_ref[:, t, head] = total[:, t * HEAD_DIM : (t + 1) * HEAD_DIM]
         mixing_ref[:, head] = total[:, cols:]
     lanes = pl.ds(cols + HEAD_DIM, HEAD_DIM)
-    for z in side:
-        total = sum(in_ref[(y * group + z) * group + x, :, lanes].astype(f32) for y in side for x in side)
+    for q in side:
+        sources = [(y * group + z) * group + x for y in side for z in side for x in side if x % 2 + 2 * (z % 2) == q]
+        total = sum(in_ref[i, :, lanes].astype(f32) for i in sources)
         half = total.shape[0] // 2
-        table_ref[z * half : (z + 1) * half, :HEAD_DIM] = total[:half]
-        table_ref[z * half : (z + 1) * half, HEAD_DIM:] = total[half:]
+        table_ref[q * half : (q + 1) * half, :HEAD_DIM] = total[:half]
+        table_ref[q * half : (q + 1) * half, HEAD_DIM:] = total[half:]
 
 
 def body(
@@ -583,14 +593,13 @@
         limit=28,
         after=(slot_ids,),
     )
-    normed_all = [normed] + [from_member(normed, s) for s in range(1, group)]
-    table = top_table.reshape(owners, group, own // group, width).swapaxes(0, 1).reshape(half_clusters, width)
-    logits, stats = call(
-        top_logits_kernel,
+    normed_all = [normed] + [from_member(normed, "y", s) for s in range(1, group)]
+    logits, stats, table = call(
+        functools.partial(top_logits_kernel, group, owners),
         "top_logits",
-        [((total, half_clusters), f32), ((total, 128), f32)],
-        (saved, table),
-        "HH VV",
+        [((total, half_clusters), f32), ((total, 128), f32), (top_table.shape, bf16)],
+        (saved, top_table),
+        "HH VVV",
         limit=40,
         after=(slot_ids,),
     )
@@ -603,7 +612,7 @@
         limit=40,
         token=True,
     )
-    top_all = [top_grads[0]] + [shifted(top_grads[s], "z", s) for s in range(1, group)]
+    top_all = [top_grads[0]] + [from_member(top_grads[s], "z", s) for s in range(1, group)]
 
     leaf, leaf_stats, got_held, book_held = leaf_scores(got, codebook, (top_token, normed[:8, :128]))
     back, leaf_grad = leaf_back(
@@ -611,16 +620,18 @@
     )
     returned = lax.all_to_all(back.reshape(owners, slots // owners, width), DEV, 0, 0, tiled=True)
 
-    late_weight, _ = lax.optimization_barrier((expand_weight, back))
-    weight = lax.optimization_barrier(late_weight.swapaxes(0, 1))
-    window_token = sum((a[:8, :128] for a in normed_all[1:]), weight[0, :8, :128])
-    table_part, table_token = call(
-        functools.partial(table_kernel, owners),
-        "table_part",
-        [((owners, 16, 128), bf16)],
-        top_all,
-        "H" * group + " H",
-        after=(back, window_token),
+    head_weight, head_token = call(
+        head_weight_kernel,
+        "head_weight",
+        [((model_width, 4 * HEAD_DIM), bf16)],
+        (expand_weight,),
+        "R H",
+        scratch=[
+            pltpu.VMEM((model_width, 4, HEAD_DIM), bf16),
+            pltpu.VMEM((model_width * 4, HEAD_DIM), f32),
+            pltpu.SemaphoreType.DMA,
+        ],
+        after=(back, sum(a[:8, :128] for a in normed_all[1:])),
         token=True,
     )
 
@@ -630,10 +641,10 @@
         [((total, width), f32)],
         (slot_ids, returned.reshape(slots, width), row_top),
         "VHH V", limit=28,
-        after=(table_token,),
+        after=(head_token,),
     )
     (row_grad,) = call(add_kernel, "row_grad", [((total, width), bf16)], (row_part, swap(row_part)), "VV V", limit=28)
-    row_all = [row_grad] + [from_member(row_grad, s) for s in range(1, group)]
+    row_all = [row_grad] + [from_member(row_grad, "y", s) for s in range(1, group)]
 
     group_rows = group * total
     group_forward = call(
@@ -648,15 +659,25 @@
             ((group_rows, HEAD_DIM), f32),
             ((group_rows, HEAD_DIM), bf16),
         ],
-        (*normed_all, weight),
+        (*normed_all, head_weight),
         "R" * (group + 1) + " " + "V" * 7,
         limit=GROUP_LIMIT,
         after=(row_grad,),
         scratch=[
-            pltpu.VMEM((4, model_width, HEAD_DIM), bf16),
+            pltpu.VMEM(head_weight.shape, bf16),
             pltpu.VMEM((group, total + 16, model_width), bf16),
             pltpu.SemaphoreType.DMA((group + 1,)),
         ],
+    )
+
+    (table_part,) = call(
+        functools.partial(table_kernel, owners),
+        "table_part",
+        [((owners, 16, 128), bf16)],
+        top_all,
+        "V" * group + " V",
+        limit=16,
+        after=(row_grad,),
     )
 
     (packed,) = call(
@@ -669,6 +690,8 @@
     )
     arrived = lax.all_to_all(packed, DEV, 0, 0, tiled=True)
 
+    late_weight, _ = lax.optimization_barrier((expand_weight, packed))
+    weight = late_weight.swapaxes(0, 1)
     out_grad, grad_part = call(
         trunk_kernel,
         "trunk",

time: 123 us -> 127 us (1.033)
  Pallas kernels: 50.2 us -> 52.3 us
  waiting for transfers between devices: 7.52 us -> 9.3 us
    all_to_all x1, waiting for transfers between devices: 5.94 us -> 1.48 us  [body(): arrived = lax.all_to_all(packed, DEV, 0, 0, tiled=True)]
    all_to_all x1, waiting for transfers between devices: 0.02 us -> 3.59 us  [body(): lax.all_to_all(back.reshape(owners, slots // owners, width), DEV, 0, 0, t...]
    all_to_all x1, starting transfers between devices: 8.24 us -> 10.5 us  [body(): lax.all_to_all(back.reshape(owners, slots // owners, width), DEV, 0, 0, t...]
    ppermute x9, starting transfers between devices: 12.9 us -> 10.7 us  [from_member(): lax.ppermute(part, (axis, 'x'), [(i, i ^ flip) for i in range(lax.axis_si...]
    pallas_call x15 -> x16, Pallas kernels: 50.2 us -> 52.3 us  [call(): pl.pallas_call(run, in_specs=[pl.BlockSpec(memory_space=spaces[k]) for k...]
    optimization_barrier x1, local copies, waits for them, and re-layouts: 3.03 us -> 5.09 us  [body(): late_weight, _ = lax.optimization_barrier((expand_weight, packed))]
    ppermute x4, waiting for transfers between devices: 1.53 us -> 3.05 us  [swap(): return lax.ppermute(part, 'section', [(0, 1), (1, 0)])]
    reshape x1 -> x0, local copies, waits for them, and re-layouts: 1.3 us -> none  [body(): top_table.reshape(owners, group, own // group, width).swapaxes(0, 1)]
  transfers between devices with their start and end apart: 16 -> 16, of which waited for: 2 -> 5; matrix products, arithmetic and copies ran while one was open for 4% -> 5% of each run, Pallas kernels for 34% -> 35%
where the time goes in v3:
time: 127 us; the launch traced here: 126 us
  Pallas kernels  52.3 us (41%)
  starting transfers between devices  43 us (34%)
  local copies, waits for them, and re-layouts  19.4 us (15%)
  waiting for transfers between devices  9.3 us (7%)
    pallas_call x16, Pallas kernels, call(): pl.pallas_call(run, in_specs=[pl.BlockSpec(memory_space=spaces[k]) for k...  52.3 us
    unnamed x44, local copies, waits for them, and re-layouts  14.3 us
    all_to_all x1, starting transfers between devices, body(): lax.all_to_all(sent.reshape(owners, slots // owners, -1), DEV, 0, 0, tile...  11.5 us
    ppermute x9, starting transfers between devices, from_member(): lax.ppermute(part, (axis, 'x'), [(i, i ^ flip) for i in range(lax.axis_si...  10.7 us
    all_to_all x1, starting transfers between devices, body(): lax.all_to_all(back.reshape(owners, slots // owners, width), DEV, 0, 0, t...  10.5 us
    all_to_all x1, starting transfers between devices, body(): arrived = lax.all_to_all(packed, DEV, 0, 0, tiled=True)  9.93 us
    optimization_barrier x1, local copies, waits for them, and re-layouts, body(): late_weight, _ = lax.optimization_barrier((expand_weight, packed))  5.09 us
    all_to_all x1, waiting for transfers between devices, body(): lax.all_to_all(back.reshape(owners, slots // owners, width), DEV, 0, 0, t...  3.59 us
  transfers between devices with their start and end apart: 16, of which 5 were waited for; matrix products, arithmetic and copies ran while one was open for 5% of the time, Pallas kernels for 35%

profile of v3, /device:TPU:0, one launch (start us, length us, event | category | flops | bytes accessed | tf_op | source)
XLA Modules:
  0.0 125.6 jit_solution(9148035353332237375)
XLA Ops:
  0.6 2.9 %dispatch.1 = (bf16[512,384]{1,0:T(8,128)(2,1)}, s32[2,128]{1,0:T(2,128)}, f32[256,128]{1,0:T(8,128)}) custom-call(s32[2,128]{1,0:T(2,128)} %refs_0_.5, s32[2,128]{1,0:T(2,128)} %refs_1_.4, bf16[2,128,256]{2,1,0:T(8,128)(2,1)} %refs_2_.1), custom_call_target="tpu_custom_call" | custom-call | tf_op jit(solution)/shard_map/dispatch/pallas_call | solution.py:100
  3.5 11.5 %all-to-all-start = ((bf16[64,8,384]{2,1,0:T(8,128)(2,1)}), bf16[64,8,384]{2,1,0:T(8,128)(2,1)S(1)}, u32[]{:S(2)}, u32[]{:S(2)}) async-start(bf16[64,8,384]{2,1,0:T(8,128)(2,1)} %bitcast.15), calls=%async_computation | async-start | bytes 786432 | tf_op jit(solution)/shard_map/all_to_all | solution.py:585
  15.0 0.9 copy-done.8
  15.9 1.2 copy-done.9
  17.2 0.7 copy-done.17
  17.8 1.1 top_logits.1
  19.0 1.0 copy-done.5
  20.1 0.7 copy-done.20
  20.7 0.9 norms.1.refs_0_.refs_4_.refs_1_
  21.6 2.6 %collective-permute-start.4 = (bf16[272,1024]{1,0:T(8,128)(2,1)S(1)}, bf16[272,1024]{1,0:T(8,128)(2,1)S(1)}, u32[]{:S(2)}, u32[]{:S(2)}) collective-permute-start(bf16[272,1024]{1,0:T(8,128)(2,1)S(1)} %norms.1.refs_0_.refs_4_.refs_1_), channel_id=1, source_target_pairs={{0,17},{1,16},{2,19},{3,18},{16,1},{17,0},{18,3},{19,2},{32,49},{3... | collective-permute-start | bytes 1671176 | tf_op jit(solution)/shard_map/ppermute | solution.py:35
  24.2 0.6 collective-permute-start.3
  24.7 0.5 collective-permute-start.2
  25.2 0.9 copy-done.16
  26.1 3.1 %top_grads.1 = (f32[256,256]{1,0:T(8,128)S(1)}, bf16[256,768]{1,0:T(8,128)(2,1)S(1)}, bf16[256,768]{1,0:T(8,128)(2,1)}, bf16[256,768]{1,0:T(8,128)(2,1)}, bf16[2...) custom-call(f32[256,2048]{1,0:T(8,128)S(1)} %get-tuple-element.40.refs_0_, f32[256,128]{1,0:T(8,128)S(1)} %get-tuple-element.41.refs_1_, ...), custom_call_target="tpu_custom_call" | custom-call | tf_op jit(solution)/shard_map/top_grads/pallas_call | solution.py:100
  29.2 0.7 copy-done.11
  30.0 0.7 copy-done.13
  30.7 7.5 %leaf_scores.1 = (f32[512,256]{1,0:T(8,128)S(1)}, f32[512,128]{1,0:T(8,128)S(1)}, bf16[512,384]{1,0:T(8,128)(2,1)S(1)}, bf16[64,256,256]{2,1,0:T(8,128)(2,1)S(1)}) custom-call(bf16[512,384]{1,0:T(8,128)(2,1)S(1)} %bitcast.9, bf16[64,256,256]{2,1,0:T(8,128)(2,1)} %refs_1_.7, f32[8,128]{1,0:T(8,128)S(1)} %get-tuple-element.44.refs_2_, ...), custom_call_target="tpu_custom_call" | custom-call | flops 4294967296 | tf_op jit(solution)/shard_map/leaf_scores/pallas_call | solution.py:100
  38.3 1.5 %collective-permute-done.1.refs_3_ = f32[512,128]{1,0:T(8,128)S(1)} collective-permute-done((f32[512,128]{1,0:T(8,128)S(1)}, f32[512,128]{1,0:T(8,128)S(1)}, u32[]{:S(2)}, u32[]{:S(2)}) %collective-permute-start.1) | collective-permute-done | bytes 262176 | tf_op jit(solution)/shard_map/ppermute | solution.py:25
  39.8 6.4 %leaf_back.1 = (bf16[512,256]{1,0:T(8,128)(2,1)}, bf16[512,256]{1,0:T(8,128)(2,1)S(1)}) custom-call(bf16[512,384]{1,0:T(8,128)(2,1)S(1)} %get-tuple-element.45.refs_0_, f32[512,256]{1,0:T(8,128)S(1)} %get-tuple-element.46.refs_1_, f32[512,128]{1,0:T(8,128)S(1)} %get-tuple-element.47.refs_2_, f32[512,128]{1,0:T(8,128)S(1)} %collective-permute-done.1.refs_3_, ...), custom_call_target="tpu_custom_call" | custom-call | tf_op jit(solution)/shard_map/leaf_back/pallas_call | solution.py:100
  46.2 0.7 copy-done.15
  46.9 10.5 %all-to-all-start.1 = ((bf16[64,8,256]{2,1,0:T(8,128)(2,1)}), bf16[64,8,256]{2,1,0:T(8,128)(2,1)S(1)}, u32[]{:S(2)}, u32[]{:S(2)}) async-start(bf16[64,8,256]{2,1,0:T(8,128)(2,1)} %bitcast.3), calls=%async_computation.1 | async-start | bytes 524288 | tf_op jit(solution)/shard_map/all_to_all | solution.py:621
  57.4 1.6 %collective-permute-start.9 = (bf16[256,768]{1,0:T(8,128)(2,1)}, bf16[256,768]{1,0:T(8,128)(2,1)}, u32[]{:S(2)}, u32[]{:S(2)}) collective-permute-start(bf16[256,768]{1,0:T(8,128)(2,1)} %get-tuple-element.61), channel_id=1, source_target_pairs={{0,1},{1,0},{2,3},{3,2},{4,5},{5,4},{6,7},{7,6},{8,9},{9,8},{10,11... | collective-permute-start | bytes 1179656 | tf_op jit(solution)/shard_map/ppermute | solution.py:35
  59.0 1.5 %collective-permute-start.10 = (bf16[256,768]{1,0:T(8,128)(2,1)}, bf16[256,768]{1,0:T(8,128)(2,1)}, u32[]{:S(2)}, u32[]{:S(2)}) collective-permute-start(bf16[256,768]{1,0:T(8,128)(2,1)} %get-tuple-element.62), channel_id=1, source_target_pairs={{0,4},{1,5},{2,6},{3,7},{4,0},{5,1},{6,2},{7,3},{8,12},{9,13},{10,... | collective-permute-start | bytes 1179656 | tf_op jit(solution)/shard_map/ppermute | solution.py:35
  60.5 0.5 collective-permute-start.11
  61.0 0.6 slice_add_fusion.refs_2_
  61.6 0.8 copy-done.1
  62.4 3.5 %head_weight.1 = (bf16[1024,512]{1,0:T(8,128)(2,1)}, f32[8,128]{1,0:T(8,128)}) custom-call(bf16[1024,4,512]{2,1,0:T(4,128)(2,1)} %refs_0_.7, bf16[512,256]{1,0:T(8,128)(2,1)} %get-tuple-element.49.refs_1_, bf16[8,128]{1,0:T(8,128)(2,1)} %slice_add_fusion.refs_2_), custom_call_target="tpu_custom_call" | custom-call | tf_op jit(solution)/shard_map/head_weight/pallas_call | solution.py:100
  65.9 3.6 %all-to-all-done.1 = bf16[64,8,256]{2,1,0:T(8,128)(2,1)S(1)} async-done(((bf16[64,8,256]{2,1,0:T(8,128)(2,1)}), bf16[64,8,256]{2,1,0:T(8,128)(2,1)S(1)}, u32[]{:S(2)}, u32[]{:S(2)}) %all-to-all-start.1) | async-done | bytes 262176 | tf_op jit(solution)/shard_map/all_to_all | solution.py:621
  69.5 0.9 copy-done.14
  70.4 0.7 copy-done.19
  71.5 1.5 %collective-permute-done.5.refs_1_ = f32[256,256]{1,0:T(8,128)S(1)} collective-permute-done((f32[256,256]{1,0:T(8,128)S(1)}, f32[256,256]{1,0:T(8,128)S(1)}, u32[]{:S(2)}, u32[]{:S(2)}) %collective-permute-start.5) | collective-permute-done | bytes 262176 | tf_op jit(solution)/shard_map/ppermute | solution.py:25
  73.1 0.6 collective-permute-start.6
  74.1 2.6 %collective-permute-start.8 = (bf16[256,256]{1,0:T(8,128)(2,1)S(1)}, bf16[256,256]{1,0:T(8,128)(2,1)S(1)}, u32[]{:S(2)}, u32[]{:S(2)}) collective-permute-start(bf16[256,256]{1,0:T(8,128)(2,1)S(1)} %row_grad.1.refs_5_.refs_4_.refs_0_.refs_2_), channel_id=1, source_target_pairs={{0,17},{1,16},{2,19},{3,18},{16,1},{17,0},{18,3},{19,2},{32,49},{3... | collective-permute-start | bytes 393224 | tf_op jit(solution)/shard_map/ppermute | solution.py:35
  76.7 1.1 copy-done.2
  77.7 1.2 copy-done.10
  78.9 2.6 %group_forward.1 = (bf16[1024,512]{1,0:T(8,128)(2,1)S(1)}, f32[1024,512]{1,0:T(8,128)S(1)}, bf16[1024,128]{1,0:T(8,128)(2,1)S(1)}, f32[1024,128]{1,0:T(8,128)S(1...) custom-call(bf16[272,1024]{1,0:T(8,128)(2,1)S(1)} %norms.1.refs_0_.refs_4_.refs_1_, ...), custom_call_target="tpu_custom_call" | custom-call | tf_op jit(solution)/shard_map/group_forward/pallas_call | solution.py:100
  81.6 1.0 copy-done.12
  82.6 1.7 %table_part.1.refs_17_ = bf16[64,16,128]{2,1,0:T(8,128)(2,1)S(1)} custom-call(bf16[256,768]{1,0:T(8,128)(2,1)S(1)} %copy-done.12, bf16[256,768]{1,0:T(8,128)(2,1)} %collective-permute-done.9.refs_1_, bf16[256,768]{1,0:T(8,128)(2,1)} %collective-permute-done.10.refs_2_, bf16[256,768]{1,0:T(8,128)(2,1)} %collective-permute-done.11.refs_3_, ...), custom_call_target="tpu_custom_call" | custom-call | tf_op jit(solution)/shard_map/table_part/pallas_call | solution.py:100
  84.3 1.2 collective-permute-done.8.refs_3_
  85.5 1.0 copy-done.3
  86.5 4.7 %weight_parts.1.refs_6_.refs_2_ = bf16[64,16,768]{2,1,0:T(8,128)(2,1)} custom-call(bf16[256,256]{1,0:T(8,128)(2,1)S(1)} %row_grad.1.refs_5_.refs_4_.refs_0_.refs_2_, bf16[256,256]{1,0:T(8,128)(2,1)S(1)} %collective-permute-done.6.refs_1_, bf16[256,256]{1,0:T(8,128)(2,1)S(1)} %collective-permute-done.7.refs_2_, ...), custom_call_target="tpu_custom_call" | custom-call | tf_op jit(solution)/shard_map/weight_parts/pallas_call | solution.py:100
  91.2 9.9 %all-to-all-start.2 = ((bf16[64,16,768]{2,1,0:T(8,128)(2,1)}), bf16[64,16,768]{2,1,0:T(8,128)(2,1)S(1)}, u32[]{:S(2)}, u32[]{:S(2)}) async-start(bf16[64,16,768]{2,1,0:T(8,128)(2,1)} %weight_parts.1.refs_6_.refs_2_), calls=%async_computation.2 | async-start | bytes 3145728 | tf_op jit(solution)/shard_map/all_to_all | solution.py:691
  101.2 5.1 %copy.17 = bf16[1024,4,512]{2,0,1:T(8,128)(2,1)} copy(bf16[1024,4,512]{2,1,0:T(4,128)(2,1)} %refs_0_.7) | data formatting | bytes 8388608 | tf_op jit(solution)/shard_map/optimization_barrier | solution.py:693
  106.3 7.8 %trunk.1 = (bf16[256,1024]{1,0:T(8,128)(2,1)S(1)}, f32[256,1024]{1,0:T(8,128)S(1)}) custom-call(s32[2,1,4]{2,1,0:T(1,128)S(1)} %copy-done.21, bf16[272,1024]{1,0:T(8,128)(2,1)S(1)} %norms.1.refs_0_.refs_4_.refs_1_, bf16[256,256]{1,0:T(8,128)(2,1)S(1)} %row_grad.1.refs_5_.refs_4_.refs_0_.refs_2_, bf16[1024,256]{1,0:T(8,128)(2,1)S(1)} %copy-done.4, ...), custom_call_target="tpu_custom_call" | custom-call | tf_op jit(solution)/shard_map/trunk/pallas_call | solution.py:100
  114.2 7.3 %leaf_book.1 = bf16[64,256,256]{2,1,0:T(8,128)(2,1)} custom-call(bf16[512,384]{1,0:T(8,128)(2,1)} %bitcast.10, bf16[512,256]{1,0:T(8,128)(2,1)} %copy-done.15, bf16[64,16,768]{2,1,0:T(8,128)(2,1)} %weight_parts.1.refs_6_.refs_2_), custom_call_target="tpu_custom_call" | custom-call | tf_op jit(solution)/shard_map/leaf_book/pallas_call | solution.py:100
  121.6 1.5 %input_grads.1 = bf16[2,128,1024]{2,1,0:T(8,128)(2,1)} custom-call(bf16[2,128,1024]{2,1,0:T(8,128)(2,1)S(1)} %copy-done.6, bf16[256,1024]{1,0:T(8,128)(2,1)S(1)} %get-tuple-element.65.refs_1_, f32[256,1024]{1,0:T(8,128)S(1)} %get-tuple-element.66.refs_2_, f32[256,1024]{1,0:T(8,128)S(1)} %collective-permute-done.12.refs_3_), custom_call_target="tpu_custom_call" | custom-call | tf_op jit(solution)/shard_map/input_grads/pallas_call | solution.py:100
  123.1 1.5 %all-to-all-done.2.refs_0_ = bf16[64,16,768]{2,1,0:T(8,128)(2,1)S(1)} async-done(((bf16[64,16,768]{2,1,0:T(8,128)(2,1)}), bf16[64,16,768]{2,1,0:T(8,128)(2,1)S(1)}, u32[]{:S(2)}, u32[]{:S(2)}) %all-to-all-start.2) | async-done | bytes 1572896 | tf_op jit(solution)/shard_map/all_to_all | solution.py:691
  124.6 0.9 weight_sums.1
  (47 shorter events, 1.2 us)
Async XLA Ops:
  3.5 27.2 %all-to-all-start = ((bf16[64,8,384]{2,1,0:T(8,128)(2,1)}), bf16[64,8,384]{2,1,0:T(8,128)(2,1)S(1)}, u32[]{:S(2)}, u32[]{:S(2)}) async-start(bf16[64,8,384]{2,1,0:T(8,128)(2,1)} %bitcast.15), calls=%async_computation | async-start | bytes 786432 | tf_op jit(solution)/shard_map/all_to_all | solution.py:585
  15.0 0.9 copy-start.8
  15.9 1.2 copy-start.9
  17.2 0.7 copy-start.17
  18.9 6.3 %collective-permute-start = (f32[256,128]{1,0:T(8,128)S(1)}, f32[256,128]{1,0:T(8,128)S(1)}, u32[]{:S(2)}, u32[]{:S(2)}) collective-permute-start(f32[256,128]{1,0:T(8,128)S(1)} %get-tuple-element.41.refs_1_), channel_id=1, source_target_pairs={{0,64},{64,0},{1,65},{65,1},{2,66},{66,2},{3,67},{67,3},{4,68},{68... | collective-permute-start | bytes 393224 | tf_op jit(solution)/shard_map/ppermute | solution.py:25
  19.0 1.0 copy-start.5
  20.1 0.7 copy-start.20
  21.6 38.9 %collective-permute-start.4 = (bf16[272,1024]{1,0:T(8,128)(2,1)S(1)}, bf16[272,1024]{1,0:T(8,128)(2,1)S(1)}, u32[]{:S(2)}, u32[]{:S(2)}) collective-permute-start(bf16[272,1024]{1,0:T(8,128)(2,1)S(1)} %norms.1.refs_0_.refs_4_.refs_1_), channel_id=1, source_target_pairs={{0,17},{1,16},{2,19},{3,18},{16,1},{17,0},{18,3},{19,2},{32,49},{3... | collective-permute-start | bytes 1671176 | tf_op jit(solution)/shard_map/ppermute | solution.py:35
  24.2 36.8 %collective-permute-start.3 = (bf16[272,1024]{1,0:T(8,128)(2,1)S(1)}, bf16[272,1024]{1,0:T(8,128)(2,1)S(1)}, u32[]{:S(2)}, u32[]{:S(2)}) collective-permute-start(bf16[272,1024]{1,0:T(8,128)(2,1)S(1)} %norms.1.refs_0_.refs_4_.refs_1_), channel_id=1, source_target_pairs={{0,16},{1,17},{2,18},{3,19},{16,0},{17,1},{18,2},{19,3},{32,48},{3... | collective-permute-start | bytes 1671176 | tf_op jit(solution)/shard_map/ppermute | solution.py:35
  24.7 36.2 %collective-permute-start.2 = (bf16[272,1024]{1,0:T(8,128)(2,1)S(1)}, bf16[272,1024]{1,0:T(8,128)(2,1)S(1)}, u32[]{:S(2)}, u32[]{:S(2)}) collective-permute-start(bf16[272,1024]{1,0:T(8,128)(2,1)S(1)} %norms.1.refs_0_.refs_4_.refs_1_), channel_id=1, source_target_pairs={{0,1},{1,0},{2,3},{3,2},{16,17},{17,16},{18,19},{19,18},{32,33},{3... | collective-permute-start | bytes 1671176 | tf_op jit(solution)/shard_map/ppermute | solution.py:35
  25.2 0.9 copy-start.16
  29.2 0.7 copy-start.11
  30.0 0.7 copy-start.13
  30.7 7.6 %copy-start.7 = (bf16[64,8,384]{2,1,0:T(8,128)(2,1)}, bf16[64,8,384]{2,1,0:T(8,128)(2,1)S(1)}, u32[]{:S(2)}) copy-start(bf16[64,8,384]{2,1,0:T(8,128)(2,1)S(1)} %all-to-all-done) | copy-start | bytes 1179652
  38.2 1.6 %collective-permute-start.1 = (f32[512,128]{1,0:T(8,128)S(1)}, f32[512,128]{1,0:T(8,128)S(1)}, u32[]{:S(2)}, u32[]{:S(2)}) collective-permute-start(f32[512,128]{1,0:T(8,128)S(1)} %get-tuple-element.47.refs_2_), channel_id=1, source_target_pairs={{0,64},{64,0},{1,65},{65,1},{2,66},{66,2},{3,67},{67,3},{4,68},{68... | collective-permute-start | bytes 786440 | tf_op jit(solution)/shard_map/ppermute | solution.py:25
  46.2 0.7 copy-start.15
  46.9 22.5 %copy-start.18 = (s32[2,128]{1,0:T(2,128)S(1)}, s32[2,128]{1,0:T(2,128)}, u32[]{:S(2)}) copy-start(s32[2,128]{1,0:T(2,128)} %get-tuple-element.38.refs_2_.refs_0_) | copy-start | bytes 3076
  46.9 22.5 %all-to-all-start.1 = ((bf16[64,8,256]{2,1,0:T(8,128)(2,1)}), bf16[64,8,256]{2,1,0:T(8,128)(2,1)S(1)}, u32[]{:S(2)}, u32[]{:S(2)}) async-start(bf16[64,8,256]{2,1,0:T(8,128)(2,1)} %bitcast.3), calls=%async_computation.1 | async-start | bytes 524288 | tf_op jit(solution)/shard_map/all_to_all | solution.py:621
  57.4 16.7 %collective-permute-start.9 = (bf16[256,768]{1,0:T(8,128)(2,1)}, bf16[256,768]{1,0:T(8,128)(2,1)}, u32[]{:S(2)}, u32[]{:S(2)}) collective-permute-start(bf16[256,768]{1,0:T(8,128)(2,1)} %get-tuple-element.61), channel_id=1, source_target_pairs={{0,1},{1,0},{2,3},{3,2},{4,5},{5,4},{6,7},{7,6},{8,9},{9,8},{10,11... | collective-permute-start | bytes 1179656 | tf_op jit(solution)/shard_map/ppermute | solution.py:35
  59.0 22.5 %collective-permute-start.10 = (bf16[256,768]{1,0:T(8,128)(2,1)}, bf16[256,768]{1,0:T(8,128)(2,1)}, u32[]{:S(2)}, u32[]{:S(2)}) collective-permute-start(bf16[256,768]{1,0:T(8,128)(2,1)} %get-tuple-element.62), channel_id=1, source_target_pairs={{0,4},{1,5},{2,6},{3,7},{4,0},{5,1},{6,2},{7,3},{8,12},{9,13},{10,... | collective-permute-start | bytes 1179656 | tf_op jit(solution)/shard_map/ppermute | solution.py:35
  60.5 21.1 %collective-permute-start.11 = (bf16[256,768]{1,0:T(8,128)(2,1)}, bf16[256,768]{1,0:T(8,128)(2,1)}, u32[]{:S(2)}, u32[]{:S(2)}) collective-permute-start(bf16[256,768]{1,0:T(8,128)(2,1)} %get-tuple-element.63), channel_id=1, source_target_pairs={{0,5},{1,4},{2,7},{3,6},{4,1},{5,0},{6,3},{7,2},{8,13},{9,12},{10,... | collective-permute-start | bytes 1179656 | tf_op jit(solution)/shard_map/ppermute | solution.py:35
  61.6 0.8 copy-start.1
  65.9 19.6 %copy-start = (bf16[512,1024]{1,0:T(8,128)(2,1)S(1)}, bf16[512,1024]{1,0:T(8,128)(2,1)}, u32[]{:S(2)}) copy-start(bf16[512,1024]{1,0:T(8,128)(2,1)} %refs_4_.1) | copy-start | bytes 3145732
  69.5 1.0 copy-start.14
  70.4 0.7 copy-start.19
  71.4 1.6 %collective-permute-start.5 = (f32[256,256]{1,0:T(8,128)S(1)}, f32[256,256]{1,0:T(8,128)S(1)}, u32[]{:S(2)}, u32[]{:S(2)}) collective-permute-start(f32[256,256]{1,0:T(8,128)S(1)} %rows.1.refs_0_), channel_id=1, source_target_pairs={{0,64},{64,0},{1,65},{65,1},{2,66},{66,2},{3,67},{67,3},{4,68},{68... | collective-permute-start | bytes 786440 | tf_op jit(solution)/shard_map/ppermute | solution.py:25
  73.1 11.2 %collective-permute-start.6 = (bf16[256,256]{1,0:T(8,128)(2,1)S(1)}, bf16[256,256]{1,0:T(8,128)(2,1)S(1)}, u32[]{:S(2)}, u32[]{:S(2)}) collective-permute-start(bf16[256,256]{1,0:T(8,128)(2,1)S(1)} %row_grad.1.refs_5_.refs_4_.refs_0_.refs_2_), channel_id=1, source_target_pairs={{0,1},{1,0},{2,3},{3,2},{16,17},{17,16},{18,19},{19,18},{32,33},{3... | collective-permute-start | bytes 393224 | tf_op jit(solution)/shard_map/ppermute | solution.py:35
  73.7 10.6 %collective-permute-start.7 = (bf16[256,256]{1,0:T(8,128)(2,1)S(1)}, bf16[256,256]{1,0:T(8,128)(2,1)S(1)}, u32[]{:S(2)}, u32[]{:S(2)}) collective-permute-start(bf16[256,256]{1,0:T(8,128)(2,1)S(1)} %row_grad.1.refs_5_.refs_4_.refs_0_.refs_2_), channel_id=1, source_target_pairs={{0,16},{1,17},{2,18},{3,19},{16,0},{17,1},{18,2},{19,3},{32,48},{3... | collective-permute-start | bytes 393224 | tf_op jit(solution)/shard_map/ppermute | solution.py:35
  74.1 11.4 %collective-permute-start.8 = (bf16[256,256]{1,0:T(8,128)(2,1)S(1)}, bf16[256,256]{1,0:T(8,128)(2,1)S(1)}, u32[]{:S(2)}, u32[]{:S(2)}) collective-permute-start(bf16[256,256]{1,0:T(8,128)(2,1)S(1)} %row_grad.1.refs_5_.refs_4_.refs_0_.refs_2_), channel_id=1, source_target_pairs={{0,17},{1,16},{2,19},{3,18},{16,1},{17,0},{18,3},{19,2},{32,49},{3... | collective-permute-start | bytes 393224 | tf_op jit(solution)/shard_map/ppermute | solution.py:35
  76.7 1.1 copy-start.2
  77.7 1.2 copy-start.10
  81.6 1.0 copy-start.12
  85.5 1.0 copy-start.3
  91.2 33.3 %all-to-all-start.2 = ((bf16[64,16,768]{2,1,0:T(8,128)(2,1)}), bf16[64,16,768]{2,1,0:T(8,128)(2,1)S(1)}, u32[]{:S(2)}, u32[]{:S(2)}) async-start(bf16[64,16,768]{2,1,0:T(8,128)(2,1)} %weight_parts.1.refs_6_.refs_2_), calls=%async_computation.2 | async-start | bytes 3145728 | tf_op jit(solution)/shard_map/all_to_all | solution.py:691
  101.2 5.1 %copy-start.4 = (bf16[1024,256]{1,0:T(8,128)(2,1)S(1)}, bf16[1024,256]{1,0:T(8,128)(2,1)}, u32[]{:S(2)}) copy-start(bf16[1024,256]{1,0:T(8,128)(2,1)} %refs_3_.1) | copy-start | bytes 1572868
  101.2 5.1 %copy-start.21 = (s32[2,1,4]{2,1,0:T(1,128)S(1)}, s32[2,1,4]{2,1,0:T(1,128)}, u32[]{:S(2)}) copy-start(s32[2,1,4]{2,1,0:T(1,128)} %refs_0_.8) | copy-start | bytes 100
  114.1 7.4 %collective-permute-start.12 = (f32[256,1024]{1,0:T(8,128)S(1)}, f32[256,1024]{1,0:T(8,128)S(1)}, u32[]{:S(2)}, u32[]{:S(2)}) collective-permute-start(f32[256,1024]{1,0:T(8,128)S(1)} %get-tuple-element.66.refs_2_), channel_id=1, source_target_pairs={{0,64},{64,0},{1,65},{65,1},{2,66},{66,2},{3,67},{67,3},{4,68},{68... | collective-permute-start | bytes 3145736 | tf_op jit(solution)/shard_map/ppermute | solution.py:25
  114.2 7.4 %copy-start.6 = (bf16[2,128,1024]{2,1,0:T(8,128)(2,1)S(1)}, bf16[2,128,1024]{2,1,0:T(8,128)(2,1)}, u32[]{:S(2)}) copy-start(bf16[2,128,1024]{2,1,0:T(8,128)(2,1)} %refs_0_.9) | copy-start | bytes 1572868

commit v4 on v3

--- a/solution.py
+++ b/solution.py
@@ -146,7 +146,16 @@
     sent_ref[:, width:] = codes_out.astype(bf16)
 
 
-def top_logits_kernel(group, owners, saved_ref, table_ref, logit_ref, stat_ref, turned_ref):
+def first_kernel(group, owners, length_ref, input_ref, saved_ref, table_ref, norm_ref, logit_ref, stat_ref, turned_ref):
+    micro, count, depth = input_ref.shape
+    for m in range(micro):
+        norm_ref[m * count : (m + 1) * count] = row_norm(input_ref[m].astype(f32))[0].astype(bf16)
+    lane = iota((16, depth), 1)
+    held = jnp.zeros((16, depth), f32)
+    for m in range(micro):
+        for i in range(SEQS):
+            held = jnp.where(lane == m * SEQS + i, length_ref[m, 0, i].astype(f32), held)
+    norm_ref[micro * count :] = held.astype(bf16)
     half, width = table_ref.shape
     rows = table_ref[...].astype(f32).reshape(owners, group, half // owners // group, width)
     turned = jnp.concatenate([rows[:, q].reshape(half // group, width) for q in range(group)], axis=0).astype(bf16)
@@ -225,6 +234,7 @@
     lax.fori_loop(0, book_ref.shape[0] // group, step, 0)
 
 
+FIRST_LIMIT = 40
 GROUP_LIMIT = 40
 BOOK_GROUP = 16
 BOOK_COPIES = 4
@@ -357,19 +367,6 @@
 
 def slope_of(argument, logistic):
     return logistic * (1.0 + argument * (1.0 - logistic))
-
-
-def norms_kernel(length_ref, input_ref, out_ref):
-    micro, rows, width = input_ref.shape
-    for m in range(micro):
-        out_ref[m * rows : (m + 1) * rows] = row_norm(input_ref[m].astype(f32))[0].astype(bf16)
-    seqs = length_ref.shape[2]
-    lane = iota((16, width), 1)
-    held = jnp.zeros((16, width), f32)
-    for m in range(micro):
-        for i in range(seqs):
-            held = jnp.where(lane == m * seqs + i, length_ref[m, 0, i].astype(f32), held)
-    out_ref[micro * rows :] = held.astype(bf16)
 
 
 def seq_mask(sizes, rows):
@@ -454,16 +451,16 @@
     return list(zip(gates, values, queries, keys))
 
 
-def rows_kernel(slot_ref, returned_ref, top_ref, out_ref):
+def rows_kernel(slot_ref, returned_ref, out_ref):
     micro, rows = slot_ref.shape
     for m in range(micro):
         lines = pl.ds(m * rows, rows)
         pick = one_hot(slot_ref[m : m + 1], returned_ref.shape[0])
-        out_ref[lines, :] = top_ref[lines, :] + dot(pick, returned_ref[...], TN)
-
-
-def add_kernel(mine_ref, other_ref, out_ref):
-    out_ref[...] = (mine_ref[...] + other_ref[...]).astype(bf16)
+        out_ref[lines, :] = dot(pick, returned_ref[...], TN)
+
+
+def add_kernel(mine_ref, other_ref, top_ref, out_ref):
+    out_ref[...] = (mine_ref[...] + other_ref[...] + top_ref[...]).astype(bf16)
 
 
 def trunk_kernel(length_ref, norm_ref, row_ref, proj_ref, mix_ref, weight_in, og_ref, part_ref, pre_ref, weight_ref, sem):
@@ -584,25 +581,21 @@
     )
     got = lax.all_to_all(sent.reshape(owners, slots // owners, -1), DEV, 0, 0, tiled=True).reshape(slots, -1)
 
-    (normed,) = call(
-        norms_kernel,
-        "norms",
-        [((total + 16, model_width), bf16)],
-        (lengths, inputs),
-        "SV V",
-        limit=28,
+    normed, logits, stats, table = call(
+        functools.partial(first_kernel, group, owners),
+        "norms_and_logits",
+        [
+            ((total + 16, model_width), bf16),
+            ((total, half_clusters), f32),
+            ((total, 128), f32),
+            (top_table.shape, bf16),
+        ],
+        (lengths, inputs, saved, top_table),
+        "SHHH VVVV",
+        limit=FIRST_LIMIT,
         after=(slot_ids,),
     )
     normed_all = [normed] + [from_member(normed, "y", s) for s in range(1, group)]
-    logits, stats, table = call(
-        functools.partial(top_logits_kernel, group, owners),
-        "top_logits",
-        [((total, half_clusters), f32), ((total, 128), f32), (top_table.shape, bf16)],
-        (saved, top_table),
-        "HH VVV",
-        limit=40,
-        after=(slot_ids,),
-    )
     row_top, *top_grads, top_token = call(
         functools.partial(top_grad_kernel, group, own),
         "top_grads",
@@ -620,6 +613,7 @@
     )
     returned = lax.all_to_all(back.reshape(owners, slots // owners, width), DEV, 0, 0, tiled=True)
 
+    row_top = row_top + swap(row_top)
     head_weight, head_token = call(
         head_weight_kernel,
         "head_weight",
@@ -635,15 +629,27 @@
         token=True,
     )
 
+    table_part, table_token = call(
+        functools.partial(table_kernel, owners),
+        "table_part",
+        [((owners, 16, 128), bf16)],
+        top_all,
+        "V" * group + " V",
+        limit=16,
+        after=(back, head_token),
+        token=True,
+    )
+
     (row_part,) = call(
         rows_kernel,
         "rows",
         [((total, width), f32)],
-        (slot_ids, returned.reshape(slots, width), row_top),
-        "VHH V", limit=28,
-        after=(head_token,),
-    )
-    (row_grad,) = call(add_kernel, "row_grad", [((total, width), bf16)], (row_part, swap(row_part)), "VV V", limit=28)
+        (slot_ids, returned.reshape(slots, width)),
+        "VH V",
+        limit=28,
+        after=(table_token,),
+    )
+    (row_grad,) = call(add_kernel, "row_grad", [((total, width), bf16)], (row_part, swap(row_part), row_top), "VVV V", limit=28)
     row_all = [row_grad] + [from_member(row_grad, "y", s) for s in range(1, group)]
 
     group_rows = group * total
@@ -668,16 +674,6 @@
             pltpu.VMEM((group, total + 16, model_width), bf16),
             pltpu.SemaphoreType.DMA((group + 1,)),
         ],
-    )
-
-    (table_part,) = call(
-        functools.partial(table_kernel, owners),
-        "table_part",
-        [((owners, 16, 128), bf16)],
-        top_all,
-        "V" * group + " V",
-        limit=16,
-        after=(row_grad,),
     )
 
     (packed,) = call(

time: 127 us -> 126 us (level)
  starting transfers between devices: 43 us -> 40.4 us
  waiting for transfers between devices: 9.3 us -> 11.1 us
    ppermute x9, waiting for transfers between devices: 1.17 us -> 5.42 us  [from_member(): lax.ppermute(part, (axis, 'x'), [(i, i ^ flip) for i in range(lax.axis_si...]
    all_to_all x1, starting transfers between devices: 9.93 us -> 7.07 us  [body(): arrived = lax.all_to_all(packed, DEV, 0, 0, tiled=True)]
    ppermute x4 -> x5, waiting for transfers between devices: 3.05 us -> 0.53 us  [swap(): return lax.ppermute(part, 'section', [(0, 1), (1, 0)])]
    pallas_call x16 -> x15, Pallas kernels: 52.3 us -> 52.1 us  [call(): pl.pallas_call(run, in_specs=[pl.BlockSpec(memory_space=spaces[k]) for k...]
  transfers between devices with their start and end apart: 16 -> 17, of which waited for: 5 -> 4; matrix products, arithmetic and copies ran while one was open for 5% -> 5% of each run, Pallas kernels for 35% -> 35%
where the time goes in v4:
time: 126 us; the launch traced here: 125 us
  Pallas kernels  52.1 us (41%)
  starting transfers between devices  40.4 us (32%)
  local copies, waits for them, and re-layouts  18.4 us (15%)
  waiting for transfers between devices  11.1 us (9%)
  other arithmetic  1.57 us (1%)
    pallas_call x15, Pallas kernels, call(): pl.pallas_call(run, in_specs=[pl.BlockSpec(memory_space=spaces[k]) for k...  52.1 us
    unnamed x44, local copies, waits for them, and re-layouts  13.3 us
    all_to_all x1, starting transfers between devices, body(): lax.all_to_all(sent.reshape(owners, slots // owners, -1), DEV, 0, 0, tile...  11.5 us
    ppermute x9, starting transfers between devices, from_member(): lax.ppermute(part, (axis, 'x'), [(i, i ^ flip) for i in range(lax.axis_si...  11.1 us
    all_to_all x1, starting transfers between devices, body(): lax.all_to_all(back.reshape(owners, slots // owners, width), DEV, 0, 0, t...  10.1 us
    all_to_all x1, starting transfers between devices, body(): arrived = lax.all_to_all(packed, DEV, 0, 0, tiled=True)  7.07 us
    ppermute x9, waiting for transfers between devices, from_member(): lax.ppermute(part, (axis, 'x'), [(i, i ^ flip) for i in range(lax.axis_si...  5.42 us
    optimization_barrier x1, local copies, waits for them, and re-layouts, body(): late_weight, _ = lax.optimization_barrier((expand_weight, packed))  5.09 us
  transfers between devices with their start and end apart: 17, of which 4 were waited for; matrix products, arithmetic and copies ran while one was open for 5% of the time, Pallas kernels for 35%

profile of v4, /device:TPU:0, one launch (start us, length us, event | category | flops | bytes accessed | tf_op | source)
XLA Modules:
  0.0 124.7 jit_solution(11505547774629930570)
XLA Ops:
  0.6 2.8 %dispatch.1 = (bf16[512,384]{1,0:T(8,128)(2,1)}, s32[2,128]{1,0:T(2,128)}, f32[256,128]{1,0:T(8,128)}) custom-call(s32[2,128]{1,0:T(2,128)} %refs_0_.5, s32[2,128]{1,0:T(2,128)} %refs_1_.3, bf16[2,128,256]{2,1,0:T(8,128)(2,1)} %refs_2_.1), custom_call_target="tpu_custom_call" | custom-call | tf_op jit(solution)/shard_map/dispatch/pallas_call | solution.py:100
  3.5 11.5 %all-to-all-start = ((bf16[64,8,384]{2,1,0:T(8,128)(2,1)}), bf16[64,8,384]{2,1,0:T(8,128)(2,1)S(1)}, u32[]{:S(2)}, u32[]{:S(2)}) async-start(bf16[64,8,384]{2,1,0:T(8,128)(2,1)} %bitcast.15), calls=%async_computation | async-start | bytes 786432 | tf_op jit(solution)/shard_map/all_to_all | solution.py:582
  15.0 1.0 copy-done.5
  16.1 0.9 copy-done.8
  17.0 1.2 copy-done.9
  18.2 0.7 copy-done.18
  18.9 0.6 copy-done.20
  19.5 1.8 %norms_and_logits.1 = (bf16[272,1024]{1,0:T(8,128)(2,1)S(1)}, f32[256,2048]{1,0:T(8,128)S(1)}, f32[256,128]{1,0:T(8,128)S(1)}, bf16[2048,256]{1,0:T(8,128)(2,1)S(1)}) custom-call(s32[2,1,4]{2,1,0:T(1,128)S(1)} %copy-done.18, bf16[2,128,1024]{2,1,0:T(8,128)(2,1)S(1)} %copy-done.5, bf16[256,256]{1,0:T(8,128)(2,1)S(1)} %bitcast.11, ...), custom_call_target="tpu_custom_call" | custom-call | tf_op jit(solution)/shard_map/norms_and_logits/pallas_call | solution.py:100
  21.4 2.6 %collective-permute-start.7 = (bf16[272,1024]{1,0:T(8,128)(2,1)S(1)}, bf16[272,1024]{1,0:T(8,128)(2,1)S(1)}, u32[]{:S(2)}, u32[]{:S(2)}) collective-permute-start(bf16[272,1024]{1,0:T(8,128)(2,1)S(1)} %get-tuple-element.42.refs_0_.refs_4_.refs_1_), channel_id=1, source_target_pairs={{0,17},{1,16},{2,19},{3,18},{16,1},{17,0},{18,3},{19,2},{32,49},{3... | collective-permute-start | bytes 1671176 | tf_op jit(solution)/shard_map/ppermute | solution.py:35
  24.0 0.6 collective-permute-start.6
  24.6 0.5 collective-permute-start.5
  25.0 0.9 copy-done.16
  25.9 3.1 %top_grads.1 = (f32[256,256]{1,0:T(8,128)S(1)}, bf16[256,768]{1,0:T(8,128)(2,1)S(1)}, bf16[256,768]{1,0:T(8,128)(2,1)}, bf16[256,768]{1,0:T(8,128)(2,1)}, bf16[2...) custom-call(f32[256,2048]{1,0:T(8,128)S(1)} %get-tuple-element.44.refs_0_, f32[256,128]{1,0:T(8,128)S(1)} %get-tuple-element.45.refs_1_, ...), custom_call_target="tpu_custom_call" | custom-call | tf_op jit(solution)/shard_map/top_grads/pallas_call | solution.py:100
  29.0 0.7 copy-done.11
  29.8 7.5 %leaf_scores.1 = (f32[512,256]{1,0:T(8,128)S(1)}, f32[512,128]{1,0:T(8,128)S(1)}, bf16[512,384]{1,0:T(8,128)(2,1)S(1)}, bf16[64,256,256]{2,1,0:T(8,128)(2,1)S(1)}) custom-call(bf16[512,384]{1,0:T(8,128)(2,1)S(1)} %bitcast.9, bf16[64,256,256]{2,1,0:T(8,128)(2,1)} %refs_1_.5, f32[8,128]{1,0:T(8,128)S(1)} %get-tuple-element.48.refs_2_, ...), custom_call_target="tpu_custom_call" | custom-call | flops 4294967296 | tf_op jit(solution)/shard_map/leaf_scores/pallas_call | solution.py:100
  37.4 1.6 %collective-permute-start.2 = (bf16[256,768]{1,0:T(8,128)(2,1)}, bf16[256,768]{1,0:T(8,128)(2,1)}, u32[]{:S(2)}, u32[]{:S(2)}) collective-permute-start(bf16[256,768]{1,0:T(8,128)(2,1)} %get-tuple-element.55), channel_id=1, source_target_pairs={{0,1},{1,0},{2,3},{3,2},{4,5},{5,4},{6,7},{7,6},{8,9},{9,8},{10,11... | collective-permute-start | bytes 1179656 | tf_op jit(solution)/shard_map/ppermute | solution.py:35
  39.0 1.5 %collective-permute-start.3 = (bf16[256,768]{1,0:T(8,128)(2,1)}, bf16[256,768]{1,0:T(8,128)(2,1)}, u32[]{:S(2)}, u32[]{:S(2)}) collective-permute-start(bf16[256,768]{1,0:T(8,128)(2,1)} %get-tuple-element.56), channel_id=1, source_target_pairs={{0,4},{1,5},{2,6},{3,7},{4,0},{5,1},{6,2},{7,3},{8,12},{9,13},{10,... | collective-permute-start | bytes 1179656 | tf_op jit(solution)/shard_map/ppermute | solution.py:35
  40.5 0.9 collective-permute-start.4
  41.4 6.4 %leaf_back.1 = (bf16[512,256]{1,0:T(8,128)(2,1)}, bf16[512,256]{1,0:T(8,128)(2,1)S(1)}) custom-call(bf16[512,384]{1,0:T(8,128)(2,1)S(1)} %get-tuple-element.49.refs_0_, f32[512,256]{1,0:T(8,128)S(1)} %get-tuple-element.50.refs_1_, f32[512,128]{1,0:T(8,128)S(1)} %get-tuple-element.51.refs_2_, f32[512,128]{1,0:T(8,128)S(1)} %collective-permute-done.1.refs_3_, ...), custom_call_target="tpu_custom_call" | custom-call | tf_op jit(solution)/shard_map/leaf_back/pallas_call | solution.py:100
  47.8 0.7 copy-done.15
  48.5 10.1 %all-to-all-start.1 = ((bf16[64,8,256]{2,1,0:T(8,128)(2,1)}), bf16[64,8,256]{2,1,0:T(8,128)(2,1)S(1)}, u32[]{:S(2)}, u32[]{:S(2)}) async-start(bf16[64,8,256]{2,1,0:T(8,128)(2,1)} %bitcast.3), calls=%async_computation.1 | async-start | bytes 524288 | tf_op jit(solution)/shard_map/all_to_all | solution.py:614
  58.5 0.3 collective-permute-start.9
  58.8 0.6 slice_add_fusion.refs_2_
  59.4 0.8 copy-done.1
  60.2 3.5 %head_weight.1 = (bf16[1024,512]{1,0:T(8,128)(2,1)}, f32[8,128]{1,0:T(8,128)}) custom-call(bf16[1024,4,512]{2,1,0:T(4,128)(2,1)} %refs_0_.7, bf16[512,256]{1,0:T(8,128)(2,1)} %get-tuple-element.53.refs_1_.refs_4_, bf16[8,128]{1,0:T(8,128)(2,1)} %slice_add_fusion.refs_2_), custom_call_target="tpu_custom_call" | custom-call | tf_op jit(solution)/shard_map/head_weight/pallas_call | solution.py:100
  63.7 5.4 %collective-permute-done.4.refs_3_ = bf16[256,768]{1,0:T(8,128)(2,1)} collective-permute-done((bf16[256,768]{1,0:T(8,128)(2,1)}, bf16[256,768]{1,0:T(8,128)(2,1)}, u32[]{:S(2)}, u32[]{:S(2)}) %collective-permute-start.4) | collective-permute-done | bytes 393248 | tf_op jit(solution)/shard_map/ppermute | solution.py:35
  69.1 1.0 copy-done.12
  70.1 0.7 copy-done.17
  70.8 1.7 %table_part.1 = (bf16[64,16,128]{2,1,0:T(8,128)(2,1)S(1)}, f32[8,128]{1,0:T(8,128)S(1)}) custom-call(bf16[256,768]{1,0:T(8,128)(2,1)S(1)} %copy-done.12, bf16[256,768]{1,0:T(8,128)(2,1)} %collective-permute-done.2.refs_1_, bf16[256,768]{1,0:T(8,128)(2,1)} %collective-permute-done.3.refs_2_, bf16[256,768]{1,0:T(8,128)(2,1)} %collective-permute-done.4.refs_3_, ...), custom_call_target="tpu_custom_call" | custom-call | tf_op jit(solution)/shard_map/table_part/pallas_call | solution.py:100
  72.5 0.7 copy-done.13
  73.2 3.8 %all-to-all-done.1 = bf16[64,8,256]{2,1,0:T(8,128)(2,1)S(1)} async-done(((bf16[64,8,256]{2,1,0:T(8,128)(2,1)}), bf16[64,8,256]{2,1,0:T(8,128)(2,1)S(1)}, u32[]{:S(2)}, u32[]{:S(2)}) %all-to-all-start.1) | async-done | bytes 262176 | tf_op jit(solution)/shard_map/all_to_all | solution.py:614
  77.0 0.3 rows.1.refs_0_
  77.4 1.0 add.11.refs_2_
  78.4 0.5 collective-permute-done.8.refs_1_
  78.9 0.3 collective-permute-start.10
  79.4 3.1 %collective-permute-start.12 = (bf16[256,256]{1,0:T(8,128)(2,1)S(1)}, bf16[256,256]{1,0:T(8,128)(2,1)S(1)}, u32[]{:S(2)}, u32[]{:S(2)}) collective-permute-start(bf16[256,256]{1,0:T(8,128)(2,1)S(1)} %row_grad.1.refs_5_.refs_0_.refs_2_), channel_id=1, source_target_pairs={{0,17},{1,16},{2,19},{3,18},{16,1},{17,0},{18,3},{19,2},{32,49},{3... | collective-permute-start | bytes 393224 | tf_op jit(solution)/shard_map/ppermute | solution.py:35
  82.5 1.1 copy-done.2
  83.6 1.2 copy-done.10
  84.8 2.6 %group_forward.1 = (bf16[1024,512]{1,0:T(8,128)(2,1)S(1)}, f32[1024,512]{1,0:T(8,128)S(1)}, bf16[1024,128]{1,0:T(8,128)(2,1)S(1)}, f32[1024,128]{1,0:T(8,128)S(1...) custom-call(bf16[272,1024]{1,0:T(8,128)(2,1)S(1)} %get-tuple-element.42.refs_0_.refs_4_.refs_1_, ...), custom_call_target="tpu_custom_call" | custom-call | tf_op jit(solution)/shard_map/group_forward/pallas_call | solution.py:100
  87.5 1.0 copy-done.3
  88.5 4.7 %weight_parts.1.refs_6_.refs_2_ = bf16[64,16,768]{2,1,0:T(8,128)(2,1)} custom-call(bf16[256,256]{1,0:T(8,128)(2,1)S(1)} %row_grad.1.refs_5_.refs_0_.refs_2_, bf16[256,256]{1,0:T(8,128)(2,1)S(1)} %collective-permute-done.10.refs_1_, bf16[256,256]{1,0:T(8,128)(2,1)S(1)} %collective-permute-done.11.refs_2_, ...), custom_call_target="tpu_custom_call" | custom-call | tf_op jit(solution)/shard_map/weight_parts/pallas_call | solution.py:100
  93.2 7.1 %all-to-all-start.2 = ((bf16[64,16,768]{2,1,0:T(8,128)(2,1)}), bf16[64,16,768]{2,1,0:T(8,128)(2,1)S(1)}, u32[]{:S(2)}, u32[]{:S(2)}) async-start(bf16[64,16,768]{2,1,0:T(8,128)(2,1)} %weight_parts.1.refs_6_.refs_2_), calls=%async_computation.2 | async-start | bytes 3145728 | tf_op jit(solution)/shard_map/all_to_all | solution.py:687
  100.3 5.1 %copy.17 = bf16[1024,4,512]{2,0,1:T(8,128)(2,1)} copy(bf16[1024,4,512]{2,1,0:T(4,128)(2,1)} %refs_0_.7) | data formatting | bytes 8388608 | tf_op jit(solution)/shard_map/optimization_barrier | solution.py:689
  105.4 7.8 %trunk.1 = (bf16[256,1024]{1,0:T(8,128)(2,1)S(1)}, f32[256,1024]{1,0:T(8,128)S(1)}) custom-call(s32[2,1,4]{2,1,0:T(1,128)S(1)} %copy-done.19, bf16[272,1024]{1,0:T(8,128)(2,1)S(1)} %get-tuple-element.42.refs_0_.refs_4_.refs_1_, bf16[256,256]{1,0:T(8,128)(2,1)S(1)} %row_grad.1.refs_5_.refs_0_.refs_2_, bf16[1024,256]{1,0:T(8,128)(2,1)S(1)} %copy-done.4, ...), custom_call_target="tpu_custom_call" | custom-call | tf_op jit(solution)/shard_map/trunk/pallas_call | solution.py:100
  113.3 7.3 %leaf_book.1 = bf16[64,256,256]{2,1,0:T(8,128)(2,1)} custom-call(bf16[512,384]{1,0:T(8,128)(2,1)} %bitcast.10, bf16[512,256]{1,0:T(8,128)(2,1)} %copy-done.15, bf16[64,16,768]{2,1,0:T(8,128)(2,1)} %weight_parts.1.refs_6_.refs_2_), custom_call_target="tpu_custom_call" | custom-call | tf_op jit(solution)/shard_map/leaf_book/pallas_call | solution.py:100
  120.7 1.5 %input_grads.1 = bf16[2,128,1024]{2,1,0:T(8,128)(2,1)} custom-call(bf16[2,128,1024]{2,1,0:T(8,128)(2,1)S(1)} %copy-done.6, bf16[256,1024]{1,0:T(8,128)(2,1)S(1)} %get-tuple-element.71.refs_1_, f32[256,1024]{1,0:T(8,128)S(1)} %get-tuple-element.72.refs_2_, f32[256,1024]{1,0:T(8,128)S(1)} %collective-permute-done.13.refs_3_), custom_call_target="tpu_custom_call" | custom-call | tf_op jit(solution)/shard_map/input_grads/pallas_call | solution.py:100
  122.2 1.4 %all-to-all-done.2.refs_0_ = bf16[64,16,768]{2,1,0:T(8,128)(2,1)S(1)} async-done(((bf16[64,16,768]{2,1,0:T(8,128)(2,1)}), bf16[64,16,768]{2,1,0:T(8,128)(2,1)S(1)}, u32[]{:S(2)}, u32[]{:S(2)}) %all-to-all-start.2) | async-done | bytes 1572896 | tf_op jit(solution)/shard_map/all_to_all | solution.py:687
  123.6 0.9 weight_sums.1
  (49 shorter events, 0.6 us)
Async XLA Ops:
  3.5 26.3 %all-to-all-start = ((bf16[64,8,384]{2,1,0:T(8,128)(2,1)}), bf16[64,8,384]{2,1,0:T(8,128)(2,1)S(1)}, u32[]{:S(2)}, u32[]{:S(2)}) async-start(bf16[64,8,384]{2,1,0:T(8,128)(2,1)} %bitcast.15), calls=%async_computation | async-start | bytes 786432 | tf_op jit(solution)/shard_map/all_to_all | solution.py:582
  15.0 1.0 copy-start.5
  16.0 0.9 copy-start.8
  17.0 1.2 copy-start.9
  18.2 0.7 copy-start.18
  18.9 0.6 copy-start.20
  21.3 3.7 %collective-permute-start = (f32[256,128]{1,0:T(8,128)S(1)}, f32[256,128]{1,0:T(8,128)S(1)}, u32[]{:S(2)}, u32[]{:S(2)}) collective-permute-start(f32[256,128]{1,0:T(8,128)S(1)} %get-tuple-element.45.refs_1_), channel_id=1, source_target_pairs={{0,64},{64,0},{1,65},{65,1},{2,66},{66,2},{3,67},{67,3},{4,68},{68... | collective-permute-start | bytes 393224 | tf_op jit(solution)/shard_map/ppermute | solution.py:25
  21.4 17.6 %collective-permute-start.7 = (bf16[272,1024]{1,0:T(8,128)(2,1)S(1)}, bf16[272,1024]{1,0:T(8,128)(2,1)S(1)}, u32[]{:S(2)}, u32[]{:S(2)}) collective-permute-start(bf16[272,1024]{1,0:T(8,128)(2,1)S(1)} %get-tuple-element.42.refs_0_.refs_4_.refs_1_), channel_id=1, source_target_pairs={{0,17},{1,16},{2,19},{3,18},{16,1},{17,0},{18,3},{19,2},{32,49},{3... | collective-permute-start | bytes 1671176 | tf_op jit(solution)/shard_map/ppermute | solution.py:35
  24.0 34.5 %collective-permute-start.6 = (bf16[272,1024]{1,0:T(8,128)(2,1)S(1)}, bf16[272,1024]{1,0:T(8,128)(2,1)S(1)}, u32[]{:S(2)}, u32[]{:S(2)}) collective-permute-start(bf16[272,1024]{1,0:T(8,128)(2,1)S(1)} %get-tuple-element.42.refs_0_.refs_4_.refs_1_), channel_id=1, source_target_pairs={{0,16},{1,17},{2,18},{3,19},{16,0},{17,1},{18,2},{19,3},{32,48},{3... | collective-permute-start | bytes 1671176 | tf_op jit(solution)/shard_map/ppermute | solution.py:35
  24.6 34.3 %collective-permute-start.5 = (bf16[272,1024]{1,0:T(8,128)(2,1)S(1)}, bf16[272,1024]{1,0:T(8,128)(2,1)S(1)}, u32[]{:S(2)}, u32[]{:S(2)}) collective-permute-start(bf16[272,1024]{1,0:T(8,128)(2,1)S(1)} %get-tuple-element.42.refs_0_.refs_4_.refs_1_), channel_id=1, source_target_pairs={{0,1},{1,0},{2,3},{3,2},{16,17},{17,16},{18,19},{19,18},{32,33},{3... | collective-permute-start | bytes 1671176 | tf_op jit(solution)/shard_map/ppermute | solution.py:35
  25.0 0.9 copy-start.16
  29.0 0.7 copy-start.11
  29.8 7.6 %copy-start.7 = (bf16[64,8,384]{2,1,0:T(8,128)(2,1)}, bf16[64,8,384]{2,1,0:T(8,128)(2,1)S(1)}, u32[]{:S(2)}) copy-start(bf16[64,8,384]{2,1,0:T(8,128)(2,1)S(1)} %all-to-all-done) | copy-start | bytes 1179652
  37.3 3.2 %collective-permute-start.1 = (f32[512,128]{1,0:T(8,128)S(1)}, f32[512,128]{1,0:T(8,128)S(1)}, u32[]{:S(2)}, u32[]{:S(2)}) collective-permute-start(f32[512,128]{1,0:T(8,128)S(1)} %get-tuple-element.51.refs_2_), channel_id=1, source_target_pairs={{0,64},{64,0},{1,65},{65,1},{2,66},{66,2},{3,67},{67,3},{4,68},{68... | collective-permute-start | bytes 786440 | tf_op jit(solution)/shard_map/ppermute | solution.py:25
  37.4 26.3 %collective-permute-start.2 = (bf16[256,768]{1,0:T(8,128)(2,1)}, bf16[256,768]{1,0:T(8,128)(2,1)}, u32[]{:S(2)}, u32[]{:S(2)}) collective-permute-start(bf16[256,768]{1,0:T(8,128)(2,1)} %get-tuple-element.55), channel_id=1, source_target_pairs={{0,1},{1,0},{2,3},{3,2},{4,5},{5,4},{6,7},{7,6},{8,9},{9,8},{10,11... | collective-permute-start | bytes 1179656 | tf_op jit(solution)/shard_map/ppermute | solution.py:35
  39.0 24.7 %collective-permute-start.3 = (bf16[256,768]{1,0:T(8,128)(2,1)}, bf16[256,768]{1,0:T(8,128)(2,1)}, u32[]{:S(2)}, u32[]{:S(2)}) collective-permute-start(bf16[256,768]{1,0:T(8,128)(2,1)} %get-tuple-element.56), channel_id=1, source_target_pairs={{0,4},{1,5},{2,6},{3,7},{4,0},{5,1},{6,2},{7,3},{8,12},{9,13},{10,... | collective-permute-start | bytes 1179656 | tf_op jit(solution)/shard_map/ppermute | solution.py:35
  40.5 28.6 %collective-permute-start.4 = (bf16[256,768]{1,0:T(8,128)(2,1)}, bf16[256,768]{1,0:T(8,128)(2,1)}, u32[]{:S(2)}, u32[]{:S(2)}) collective-permute-start(bf16[256,768]{1,0:T(8,128)(2,1)} %get-tuple-element.57), channel_id=1, source_target_pairs={{0,5},{1,4},{2,7},{3,6},{4,1},{5,0},{6,3},{7,2},{8,13},{9,12},{10,... | collective-permute-start | bytes 1179656 | tf_op jit(solution)/shard_map/ppermute | solution.py:35
  47.8 0.7 copy-start.15
  48.5 28.5 %copy-start.21 = (s32[2,128]{1,0:T(2,128)S(1)}, s32[2,128]{1,0:T(2,128)}, u32[]{:S(2)}) copy-start(s32[2,128]{1,0:T(2,128)} %get-tuple-element.41.refs_4_.refs_0_) | copy-start | bytes 3076
  48.5 28.5 %all-to-all-start.1 = ((bf16[64,8,256]{2,1,0:T(8,128)(2,1)}), bf16[64,8,256]{2,1,0:T(8,128)(2,1)S(1)}, u32[]{:S(2)}, u32[]{:S(2)}) async-start(bf16[64,8,256]{2,1,0:T(8,128)(2,1)} %bitcast.3), calls=%async_computation.1 | async-start | bytes 524288 | tf_op jit(solution)/shard_map/all_to_all | solution.py:614
  58.5 18.8 %collective-permute-start.9 = (f32[256,256]{1,0:T(8,128)S(1)}, f32[256,256]{1,0:T(8,128)}, u32[]{:S(2)}, u32[]{:S(2)}) collective-permute-start(f32[256,256]{1,0:T(8,128)S(1)} %get-tuple-element.60), channel_id=1, source_target_pairs={{0,64},{64,0},{1,65},{65,1},{2,66},{66,2},{3,67},{67,3},{4,68},{68... | collective-permute-start | bytes 786440 | tf_op jit(solution)/shard_map/ppermute | solution.py:25
  59.4 0.8 copy-start.1
  63.7 23.8 %copy-start = (bf16[512,1024]{1,0:T(8,128)(2,1)S(1)}, bf16[512,1024]{1,0:T(8,128)(2,1)}, u32[]{:S(2)}) copy-start(bf16[512,1024]{1,0:T(8,128)(2,1)} %refs_4_.1) | copy-start | bytes 3145732
  69.1 1.0 copy-start.12
  70.1 0.7 copy-start.17
  72.5 0.7 copy-start.13
  77.0 10.5 %copy-start.14 = (bf16[64,16,128]{2,1,0:T(8,128)(2,1)S(1)}, bf16[64,16,128]{2,1,0:T(8,128)(2,1)}, u32[]{:S(2)}) copy-start(bf16[64,16,128]{2,1,0:T(8,128)(2,1)} %copy-done.13) | copy-start | bytes 786436
  77.3 1.6 %collective-permute-start.8 = (f32[256,256]{1,0:T(8,128)S(1)}, f32[256,256]{1,0:T(8,128)S(1)}, u32[]{:S(2)}, u32[]{:S(2)}) collective-permute-start(f32[256,256]{1,0:T(8,128)S(1)} %rows.1.refs_0_), channel_id=1, source_target_pairs={{0,64},{64,0},{1,65},{65,1},{2,66},{66,2},{3,67},{67,3},{4,68},{68... | collective-permute-start | bytes 786440 | tf_op jit(solution)/shard_map/ppermute | solution.py:25
  78.9 8.5 %collective-permute-start.10 = (bf16[256,256]{1,0:T(8,128)(2,1)S(1)}, bf16[256,256]{1,0:T(8,128)(2,1)S(1)}, u32[]{:S(2)}, u32[]{:S(2)}) collective-permute-start(bf16[256,256]{1,0:T(8,128)(2,1)S(1)} %row_grad.1.refs_5_.refs_0_.refs_2_), channel_id=1, source_target_pairs={{0,1},{1,0},{2,3},{3,2},{16,17},{17,16},{18,19},{19,18},{32,33},{3... | collective-permute-start | bytes 393224 | tf_op jit(solution)/shard_map/ppermute | solution.py:35
  79.2 8.2 %collective-permute-start.11 = (bf16[256,256]{1,0:T(8,128)(2,1)S(1)}, bf16[256,256]{1,0:T(8,128)(2,1)S(1)}, u32[]{:S(2)}, u32[]{:S(2)}) collective-permute-start(bf16[256,256]{1,0:T(8,128)(2,1)S(1)} %row_grad.1.refs_5_.refs_0_.refs_2_), channel_id=1, source_target_pairs={{0,16},{1,17},{2,18},{3,19},{16,0},{17,1},{18,2},{19,3},{32,48},{3... | collective-permute-start | bytes 393224 | tf_op jit(solution)/shard_map/ppermute | solution.py:35
  79.4 8.1 %collective-permute-start.12 = (bf16[256,256]{1,0:T(8,128)(2,1)S(1)}, bf16[256,256]{1,0:T(8,128)(2,1)S(1)}, u32[]{:S(2)}, u32[]{:S(2)}) collective-permute-start(bf16[256,256]{1,0:T(8,128)(2,1)S(1)} %row_grad.1.refs_5_.refs_0_.refs_2_), channel_id=1, source_target_pairs={{0,17},{1,16},{2,19},{3,18},{16,1},{17,0},{18,3},{19,2},{32,49},{3... | collective-permute-start | bytes 393224 | tf_op jit(solution)/shard_map/ppermute | solution.py:35
  82.5 1.1 copy-start.2
  83.6 1.2 copy-start.10
  87.5 1.0 copy-start.3
  93.2 30.4 %all-to-all-start.2 = ((bf16[64,16,768]{2,1,0:T(8,128)(2,1)}), bf16[64,16,768]{2,1,0:T(8,128)(2,1)S(1)}, u32[]{:S(2)}, u32[]{:S(2)}) async-start(bf16[64,16,768]{2,1,0:T(8,128)(2,1)} %weight_parts.1.refs_6_.refs_2_), calls=%async_computation.2 | async-start | bytes 3145728 | tf_op jit(solution)/shard_map/all_to_all | solution.py:687
  100.3 5.1 %copy-start.4 = (bf16[1024,256]{1,0:T(8,128)(2,1)S(1)}, bf16[1024,256]{1,0:T(8,128)(2,1)}, u32[]{:S(2)}) copy-start(bf16[1024,256]{1,0:T(8,128)(2,1)} %refs_3_.3) | copy-start | bytes 1572868
  100.3 5.1 %copy-start.19 = (s32[2,1,4]{2,1,0:T(1,128)S(1)}, s32[2,1,4]{2,1,0:T(1,128)}, u32[]{:S(2)}) copy-start(s32[2,1,4]{2,1,0:T(1,128)} %refs_0_.8) | copy-start | bytes 100
  113.2 7.4 %collective-permute-start.13 = (f32[256,1024]{1,0:T(8,128)S(1)}, f32[256,1024]{1,0:T(8,128)S(1)}, u32[]{:S(2)}, u32[]{:S(2)}) collective-permute-start(f32[256,1024]{1,0:T(8,128)S(1)} %get-tuple-element.72.refs_2_), channel_id=1, source_target_pairs={{0,64},{64,0},{1,65},{65,1},{2,66},{66,2},{3,67},{67,3},{4,68},{68... | collective-permute-start | bytes 3145736 | tf_op jit(solution)/shard_map/ppermute | solution.py:25
  113.3 7.4 %copy-start.6 = (bf16[2,128,1024]{2,1,0:T(8,128)(2,1)S(1)}, bf16[2,128,1024]{2,1,0:T(8,128)(2,1)}, u32[]{:S(2)}) copy-start(bf16[2,128,1024]{2,1,0:T(8,128)(2,1)} %refs_0_.9) | copy-start | bytes 1572868

commit v5 on v4

--- a/solution.py
+++ b/solution.py
@@ -25,14 +25,19 @@
     return lax.ppermute(part, "section", [(0, 1), (1, 0)])
 
 
-def member(axis):
-    return lax.rem(lax.axis_index("x"), 2) + 2 * lax.rem(lax.axis_index(axis), 2)
-
-
-def from_member(part, axis, other):
+def shifted(part, axis, step):
+    count = lax.axis_size(axis)
+    return lax.ppermute(part, axis, [(i, (i + step) % count) for i in range(count)])
+
+
+def member():
+    return lax.rem(lax.axis_index("x"), 2) + 2 * lax.rem(lax.axis_index("y"), 2)
+
+
+def from_member(part, other):
     count = lax.axis_size("x")
     flip = count * (other // 2) + other % 2
-    return lax.ppermute(part, (axis, "x"), [(i, i ^ flip) for i in range(lax.axis_size(axis) * count)])
+    return lax.ppermute(part, ("y", "x"), [(i, i ^ flip) for i in range(lax.axis_size("y") * count)])
 
 
 def dot(left, right, dims):
@@ -180,7 +185,7 @@
     quarter = half // group
     piece = own // group
     base = lax.axis_index("section") * half
-    me = member("z")
+    me = lax.axis_index("z")
     peak, mass = joined(mine_ref, other_ref)
     target = mark_ref[:, 0:1].astype(jnp.int32) - base
     total = 0.0
@@ -193,7 +198,7 @@
         total += dot(grad, table_ref[cols, :], NN)
         for s in range(group):
 
-            @pl.when(lax.bitwise_xor(me, s) == q)
+            @pl.when(lax.rem(me + s, group) == q)
             def _(s=s, grad=grad):
                 grad_refs[s][:, :quarter] = grad
                 grad_refs[s][:, quarter:] = saved_ref[...]
@@ -395,7 +400,7 @@
 
 
 def my_head():
-    return pl.ds(pl.multiple_of(member("y") * HEAD_DIM, HEAD_DIM), HEAD_DIM)
+    return pl.ds(pl.multiple_of(member() * HEAD_DIM, HEAD_DIM), HEAD_DIM)
 
 
 def head_weight_kernel(weight_in, out_ref, part_ref, flat_ref, sem):
@@ -542,7 +547,7 @@
         mixing_ref[:, head] = total[:, cols:]
     lanes = pl.ds(cols + HEAD_DIM, HEAD_DIM)
     for q in side:
-        sources = [(y * group + z) * group + x for y in side for z in side for x in side if x % 2 + 2 * (z % 2) == q]
+        sources = [(y * group + q) * group + x for y in side for x in side]
         total = sum(in_ref[i, :, lanes].astype(f32) for i in sources)
         half = total.shape[0] // 2
         table_ref[q * half : (q + 1) * half, :HEAD_DIM] = total[:half]
@@ -595,7 +600,7 @@
         limit=FIRST_LIMIT,
         after=(slot_ids,),
     )
-    normed_all = [normed] + [from_member(normed, "y", s) for s in range(1, group)]
+    normed_all = [normed] + [from_member(normed, s) for s in range(1, group)]
     row_top, *top_grads, top_token = call(
         functools.partial(top_grad_kernel, group, own),
         "top_grads",
@@ -605,7 +610,7 @@
         limit=40,
         token=True,
     )
-    top_all = [top_grads[0]] + [from_member(top_grads[s], "z", s) for s in range(1, group)]
+    top_all = [top_grads[0]] + [shifted(top_grads[s], "z", s) for s in range(1, group)]
 
     leaf, leaf_stats, got_held, book_held = leaf_scores(got, codebook, (top_token, normed[:8, :128]))
     back, leaf_grad = leaf_back(
@@ -650,7 +655,7 @@
         after=(table_token,),
     )
     (row_grad,) = call(add_kernel, "row_grad", [((total, width), bf16)], (row_part, swap(row_part), row_top), "VVV V", limit=28)
-    row_all = [row_grad] + [from_member(row_grad, "y", s) for s in range(1, group)]
+    row_all = [row_grad] + [from_member(row_grad, s) for s in range(1, group)]
 
     group_rows = group * total
     group_forward = call(

time: 126 us -> 121 us (0.960)
  waiting for transfers between devices: 11.1 us -> 4.18 us
  starting transfers between devices: 40.4 us -> 43.2 us
    ppermute x9, waiting for transfers between devices: 5.42 us -> 0.39 us  [the longest x6 0.38 us: from_member(): lax.ppermute(part, ('y', 'x'), [(i, i ^ flip) for i in range(lax.axis_siz...]
    all_to_all x1, starting transfers between devices: 7.07 us -> 10.2 us  [body(): arrived = lax.all_to_all(packed, DEV, 0, 0, tiled=True)]
    all_to_all x1, waiting for transfers between devices: 3.76 us -> 1.22 us  [body(): lax.all_to_all(back.reshape(owners, slots // owners, width), DEV, 0, 0, t...]
    all_to_all x1, starting transfers between devices: 10.1 us -> 7.99 us  [body(): lax.all_to_all(back.reshape(owners, slots // owners, width), DEV, 0, 0, t...]
    ppermute x9, starting transfers between devices: 11.1 us -> 12.9 us  [the longest x6 7.14 us: from_member(): lax.ppermute(part, ('y', 'x'), [(i, i ^ flip) for i in range(lax.axis_siz...]
  transfers between devices with their start and end apart: 17 -> 17, of which waited for: 4 -> 4; matrix products, arithmetic and copies ran while one was open for 5% -> 6% of each run, Pallas kernels for 35% -> 36%
where the time goes in v5:
time: 121 us
  Pallas kernels  52.1 us (43%)
  starting transfers between devices  43.2 us (36%)
  local copies, waits for them, and re-layouts  18.5 us (15%)
  waiting for transfers between devices  4.18 us (3%)
  other arithmetic  1.57 us (1%)
    pallas_call x15, Pallas kernels, call(): pl.pallas_call(run, in_specs=[pl.BlockSpec(memory_space=spaces[k]) for k...  52.1 us
    unnamed x44, local copies, waits for them, and re-layouts  13.4 us
    all_to_all x1, starting transfers between devices, body(): lax.all_to_all(sent.reshape(owners, slots // owners, -1), DEV, 0, 0, tile...  11.5 us
    all_to_all x1, starting transfers between devices, body(): arrived = lax.all_to_all(packed, DEV, 0, 0, tiled=True)  10.2 us
    all_to_all x1, starting transfers between devices, body(): lax.all_to_all(back.reshape(owners, slots // owners, width), DEV, 0, 0, t...  7.99 us
    ppermute x6, starting transfers between devices, from_member(): lax.ppermute(part, ('y', 'x'), [(i, i ^ flip) for i in range(lax.axis_siz...  7.14 us
    ppermute x3, starting transfers between devices, shifted(): lax.ppermute(part, axis, [(i, (i + step) % count) for i in range(count)])  5.77 us
    optimization_barrier x1, local copies, waits for them, and re-layouts, body(): late_weight, _ = lax.optimization_barrier((expand_weight, packed))  5.09 us
  transfers between devices with their start and end apart: 17, of which 4 were waited for; matrix products, arithmetic and copies ran while one was open for 6% of the time, Pallas kernels for 36%

profile of v5, /device:TPU:0, one launch (start us, length us, event | category | flops | bytes accessed | tf_op | source)
XLA Modules:
  0.0 120.6 jit_solution(1074464053029483957)
XLA Ops:
  0.6 2.8 %dispatch.1 = (bf16[512,384]{1,0:T(8,128)(2,1)}, s32[2,128]{1,0:T(2,128)}, f32[256,128]{1,0:T(8,128)}) custom-call(s32[2,128]{1,0:T(2,128)} %refs_0_.5, s32[2,128]{1,0:T(2,128)} %refs_1_.3, bf16[2,128,256]{2,1,0:T(8,128)(2,1)} %refs_2_.1), custom_call_target="tpu_custom_call" | custom-call | tf_op jit(solution)/shard_map/dispatch/pallas_call | solution.py:105
  3.5 11.5 %all-to-all-start = ((bf16[64,8,384]{2,1,0:T(8,128)(2,1)}), bf16[64,8,384]{2,1,0:T(8,128)(2,1)S(1)}, u32[]{:S(2)}, u32[]{:S(2)}) async-start(bf16[64,8,384]{2,1,0:T(8,128)(2,1)} %bitcast.15), calls=%async_computation | async-start | bytes 786432 | tf_op jit(solution)/shard_map/all_to_all | solution.py:587
  15.0 1.0 copy-done.5
  16.1 0.9 copy-done.8
  17.0 1.2 %copy-done.9 = bf16[2048,256]{1,0:T(8,128)(2,1)S(1)} copy-done((bf16[2048,256]{1,0:T(8,128)(2,1)S(1)}, bf16[2048,256]{1,0:T(8,128)(2,1)}, u32[]{:S(2)}) %copy-start.9) | copy-done | bytes 1048600
  18.2 0.7 copy-done.18
  18.9 0.6 copy-done.20
  19.5 1.8 %norms_and_logits.1 = (bf16[272,1024]{1,0:T(8,128)(2,1)S(1)}, f32[256,2048]{1,0:T(8,128)S(1)}, f32[256,128]{1,0:T(8,128)S(1)}, bf16[2048,256]{1,0:T(8,128)(2,1)S(1)}) custom-call(s32[2,1,4]{2,1,0:T(1,128)S(1)} %copy-done.18, bf16[2,128,1024]{2,1,0:T(8,128)(2,1)S(1)} %copy-done.5, bf16[256,256]{1,0:T(8,128)(2,1)S(1)} %bitcast.11, ...), custom_call_target="tpu_custom_call" | custom-call | tf_op jit(solution)/shard_map/norms_and_logits/pallas_call | solution.py:105
  21.4 2.6 %collective-permute-start.7 = (bf16[272,1024]{1,0:T(8,128)(2,1)S(1)}, bf16[272,1024]{1,0:T(8,128)(2,1)S(1)}, u32[]{:S(2)}, u32[]{:S(2)}) collective-permute-start(bf16[272,1024]{1,0:T(8,128)(2,1)S(1)} %get-tuple-element.42.refs_0_.refs_4_.refs_1_), channel_id=1, source_target_pairs={{0,17},{1,16},{2,19},{3,18},{16,1},{17,0},{18,3},{19,2},{32,49},{3... | collective-permute-start | bytes 1671176 | tf_op jit(solution)/shard_map/ppermute | solution.py:40
  24.0 0.6 collective-permute-start.6
  24.6 0.5 collective-permute-start.5
  25.0 0.9 copy-done.16
  25.9 3.1 %top_grads.1 = (f32[256,256]{1,0:T(8,128)S(1)}, bf16[256,768]{1,0:T(8,128)(2,1)S(1)}, bf16[256,768]{1,0:T(8,128)(2,1)}, bf16[256,768]{1,0:T(8,128)(2,1)}, bf16[2...) custom-call(f32[256,2048]{1,0:T(8,128)S(1)} %get-tuple-element.44.refs_0_, f32[256,128]{1,0:T(8,128)S(1)} %get-tuple-element.45.refs_1_, ...), custom_call_target="tpu_custom_call" | custom-call | tf_op jit(solution)/shard_map/top_grads/pallas_call | solution.py:105
  29.0 0.7 copy-done.11
  29.8 7.5 %leaf_scores.1 = (f32[512,256]{1,0:T(8,128)S(1)}, f32[512,128]{1,0:T(8,128)S(1)}, bf16[512,384]{1,0:T(8,128)(2,1)S(1)}, bf16[64,256,256]{2,1,0:T(8,128)(2,1)S(1)}) custom-call(bf16[512,384]{1,0:T(8,128)(2,1)S(1)} %bitcast.9, bf16[64,256,256]{2,1,0:T(8,128)(2,1)} %refs_1_.5, f32[8,128]{1,0:T(8,128)S(1)} %get-tuple-element.48.refs_2_, ...), custom_call_target="tpu_custom_call" | custom-call | flops 4294967296 | tf_op jit(solution)/shard_map/leaf_scores/pallas_call | solution.py:105
  37.4 1.6 %collective-permute-start.2 = (bf16[256,768]{1,0:T(8,128)(2,1)}, bf16[256,768]{1,0:T(8,128)(2,1)}, u32[]{:S(2)}, u32[]{:S(2)}) collective-permute-start(bf16[256,768]{1,0:T(8,128)(2,1)} %get-tuple-element.55), channel_id=1, source_target_pairs={{0,4},{4,8},{8,12},{12,0},{1,5},{5,9},{9,13},{13,1},{2,6},{6,10},{... | collective-permute-start | bytes 1179656 | tf_op jit(solution)/shard_map/ppermute | solution.py:30
  39.0 2.7 %collective-permute-start.3 = (bf16[256,768]{1,0:T(8,128)(2,1)}, bf16[256,768]{1,0:T(8,128)(2,1)}, u32[]{:S(2)}, u32[]{:S(2)}) collective-permute-start(bf16[256,768]{1,0:T(8,128)(2,1)} %get-tuple-element.56), channel_id=1, source_target_pairs={{0,8},{4,12},{8,0},{12,4},{1,9},{5,13},{9,1},{13,5},{2,10},{6,14},... | collective-permute-start | bytes 1179656 | tf_op jit(solution)/shard_map/ppermute | solution.py:30
  41.7 1.5 %collective-permute-start.4 = (bf16[256,768]{1,0:T(8,128)(2,1)}, bf16[256,768]{1,0:T(8,128)(2,1)}, u32[]{:S(2)}, u32[]{:S(2)}) collective-permute-start(bf16[256,768]{1,0:T(8,128)(2,1)} %get-tuple-element.57), channel_id=1, source_target_pairs={{0,12},{4,0},{8,4},{12,8},{1,13},{5,1},{9,5},{13,9},{2,14},{6,2},{... | collective-permute-start | bytes 1179656 | tf_op jit(solution)/shard_map/ppermute | solution.py:30
  43.2 6.4 %leaf_back.1 = (bf16[512,256]{1,0:T(8,128)(2,1)}, bf16[512,256]{1,0:T(8,128)(2,1)S(1)}) custom-call(bf16[512,384]{1,0:T(8,128)(2,1)S(1)} %get-tuple-element.49.refs_0_, f32[512,256]{1,0:T(8,128)S(1)} %get-tuple-element.50.refs_1_, f32[512,128]{1,0:T(8,128)S(1)} %get-tuple-element.51.refs_2_, f32[512,128]{1,0:T(8,128)S(1)} %collective-permute-done.1.refs_3_, ...), custom_call_target="tpu_custom_call" | custom-call | tf_op jit(solution)/shard_map/leaf_back/pallas_call | solution.py:105
  49.6 0.7 copy-done.15
  50.2 8.0 %all-to-all-start.1 = ((bf16[64,8,256]{2,1,0:T(8,128)(2,1)}), bf16[64,8,256]{2,1,0:T(8,128)(2,1)S(1)}, u32[]{:S(2)}, u32[]{:S(2)}) async-start(bf16[64,8,256]{2,1,0:T(8,128)(2,1)} %bitcast.3), calls=%async_computation.1 | async-start | bytes 524288 | tf_op jit(solution)/shard_map/all_to_all | solution.py:619
  58.5 0.6 slice_add_fusion.refs_2_
  59.1 0.8 copy-done.1
  59.9 3.5 %head_weight.1 = (bf16[1024,512]{1,0:T(8,128)(2,1)}, f32[8,128]{1,0:T(8,128)}) custom-call(bf16[1024,4,512]{2,1,0:T(4,128)(2,1)} %refs_0_.7, bf16[512,256]{1,0:T(8,128)(2,1)} %get-tuple-element.53.refs_1_.refs_4_, bf16[8,128]{1,0:T(8,128)(2,1)} %slice_add_fusion.refs_2_), custom_call_target="tpu_custom_call" | custom-call | tf_op jit(solution)/shard_map/head_weight/pallas_call | solution.py:105
  63.5 1.1 copy-done.12
  64.5 0.7 copy-done.17
  65.2 1.7 %table_part.1 = (bf16[64,16,128]{2,1,0:T(8,128)(2,1)S(1)}, f32[8,128]{1,0:T(8,128)S(1)}) custom-call(bf16[256,768]{1,0:T(8,128)(2,1)S(1)} %copy-done.12, bf16[256,768]{1,0:T(8,128)(2,1)} %collective-permute-done.2.refs_1_, bf16[256,768]{1,0:T(8,128)(2,1)} %collective-permute-done.3.refs_2_, bf16[256,768]{1,0:T(8,128)(2,1)} %collective-permute-done.4.refs_3_, ...), custom_call_target="tpu_custom_call" | custom-call | tf_op jit(solution)/shard_map/table_part/pallas_call | solution.py:105
  66.9 0.7 copy-done.13
  67.6 1.2 %all-to-all-done.1 = bf16[64,8,256]{2,1,0:T(8,128)(2,1)S(1)} async-done(((bf16[64,8,256]{2,1,0:T(8,128)(2,1)}), bf16[64,8,256]{2,1,0:T(8,128)(2,1)S(1)}, u32[]{:S(2)}, u32[]{:S(2)}) %all-to-all-start.1) | async-done | bytes 262176 | tf_op jit(solution)/shard_map/all_to_all | solution.py:619
  68.9 0.3 rows.1.refs_0_
  69.3 1.0 add.11.refs_2_
  70.3 0.5 collective-permute-done.8.refs_1_
  70.8 0.7 collective-permute-start.10
  71.5 1.4 %collective-permute-start.11 = (bf16[256,256]{1,0:T(8,128)(2,1)S(1)}, bf16[256,256]{1,0:T(8,128)(2,1)S(1)}, u32[]{:S(2)}, u32[]{:S(2)}) collective-permute-start(bf16[256,256]{1,0:T(8,128)(2,1)S(1)} %row_grad.1.refs_5_.refs_0_.refs_2_), channel_id=1, source_target_pairs={{0,16},{1,17},{2,18},{3,19},{16,0},{17,1},{18,2},{19,3},{32,48},{3... | collective-permute-start | bytes 393224 | tf_op jit(solution)/shard_map/ppermute | solution.py:40
  72.9 1.5 %collective-permute-start.12 = (bf16[256,256]{1,0:T(8,128)(2,1)S(1)}, bf16[256,256]{1,0:T(8,128)(2,1)S(1)}, u32[]{:S(2)}, u32[]{:S(2)}) collective-permute-start(bf16[256,256]{1,0:T(8,128)(2,1)S(1)} %row_grad.1.refs_5_.refs_0_.refs_2_), channel_id=1, source_target_pairs={{0,17},{1,16},{2,19},{3,18},{16,1},{17,0},{18,3},{19,2},{32,49},{3... | collective-permute-start | bytes 393224 | tf_op jit(solution)/shard_map/ppermute | solution.py:40
  74.4 1.1 copy-done.2
  75.5 1.2 %copy-done.10 = bf16[1024,512]{1,0:T(8,128)(2,1)S(1)} copy-done((bf16[1024,512]{1,0:T(8,128)(2,1)S(1)}, bf16[1024,512]{1,0:T(8,128)(2,1)}, u32[]{:S(2)}) %copy-start.10) | copy-done | bytes 1048600
  76.7 2.6 %group_forward.1 = (bf16[1024,512]{1,0:T(8,128)(2,1)S(1)}, f32[1024,512]{1,0:T(8,128)S(1)}, bf16[1024,128]{1,0:T(8,128)(2,1)S(1)}, f32[1024,128]{1,0:T(8,128)S(1...) custom-call(bf16[272,1024]{1,0:T(8,128)(2,1)S(1)} %get-tuple-element.42.refs_0_.refs_4_.refs_1_, ...), custom_call_target="tpu_custom_call" | custom-call | tf_op jit(solution)/shard_map/group_forward/pallas_call | solution.py:105
  79.3 0.4 collective-permute-done.11.refs_2_
  79.7 1.0 copy-done.3
  80.7 4.7 %weight_parts.1.refs_6_.refs_2_ = bf16[64,16,768]{2,1,0:T(8,128)(2,1)} custom-call(bf16[256,256]{1,0:T(8,128)(2,1)S(1)} %row_grad.1.refs_5_.refs_0_.refs_2_, bf16[256,256]{1,0:T(8,128)(2,1)S(1)} %collective-permute-done.10.refs_1_, bf16[256,256]{1,0:T(8,128)(2,1)S(1)} %collective-permute-done.11.refs_2_, ...), custom_call_target="tpu_custom_call" | custom-call | tf_op jit(solution)/shard_map/weight_parts/pallas_call | solution.py:105
  85.4 10.2 %all-to-all-start.2 = ((bf16[64,16,768]{2,1,0:T(8,128)(2,1)}), bf16[64,16,768]{2,1,0:T(8,128)(2,1)S(1)}, u32[]{:S(2)}, u32[]{:S(2)}) async-start(bf16[64,16,768]{2,1,0:T(8,128)(2,1)} %weight_parts.1.refs_6_.refs_2_), calls=%async_computation.2 | async-start | bytes 3145728 | tf_op jit(solution)/shard_map/all_to_all | solution.py:692
  95.6 5.1 %copy.17 = bf16[1024,4,512]{2,0,1:T(8,128)(2,1)} copy(bf16[1024,4,512]{2,1,0:T(4,128)(2,1)} %refs_0_.7) | data formatting | bytes 8388608 | tf_op jit(solution)/shard_map/optimization_barrier | solution.py:694
  100.7 7.8 %trunk.1 = (bf16[256,1024]{1,0:T(8,128)(2,1)S(1)}, f32[256,1024]{1,0:T(8,128)S(1)}) custom-call(s32[2,1,4]{2,1,0:T(1,128)S(1)} %copy-done.19, bf16[272,1024]{1,0:T(8,128)(2,1)S(1)} %get-tuple-element.42.refs_0_.refs_4_.refs_1_, bf16[256,256]{1,0:T(8,128)(2,1)S(1)} %row_grad.1.refs_5_.refs_0_.refs_2_, bf16[1024,256]{1,0:T(8,128)(2,1)S(1)} %copy-done.4, ...), custom_call_target="tpu_custom_call" | custom-call | tf_op jit(solution)/shard_map/trunk/pallas_call | solution.py:105
  108.7 7.3 %leaf_book.1 = bf16[64,256,256]{2,1,0:T(8,128)(2,1)} custom-call(bf16[512,384]{1,0:T(8,128)(2,1)} %bitcast.10, bf16[512,256]{1,0:T(8,128)(2,1)} %copy-done.15, bf16[64,16,768]{2,1,0:T(8,128)(2,1)} %weight_parts.1.refs_6_.refs_2_), custom_call_target="tpu_custom_call" | custom-call | tf_op jit(solution)/shard_map/leaf_book/pallas_call | solution.py:105
  116.0 1.5 %input_grads.1 = bf16[2,128,1024]{2,1,0:T(8,128)(2,1)} custom-call(bf16[2,128,1024]{2,1,0:T(8,128)(2,1)S(1)} %copy-done.6, bf16[256,1024]{1,0:T(8,128)(2,1)S(1)} %get-tuple-element.71.refs_1_, f32[256,1024]{1,0:T(8,128)S(1)} %get-tuple-element.72.refs_2_, f32[256,1024]{1,0:T(8,128)S(1)} %collective-permute-done.13.refs_3_), custom_call_target="tpu_custom_call" | custom-call | tf_op jit(solution)/shard_map/input_grads/pallas_call | solution.py:105
  117.5 2.0 %all-to-all-done.2.refs_0_ = bf16[64,16,768]{2,1,0:T(8,128)(2,1)S(1)} async-done(((bf16[64,16,768]{2,1,0:T(8,128)(2,1)}), bf16[64,16,768]{2,1,0:T(8,128)(2,1)S(1)}, u32[]{:S(2)}, u32[]{:S(2)}) %all-to-all-start.2) | async-done | bytes 1572896 | tf_op jit(solution)/shard_map/all_to_all | solution.py:692
  119.6 0.9 weight_sums.1
  (49 shorter events, 0.7 us)
Async XLA Ops:
  3.5 26.3 %all-to-all-start = ((bf16[64,8,384]{2,1,0:T(8,128)(2,1)}), bf16[64,8,384]{2,1,0:T(8,128)(2,1)S(1)}, u32[]{:S(2)}, u32[]{:S(2)}) async-start(bf16[64,8,384]{2,1,0:T(8,128)(2,1)} %bitcast.15), calls=%async_computation | async-start | bytes 786432 | tf_op jit(solution)/shard_map/all_to_all | solution.py:587
  15.0 1.0 copy-start.5
  16.0 0.9 copy-start.8
  17.0 1.2 %copy-start.9 = (bf16[2048,256]{1,0:T(8,128)(2,1)S(1)}, bf16[2048,256]{1,0:T(8,128)(2,1)}, u32[]{:S(2)}) copy-start(bf16[2048,256]{1,0:T(8,128)(2,1)} %refs_3_.2) | copy-start | bytes 3145732
  18.2 0.7 copy-start.18
  18.9 0.6 copy-start.20
  21.3 3.7 %collective-permute-start = (f32[256,128]{1,0:T(8,128)S(1)}, f32[256,128]{1,0:T(8,128)S(1)}, u32[]{:S(2)}, u32[]{:S(2)}) collective-permute-start(f32[256,128]{1,0:T(8,128)S(1)} %get-tuple-element.45.refs_1_), channel_id=1, source_target_pairs={{0,64},{64,0},{1,65},{65,1},{2,66},{66,2},{3,67},{67,3},{4,68},{68... | collective-permute-start | bytes 393224 | tf_op jit(solution)/shard_map/ppermute | solution.py:25
  21.4 17.6 %collective-permute-start.7 = (bf16[272,1024]{1,0:T(8,128)(2,1)S(1)}, bf16[272,1024]{1,0:T(8,128)(2,1)S(1)}, u32[]{:S(2)}, u32[]{:S(2)}) collective-permute-start(bf16[272,1024]{1,0:T(8,128)(2,1)S(1)} %get-tuple-element.42.refs_0_.refs_4_.refs_1_), channel_id=1, source_target_pairs={{0,17},{1,16},{2,19},{3,18},{16,1},{17,0},{18,3},{19,2},{32,49},{3... | collective-permute-start | bytes 1671176 | tf_op jit(solution)/shard_map/ppermute | solution.py:40
  24.0 34.2 %collective-permute-start.6 = (bf16[272,1024]{1,0:T(8,128)(2,1)S(1)}, bf16[272,1024]{1,0:T(8,128)(2,1)S(1)}, u32[]{:S(2)}, u32[]{:S(2)}) collective-permute-start(bf16[272,1024]{1,0:T(8,128)(2,1)S(1)} %get-tuple-element.42.refs_0_.refs_4_.refs_1_), channel_id=1, source_target_pairs={{0,16},{1,17},{2,18},{3,19},{16,0},{17,1},{18,2},{19,3},{32,48},{3... | collective-permute-start | bytes 1671176 | tf_op jit(solution)/shard_map/ppermute | solution.py:40
  24.6 34.0 %collective-permute-start.5 = (bf16[272,1024]{1,0:T(8,128)(2,1)S(1)}, bf16[272,1024]{1,0:T(8,128)(2,1)S(1)}, u32[]{:S(2)}, u32[]{:S(2)}) collective-permute-start(bf16[272,1024]{1,0:T(8,128)(2,1)S(1)} %get-tuple-element.42.refs_0_.refs_4_.refs_1_), channel_id=1, source_target_pairs={{0,1},{1,0},{2,3},{3,2},{16,17},{17,16},{18,19},{19,18},{32,33},{3... | collective-permute-start | bytes 1671176 | tf_op jit(solution)/shard_map/ppermute | solution.py:40
  25.0 0.9 copy-start.16
  29.0 0.7 copy-start.11
  29.8 7.5 %copy-start.7 = (bf16[64,8,384]{2,1,0:T(8,128)(2,1)}, bf16[64,8,384]{2,1,0:T(8,128)(2,1)S(1)}, u32[]{:S(2)}) copy-start(bf16[64,8,384]{2,1,0:T(8,128)(2,1)S(1)} %all-to-all-done) | copy-start | bytes 1179652
  37.3 4.4 %collective-permute-start.1 = (f32[512,128]{1,0:T(8,128)S(1)}, f32[512,128]{1,0:T(8,128)S(1)}, u32[]{:S(2)}, u32[]{:S(2)}) collective-permute-start(f32[512,128]{1,0:T(8,128)S(1)} %get-tuple-element.51.refs_2_), channel_id=1, source_target_pairs={{0,64},{64,0},{1,65},{65,1},{2,66},{66,2},{3,67},{67,3},{4,68},{68... | collective-permute-start | bytes 786440 | tf_op jit(solution)/shard_map/ppermute | solution.py:25
  37.4 26.0 %collective-permute-start.2 = (bf16[256,768]{1,0:T(8,128)(2,1)}, bf16[256,768]{1,0:T(8,128)(2,1)}, u32[]{:S(2)}, u32[]{:S(2)}) collective-permute-start(bf16[256,768]{1,0:T(8,128)(2,1)} %get-tuple-element.55), channel_id=1, source_target_pairs={{0,4},{4,8},{8,12},{12,0},{1,5},{5,9},{9,13},{13,1},{2,6},{6,10},{... | collective-permute-start | bytes 1179656 | tf_op jit(solution)/shard_map/ppermute | solution.py:30
  39.0 24.4 %collective-permute-start.3 = (bf16[256,768]{1,0:T(8,128)(2,1)}, bf16[256,768]{1,0:T(8,128)(2,1)}, u32[]{:S(2)}, u32[]{:S(2)}) collective-permute-start(bf16[256,768]{1,0:T(8,128)(2,1)} %get-tuple-element.56), channel_id=1, source_target_pairs={{0,8},{4,12},{8,0},{12,4},{1,9},{5,13},{9,1},{13,5},{2,10},{6,14},... | collective-permute-start | bytes 1179656 | tf_op jit(solution)/shard_map/ppermute | solution.py:30
  41.7 21.7 %collective-permute-start.4 = (bf16[256,768]{1,0:T(8,128)(2,1)}, bf16[256,768]{1,0:T(8,128)(2,1)}, u32[]{:S(2)}, u32[]{:S(2)}) collective-permute-start(bf16[256,768]{1,0:T(8,128)(2,1)} %get-tuple-element.57), channel_id=1, source_target_pairs={{0,12},{4,0},{8,4},{12,8},{1,13},{5,1},{9,5},{13,9},{2,14},{6,2},{... | collective-permute-start | bytes 1179656 | tf_op jit(solution)/shard_map/ppermute | solution.py:30
  49.6 0.7 copy-start.15
  50.2 18.6 %copy-start.21 = (s32[2,128]{1,0:T(2,128)S(1)}, s32[2,128]{1,0:T(2,128)}, u32[]{:S(2)}) copy-start(s32[2,128]{1,0:T(2,128)} %get-tuple-element.41.refs_4_.refs_0_) | copy-start | bytes 3076
  50.2 18.6 %all-to-all-start.1 = ((bf16[64,8,256]{2,1,0:T(8,128)(2,1)}), bf16[64,8,256]{2,1,0:T(8,128)(2,1)S(1)}, u32[]{:S(2)}, u32[]{:S(2)}) async-start(bf16[64,8,256]{2,1,0:T(8,128)(2,1)} %bitcast.3), calls=%async_computation.1 | async-start | bytes 524288 | tf_op jit(solution)/shard_map/all_to_all | solution.py:619
  58.3 11.0 %collective-permute-start.9 = (f32[256,256]{1,0:T(8,128)S(1)}, f32[256,256]{1,0:T(8,128)}, u32[]{:S(2)}, u32[]{:S(2)}) collective-permute-start(f32[256,256]{1,0:T(8,128)S(1)} %get-tuple-element.60), channel_id=1, source_target_pairs={{0,64},{64,0},{1,65},{65,1},{2,66},{66,2},{3,67},{67,3},{4,68},{68... | collective-permute-start | bytes 786440 | tf_op jit(solution)/shard_map/ppermute | solution.py:25
  59.1 0.8 copy-start.1
  63.4 16.3 %copy-start = (bf16[512,1024]{1,0:T(8,128)(2,1)S(1)}, bf16[512,1024]{1,0:T(8,128)(2,1)}, u32[]{:S(2)}) copy-start(bf16[512,1024]{1,0:T(8,128)(2,1)} %refs_4_.1) | copy-start | bytes 3145732
  63.4 1.1 copy-start.12
  64.5 0.7 copy-start.17
  66.9 0.7 copy-start.13
  68.9 10.8 %copy-start.14 = (bf16[64,16,128]{2,1,0:T(8,128)(2,1)S(1)}, bf16[64,16,128]{2,1,0:T(8,128)(2,1)}, u32[]{:S(2)}) copy-start(bf16[64,16,128]{2,1,0:T(8,128)(2,1)} %copy-done.13) | copy-start | bytes 786436
  69.2 1.6 %collective-permute-start.8 = (f32[256,256]{1,0:T(8,128)S(1)}, f32[256,256]{1,0:T(8,128)S(1)}, u32[]{:S(2)}, u32[]{:S(2)}) collective-permute-start(f32[256,256]{1,0:T(8,128)S(1)} %rows.1.refs_0_), channel_id=1, source_target_pairs={{0,64},{64,0},{1,65},{65,1},{2,66},{66,2},{3,67},{67,3},{4,68},{68... | collective-permute-start | bytes 786440 | tf_op jit(solution)/shard_map/ppermute | solution.py:25
  70.8 8.5 %collective-permute-start.10 = (bf16[256,256]{1,0:T(8,128)(2,1)S(1)}, bf16[256,256]{1,0:T(8,128)(2,1)S(1)}, u32[]{:S(2)}, u32[]{:S(2)}) collective-permute-start(bf16[256,256]{1,0:T(8,128)(2,1)S(1)} %row_grad.1.refs_5_.refs_0_.refs_2_), channel_id=1, source_target_pairs={{0,1},{1,0},{2,3},{3,2},{16,17},{17,16},{18,19},{19,18},{32,33},{3... | collective-permute-start | bytes 393224 | tf_op jit(solution)/shard_map/ppermute | solution.py:40
  71.5 8.2 %collective-permute-start.11 = (bf16[256,256]{1,0:T(8,128)(2,1)S(1)}, bf16[256,256]{1,0:T(8,128)(2,1)S(1)}, u32[]{:S(2)}, u32[]{:S(2)}) collective-permute-start(bf16[256,256]{1,0:T(8,128)(2,1)S(1)} %row_grad.1.refs_5_.refs_0_.refs_2_), channel_id=1, source_target_pairs={{0,16},{1,17},{2,18},{3,19},{16,0},{17,1},{18,2},{19,3},{32,48},{3... | collective-permute-start | bytes 393224 | tf_op jit(solution)/shard_map/ppermute | solution.py:40
  72.9 6.8 %collective-permute-start.12 = (bf16[256,256]{1,0:T(8,128)(2,1)S(1)}, bf16[256,256]{1,0:T(8,128)(2,1)S(1)}, u32[]{:S(2)}, u32[]{:S(2)}) collective-permute-start(bf16[256,256]{1,0:T(8,128)(2,1)S(1)} %row_grad.1.refs_5_.refs_0_.refs_2_), channel_id=1, source_target_pairs={{0,17},{1,16},{2,19},{3,18},{16,1},{17,0},{18,3},{19,2},{32,49},{3... | collective-permute-start | bytes 393224 | tf_op jit(solution)/shard_map/ppermute | solution.py:40
  74.4 1.1 copy-start.2
  75.5 1.2 %copy-start.10 = (bf16[1024,512]{1,0:T(8,128)(2,1)S(1)}, bf16[1024,512]{1,0:T(8,128)(2,1)}, u32[]{:S(2)}) copy-start(bf16[1024,512]{1,0:T(8,128)(2,1)} %get-tuple-element.61.refs_4_) | copy-start | bytes 3145732
  79.7 1.0 copy-start.3
  85.4 34.1 %all-to-all-start.2 = ((bf16[64,16,768]{2,1,0:T(8,128)(2,1)}), bf16[64,16,768]{2,1,0:T(8,128)(2,1)S(1)}, u32[]{:S(2)}, u32[]{:S(2)}) async-start(bf16[64,16,768]{2,1,0:T(8,128)(2,1)} %weight_parts.1.refs_6_.refs_2_), calls=%async_computation.2 | async-start | bytes 3145728 | tf_op jit(solution)/shard_map/all_to_all | solution.py:692
  95.6 5.1 %copy-start.4 = (bf16[1024,256]{1,0:T(8,128)(2,1)S(1)}, bf16[1024,256]{1,0:T(8,128)(2,1)}, u32[]{:S(2)}) copy-start(bf16[1024,256]{1,0:T(8,128)(2,1)} %refs_3_.3) | copy-start | bytes 1572868
  95.6 5.1 %copy-start.19 = (s32[2,1,4]{2,1,0:T(1,128)S(1)}, s32[2,1,4]{2,1,0:T(1,128)}, u32[]{:S(2)}) copy-start(s32[2,1,4]{2,1,0:T(1,128)} %refs_0_.8) | copy-start | bytes 100
  108.5 7.4 %collective-permute-start.13 = (f32[256,1024]{1,0:T(8,128)S(1)}, f32[256,1024]{1,0:T(8,128)S(1)}, u32[]{:S(2)}, u32[]{:S(2)}) collective-permute-start(f32[256,1024]{1,0:T(8,128)S(1)} %get-tuple-element.72.refs_2_), channel_id=1, source_target_pairs={{0,64},{64,0},{1,65},{65,1},{2,66},{66,2},{3,67},{67,3},{4,68},{68... | collective-permute-start | bytes 3145736 | tf_op jit(solution)/shard_map/ppermute | solution.py:25
  108.6 7.4 %copy-start.6 = (bf16[2,128,1024]{2,1,0:T(8,128)(2,1)S(1)}, bf16[2,128,1024]{2,1,0:T(8,128)(2,1)}, u32[]{:S(2)}) copy-start(bf16[2,128,1024]{2,1,0:T(8,128)(2,1)} %refs_0_.9) | copy-start | bytes 1572868

commit v6 on v5

--- a/solution.py
+++ b/solution.py
@@ -12,6 +12,7 @@
 SEQ_MOST = 64
 SEQS = 4
 CAP = 4
+PARTS = 2
 eps = 1e-05
 DEV = ("y", "z", "x")
 f32 = jnp.float32
@@ -25,9 +26,9 @@
     return lax.ppermute(part, "section", [(0, 1), (1, 0)])
 
 
-def shifted(part, axis, step):
+def from_pair(part, axis):
     count = lax.axis_size(axis)
-    return lax.ppermute(part, axis, [(i, (i + step) % count) for i in range(count)])
+    return lax.ppermute(part, axis, [(i, i ^ 1) for i in range(count)])
 
 
 def member():
@@ -185,7 +186,7 @@
     quarter = half // group
     piece = own // group
     base = lax.axis_index("section") * half
-    me = lax.axis_index("z")
+    me = lax.rem(lax.axis_index("z"), 2)
     peak, mass = joined(mine_ref, other_ref)
     target = mark_ref[:, 0:1].astype(jnp.int32) - base
     total = 0.0
@@ -208,11 +209,10 @@
 
 def table_kernel(owners, *refs):
     *in_refs, out_ref = refs
-    quarter = in_refs[0].shape[1] - 256
-    total = sum(dot(r[:, :quarter], r[:, quarter:], TN) for r in in_refs)
-    left = total[:, :128].reshape(owners, -1, 128)
-    right = total[:, 128:].reshape(owners, -1, 128)
-    out_ref[...] = jnp.concatenate([left, right], axis=1).astype(bf16)
+    width = out_ref.shape[2]
+    part = in_refs[0].shape[1] - width
+    total = sum(dot(r[:, :part], r[:, part:], TN) for r in in_refs)
+    out_ref[...] = total.reshape(owners, -1, width).astype(bf16)
 
 
 def masked_product(code_ref, left_ref, width, book_ref, out_ref, dims, group, ready):
@@ -545,13 +545,11 @@
         for t in range(4):
             expand_ref[:, t, head] = total[:, t * HEAD_DIM : (t + 1) * HEAD_DIM]
         mixing_ref[:, head] = total[:, cols:]
-    lanes = pl.ds(cols + HEAD_DIM, HEAD_DIM)
-    for q in side:
-        sources = [(y * group + q) * group + x for y in side for x in side]
+    lanes = pl.ds(cols + HEAD_DIM, table_ref.shape[1])
+    for q in range(PARTS):
+        sources = [(y * group + z) * group + x for y in side for z in side for x in side if z % PARTS == q]
         total = sum(in_ref[i, :, lanes].astype(f32) for i in sources)
-        half = total.shape[0] // 2
-        table_ref[q * half : (q + 1) * half, :HEAD_DIM] = total[:half]
-        table_ref[q * half : (q + 1) * half, HEAD_DIM:] = total[half:]
+        table_ref[q * total.shape[0] : (q + 1) * total.shape[0], :] = total
 
 
 def body(
@@ -587,7 +585,7 @@
     got = lax.all_to_all(sent.reshape(owners, slots // owners, -1), DEV, 0, 0, tiled=True).reshape(slots, -1)
 
     normed, logits, stats, table = call(
-        functools.partial(first_kernel, group, owners),
+        functools.partial(first_kernel, PARTS, owners),
         "norms_and_logits",
         [
             ((total + 16, model_width), bf16),
@@ -602,15 +600,15 @@
     )
     normed_all = [normed] + [from_member(normed, s) for s in range(1, group)]
     row_top, *top_grads, top_token = call(
-        functools.partial(top_grad_kernel, group, own),
+        functools.partial(top_grad_kernel, PARTS, own),
         "top_grads",
-        [((total, width), f32)] + [((total, half_clusters // group + width), bf16)] * group,
+        [((total, width), f32)] + [((total, half_clusters // PARTS + width), bf16)] * PARTS,
         (logits, stats, swap(stats), marks, table, saved),
-        "VVVHHH " + "H" * (1 + group),
+        "VVVHHH " + "H" * (1 + PARTS),
         limit=40,
         token=True,
     )
-    top_all = [top_grads[0]] + [shifted(top_grads[s], "z", s) for s in range(1, group)]
+    top_all = [top_grads[0], from_pair(top_grads[1], "z")]
 
     leaf, leaf_stats, got_held, book_held = leaf_scores(got, codebook, (top_token, normed[:8, :128]))
     back, leaf_grad = leaf_back(
@@ -637,9 +635,9 @@
     table_part, table_token = call(
         functools.partial(table_kernel, owners),
         "table_part",
-        [((owners, 16, 128), bf16)],
+        [((owners, own // PARTS, width), bf16)],
         top_all,
-        "V" * group + " V",
+        "V" * PARTS + " V",
         limit=16,
         after=(back, head_token),
         token=True,
@@ -684,7 +682,7 @@
     (packed,) = call(
         functools.partial(weights_kernel, group, owners),
         "weight_parts",
-        [((owners, model_width // owners, cols + 2 * HEAD_DIM), bf16)],
+        [((owners, model_width // owners, cols + HEAD_DIM + width), bf16)],
         (*row_all, *normed_all, *group_forward, projection, mixing_weight, table_part),
         "V" * (2 * group + 10) + " H",
         limit=28,
@@ -699,7 +697,7 @@
         [((total, model_width), bf16), ((total, model_width), f32)],
         (lengths, normed, row_grad, projection, mixing_weight, weight),
         "SHHHHR VV",
-        limit=48,
+        limit=28,
         scratch=[pltpu.VMEM((4, total, cols), bf16), pltpu.VMEM(weight.shape, bf16), pltpu.SemaphoreType.DMA((4,))],
         after=(packed,),
     )

time: 121 us -> 123 us (1.017)
  waiting for transfers between devices: 4.18 us -> 13.8 us
  local copies, waits for them, and re-layouts: 18.5 us -> 13.9 us
  starting transfers between devices: 43.2 us -> 40.5 us
    all_to_all x1, waiting for transfers between devices: 2.03 us -> 8.39 us  [body(): arrived = lax.all_to_all(packed, DEV, 0, 0, tiled=True)]
    ppermute x3 -> x1, starting transfers between devices: 5.77 us -> 1.58 us  [from_pair(): return lax.ppermute(part, axis, [(i, i ^ 1) for i in range(count)])]
    unnamed x44, local copies, waits for them, and re-layouts: 13.4 us -> 10.8 us
    all_to_all x1, starting transfers between devices: 7.99 us -> 10.4 us  [body(): lax.all_to_all(back.reshape(owners, slots // owners, width), DEV, 0, 0, t...]
    optimization_barrier x1, local copies, waits for them, and re-layouts: 5.09 us -> 3.09 us  [body(): late_weight, _ = lax.optimization_barrier((expand_weight, packed))]
    ppermute x5, waiting for transfers between devices: 0.53 us -> 1.97 us  [swap(): return lax.ppermute(part, 'section', [(0, 1), (1, 0)])]
  transfers between devices with their start and end apart: 17 -> 15, of which waited for: 4 -> 5; matrix products, arithmetic and copies ran while one was open for 6% -> 4% of each run, Pallas kernels for 36% -> 35%
where the time goes in v6:
time: 123 us; the launch traced here: 122 us
  Pallas kernels  50.9 us (41%)
  starting transfers between devices  40.5 us (33%)
  local copies, waits for them, and re-layouts  13.9 us (11%)
  waiting for transfers between devices  13.8 us (11%)
  other arithmetic  1.65 us (1%)
    pallas_call x15, Pallas kernels, call(): pl.pallas_call(run, in_specs=[pl.BlockSpec(memory_space=spaces[k]) for k...  50.9 us
    all_to_all x1, starting transfers between devices, body(): lax.all_to_all(sent.reshape(owners, slots // owners, -1), DEV, 0, 0, tile...  11.5 us
    unnamed x44, local copies, waits for them, and re-layouts  10.8 us
    all_to_all x1, starting transfers between devices, body(): lax.all_to_all(back.reshape(owners, slots // owners, width), DEV, 0, 0, t...  10.4 us
    all_to_all x1, starting transfers between devices, body(): arrived = lax.all_to_all(packed, DEV, 0, 0, tiled=True)  9.3 us
    all_to_all x1, waiting for transfers between devices, body(): arrived = lax.all_to_all(packed, DEV, 0, 0, tiled=True)  8.39 us
    ppermute x6, starting transfers between devices, from_member(): lax.ppermute(part, ('y', 'x'), [(i, i ^ flip) for i in range(lax.axis_siz...  7.14 us
    optimization_barrier x1, local copies, waits for them, and re-layouts, body(): late_weight, _ = lax.optimization_barrier((expand_weight, packed))  3.09 us
  transfers between devices with their start and end apart: 15, of which 5 were waited for; matrix products, arithmetic and copies ran while one was open for 4% of the time, Pallas kernels for 35%

profile of v6, /device:TPU:0, one launch (start us, length us, event | category | flops | bytes accessed | tf_op | source)
XLA Modules:
  0.0 122.0 jit_solution(16953474177736514176)
XLA Ops:
  0.6 2.8 %dispatch.1 = (bf16[512,384]{1,0:T(8,128)(2,1)}, s32[2,128]{1,0:T(2,128)}, f32[256,128]{1,0:T(8,128)}) custom-call(s32[2,128]{1,0:T(2,128)} %refs_0_.5, s32[2,128]{1,0:T(2,128)} %refs_1_.3, bf16[2,128,256]{2,1,0:T(8,128)(2,1)} %refs_2_.1), custom_call_target="tpu_custom_call" | custom-call | tf_op jit(solution)/shard_map/dispatch/pallas_call | solution.py:106
  3.5 11.5 %all-to-all-start = ((bf16[64,8,384]{2,1,0:T(8,128)(2,1)}), bf16[64,8,384]{2,1,0:T(8,128)(2,1)S(1)}, u32[]{:S(2)}, u32[]{:S(2)}) async-start(bf16[64,8,384]{2,1,0:T(8,128)(2,1)} %bitcast.14), calls=%async_computation | async-start | bytes 786432 | tf_op jit(solution)/shard_map/all_to_all | solution.py:585
  15.0 1.0 copy-done.5
  16.1 0.9 copy-done.8
  17.0 1.2 %copy-done.9 = bf16[2048,256]{1,0:T(8,128)(2,1)S(1)} copy-done((bf16[2048,256]{1,0:T(8,128)(2,1)S(1)}, bf16[2048,256]{1,0:T(8,128)(2,1)}, u32[]{:S(2)}) %copy-start.9) | copy-done | bytes 1048600
  18.2 0.7 copy-done.18
  18.9 0.6 copy-done.20
  19.5 1.8 %norms_and_logits.1 = (bf16[272,1024]{1,0:T(8,128)(2,1)S(1)}, f32[256,2048]{1,0:T(8,128)S(1)}, f32[256,128]{1,0:T(8,128)S(1)}, bf16[2048,256]{1,0:T(8,128)(2,1)S(1)}) custom-call(s32[2,1,4]{2,1,0:T(1,128)S(1)} %copy-done.18, bf16[2,128,1024]{2,1,0:T(8,128)(2,1)S(1)} %copy-done.5, bf16[256,256]{1,0:T(8,128)(2,1)S(1)} %bitcast.12, ...), custom_call_target="tpu_custom_call" | custom-call | tf_op jit(solution)/shard_map/norms_and_logits/pallas_call | solution.py:106
  21.3 0.1 collective-permute-start
  21.4 2.6 %collective-permute-start.5 = (bf16[272,1024]{1,0:T(8,128)(2,1)S(1)}, bf16[272,1024]{1,0:T(8,128)(2,1)S(1)}, u32[]{:S(2)}, u32[]{:S(2)}) collective-permute-start(bf16[272,1024]{1,0:T(8,128)(2,1)S(1)} %get-tuple-element.40.refs_0_.refs_4_.refs_1_), channel_id=1, source_target_pairs={{0,17},{1,16},{2,19},{3,18},{16,1},{17,0},{18,3},{19,2},{32,49},{3... | collective-permute-start | bytes 1671176 | tf_op jit(solution)/shard_map/ppermute | solution.py:41
  24.0 0.5 collective-permute-start.4
  24.5 0.4 collective-permute-start.3
  25.0 0.9 copy-done.16
  25.9 2.5 %top_grads.1 = (f32[256,256]{1,0:T(8,128)}, bf16[256,1280]{1,0:T(8,128)(2,1)S(1)}, bf16[256,1280]{1,0:T(8,128)(2,1)}, f32[8,128]{1,0:T(8,128)S(1)}) custom-call(f32[256,2048]{1,0:T(8,128)S(1)} %get-tuple-element.42.refs_0_, f32[256,128]{1,0:T(8,128)S(1)} %get-tuple-element.43.refs_1_, f32[256,128]{1,0:T(8,128)S(1)} %collective-permute-done.refs_2_, ...), custom_call_target="tpu_custom_call" | custom-call | tf_op jit(solution)/shard_map/top_grads/pallas_call | solution.py:106
  28.5 0.8 copy-done.11
  29.3 1.6 %collective-permute-start.2 = (bf16[256,1280]{1,0:T(8,128)(2,1)}, bf16[256,1280]{1,0:T(8,128)(2,1)}, u32[]{:S(2)}, u32[]{:S(2)}) collective-permute-start(bf16[256,1280]{1,0:T(8,128)(2,1)} %get-tuple-element.53), channel_id=1, source_target_pairs={{0,4},{4,0},{8,12},{12,8},{1,5},{5,1},{9,13},{13,9},{2,6},{6,2},{1... | collective-permute-start | bytes 1966088 | tf_op jit(solution)/shard_map/ppermute | solution.py:31
  30.9 7.5 %leaf_scores.1 = (f32[512,256]{1,0:T(8,128)S(1)}, f32[512,128]{1,0:T(8,128)S(1)}, bf16[512,384]{1,0:T(8,128)(2,1)S(1)}, bf16[64,256,256]{2,1,0:T(8,128)(2,1)S(1)}) custom-call(bf16[512,384]{1,0:T(8,128)(2,1)S(1)} %bitcast.10, bf16[64,256,256]{2,1,0:T(8,128)(2,1)} %refs_1_.5, f32[8,128]{1,0:T(8,128)S(1)} %get-tuple-element.46.refs_2_, ...), custom_call_target="tpu_custom_call" | custom-call | flops 4294967296 | tf_op jit(solution)/shard_map/leaf_scores/pallas_call | solution.py:106
  38.5 0.1 collective-permute-start.1
  38.5 1.5 %collective-permute-done.1.refs_3_ = f32[512,128]{1,0:T(8,128)S(1)} collective-permute-done((f32[512,128]{1,0:T(8,128)S(1)}, f32[512,128]{1,0:T(8,128)S(1)}, u32[]{:S(2)}, u32[]{:S(2)}) %collective-permute-start.1) | collective-permute-done | bytes 262176 | tf_op jit(solution)/shard_map/ppermute | solution.py:26
  40.1 6.4 %leaf_back.1 = (bf16[512,256]{1,0:T(8,128)(2,1)}, bf16[512,256]{1,0:T(8,128)(2,1)S(1)}) custom-call(bf16[512,384]{1,0:T(8,128)(2,1)S(1)} %get-tuple-element.47.refs_0_, f32[512,256]{1,0:T(8,128)S(1)} %get-tuple-element.48.refs_1_, f32[512,128]{1,0:T(8,128)S(1)} %get-tuple-element.49.refs_2_, f32[512,128]{1,0:T(8,128)S(1)} %collective-permute-done.1.refs_3_, ...), custom_call_target="tpu_custom_call" | custom-call | tf_op jit(solution)/shard_map/leaf_back/pallas_call | solution.py:106
  46.5 0.7 copy-done.15
  47.2 10.4 %all-to-all-start.1 = ((bf16[64,8,256]{2,1,0:T(8,128)(2,1)}), bf16[64,8,256]{2,1,0:T(8,128)(2,1)}, u32[]{:S(2)}, u32[]{:S(2)}) async-start(bf16[64,8,256]{2,1,0:T(8,128)(2,1)} %bitcast.3), calls=%async_computation.1 | async-start | bytes 524288 | tf_op jit(solution)/shard_map/all_to_all | solution.py:617
  57.5 0.3 collective-permute-start.7
  57.9 0.6 slice_add_fusion.refs_2_
  58.4 3.5 %head_weight.1 = (bf16[1024,512]{1,0:T(8,128)(2,1)}, f32[8,128]{1,0:T(8,128)}) custom-call(bf16[1024,4,512]{2,1,0:T(4,128)(2,1)} %refs_0_.7, bf16[512,256]{1,0:T(8,128)(2,1)} %get-tuple-element.51.refs_1_.refs_2_, bf16[8,128]{1,0:T(8,128)(2,1)} %slice_add_fusion.refs_2_), custom_call_target="tpu_custom_call" | custom-call | tf_op jit(solution)/shard_map/head_weight/pallas_call | solution.py:106
  61.9 1.2 copy-done.12
  63.1 0.7 copy-done.17
  63.8 1.6 %table_part.1 = (bf16[64,16,256]{2,1,0:T(8,128)(2,1)S(1)}, f32[8,128]{1,0:T(8,128)S(1)}) custom-call(bf16[256,1280]{1,0:T(8,128)(2,1)S(1)} %copy-done.12, bf16[256,1280]{1,0:T(8,128)(2,1)} %collective-permute-done.2.refs_1_, bf16[512,256]{1,0:T(8,128)(2,1)} %get-tuple-element.51.refs_1_.refs_2_, f32[8,128]{1,0:T(8,128)S(1)} %copy-done.17), custom_call_target="tpu_custom_call" | custom-call | tf_op jit(solution)/shard_map/table_part/pallas_call | solution.py:106
  65.4 0.8 copy-done.13
  66.2 2.1 %all-to-all-done.1 = bf16[64,8,256]{2,1,0:T(8,128)(2,1)} async-done(((bf16[64,8,256]{2,1,0:T(8,128)(2,1)}), bf16[64,8,256]{2,1,0:T(8,128)(2,1)}, u32[]{:S(2)}, u32[]{:S(2)}) %all-to-all-start.1) | async-done | bytes 262176 | tf_op jit(solution)/shard_map/all_to_all | solution.py:617
  68.3 1.3 %rows.1.refs_0_ = f32[256,256]{1,0:T(8,128)S(1)} custom-call(s32[2,128]{1,0:T(2,128)S(1)} %copy-done.21, bf16[512,256]{1,0:T(8,128)(2,1)} %bitcast.4.refs_1_, f32[8,128]{1,0:T(8,128)S(1)} %get-tuple-element.55.refs_2_), custom_call_target="tpu_custom_call" | custom-call | tf_op jit(solution)/shard_map/rows/pallas_call | solution.py:106
  69.6 0.1 collective-permute-start.6
  69.7 1.1 add.11.refs_2_
  70.8 0.4 collective-permute-done.6.refs_1_
  71.3 0.7 collective-permute-start.8
  72.0 0.5 collective-permute-start.9
  72.4 2.4 %collective-permute-start.10 = (bf16[256,256]{1,0:T(8,128)(2,1)S(1)}, bf16[256,256]{1,0:T(8,128)(2,1)S(1)}, u32[]{:S(2)}, u32[]{:S(2)}) collective-permute-start(bf16[256,256]{1,0:T(8,128)(2,1)S(1)} %row_grad.1.refs_5_.refs_0_.refs_2_), channel_id=1, source_target_pairs={{0,17},{1,16},{2,19},{3,18},{16,1},{17,0},{18,3},{19,2},{32,49},{3... | collective-permute-start | bytes 393224 | tf_op jit(solution)/shard_map/ppermute | solution.py:41
  74.9 1.2 %copy-done.10 = bf16[1024,512]{1,0:T(8,128)(2,1)S(1)} copy-done((bf16[1024,512]{1,0:T(8,128)(2,1)S(1)}, bf16[1024,512]{1,0:T(8,128)(2,1)}, u32[]{:S(2)}) %copy-start.10) | copy-done | bytes 1048600
  76.1 2.6 %group_forward.1 = (bf16[1024,512]{1,0:T(8,128)(2,1)S(1)}, f32[1024,512]{1,0:T(8,128)S(1)}, bf16[1024,128]{1,0:T(8,128)(2,1)S(1)}, f32[1024,128]{1,0:T(8,128)S(1...) custom-call(bf16[272,1024]{1,0:T(8,128)(2,1)S(1)} %get-tuple-element.40.refs_0_.refs_4_.refs_1_, ...), custom_call_target="tpu_custom_call" | custom-call | tf_op jit(solution)/shard_map/group_forward/pallas_call | solution.py:106
  78.7 1.3 %collective-permute-done.9.refs_2_ = bf16[256,256]{1,0:T(8,128)(2,1)S(1)} collective-permute-done((bf16[256,256]{1,0:T(8,128)(2,1)S(1)}, bf16[256,256]{1,0:T(8,128)(2,1)S(1)}, u32[]{:S(2)}, u32[]{:S(2)}) %collective-permute-start.9) | collective-permute-done | bytes 131104 | tf_op jit(solution)/shard_map/ppermute | solution.py:41
  80.1 4.8 %weight_parts.1.refs_6_.refs_2_ = bf16[64,16,896]{2,1,0:T(8,128)(2,1)} custom-call(bf16[256,256]{1,0:T(8,128)(2,1)S(1)} %row_grad.1.refs_5_.refs_0_.refs_2_, bf16[256,256]{1,0:T(8,128)(2,1)S(1)} %collective-permute-done.8.refs_1_, bf16[256,256]{1,0:T(8,128)(2,1)S(1)} %collective-permute-done.9.refs_2_, bf16[256,256]{1,0:T(8,128)(2,1)S(1)} %collective-permute-done.10.refs_3_, ...), custom_call_target="tpu_custom_call" | custom-call | tf_op jit(solution)/shard_map/weight_parts/pallas_call | solution.py:106
  84.9 9.3 %all-to-all-start.2 = ((bf16[64,16,896]{2,1,0:T(8,128)(2,1)}), bf16[64,16,896]{2,1,0:T(8,128)(2,1)S(1)}, u32[]{:S(2)}, u32[]{:S(2)}) async-start(bf16[64,16,896]{2,1,0:T(8,128)(2,1)} %weight_parts.1.refs_6_.refs_2_), calls=%async_computation.2 | async-start | bytes 3670016 | tf_op jit(solution)/shard_map/all_to_all | solution.py:690
  94.2 3.1 %copy.17 = bf16[1024,4,512]{2,0,1:T(8,128)(2,1)S(1)} copy(bf16[1024,4,512]{2,1,0:T(4,128)(2,1)} %refs_0_.7) | data formatting | bytes 8388608 | tf_op jit(solution)/shard_map/optimization_barrier | solution.py:692
  97.3 6.2 %trunk.1 = (bf16[256,1024]{1,0:T(8,128)(2,1)S(1)}, f32[256,1024]{1,0:T(8,128)S(1)}) custom-call(s32[2,1,4]{2,1,0:T(1,128)S(1)} %copy-done.19, bf16[272,1024]{1,0:T(8,128)(2,1)S(1)} %get-tuple-element.40.refs_0_.refs_4_.refs_1_, bf16[256,256]{1,0:T(8,128)(2,1)S(1)} %copy-done.2, bf16[1024,256]{1,0:T(8,128)(2,1)S(1)} %copy-done.4, ...), custom_call_target="tpu_custom_call" | custom-call | tf_op jit(solution)/shard_map/trunk/pallas_call | solution.py:106
  103.7 7.3 %leaf_book.1 = bf16[64,256,256]{2,1,0:T(8,128)(2,1)} custom-call(bf16[512,384]{1,0:T(8,128)(2,1)} %bitcast.11, bf16[512,256]{1,0:T(8,128)(2,1)} %copy-done.15, bf16[64,16,896]{2,1,0:T(8,128)(2,1)} %weight_parts.1.refs_6_.refs_2_), custom_call_target="tpu_custom_call" | custom-call | tf_op jit(solution)/shard_map/leaf_book/pallas_call | solution.py:106
  111.0 1.5 %input_grads.1 = bf16[2,128,1024]{2,1,0:T(8,128)(2,1)} custom-call(bf16[2,128,1024]{2,1,0:T(8,128)(2,1)S(1)} %copy-done.6, bf16[256,1024]{1,0:T(8,128)(2,1)S(1)} %get-tuple-element.67.refs_1_, f32[256,1024]{1,0:T(8,128)S(1)} %get-tuple-element.68.refs_2_, f32[256,1024]{1,0:T(8,128)S(1)} %collective-permute-done.11.refs_3_), custom_call_target="tpu_custom_call" | custom-call | tf_op jit(solution)/shard_map/input_grads/pallas_call | solution.py:106
  112.5 8.4 %all-to-all-done.2.refs_0_ = bf16[64,16,896]{2,1,0:T(8,128)(2,1)S(1)} async-done(((bf16[64,16,896]{2,1,0:T(8,128)(2,1)}), bf16[64,16,896]{2,1,0:T(8,128)(2,1)S(1)}, u32[]{:S(2)}, u32[]{:S(2)}) %all-to-all-start.2) | async-done | bytes 1835040 | tf_op jit(solution)/shard_map/all_to_all | solution.py:690
  120.9 0.9 weight_sums.1
  (45 shorter events, 0.2 us)
Async XLA Ops:
  3.5 27.4 %all-to-all-start = ((bf16[64,8,384]{2,1,0:T(8,128)(2,1)}), bf16[64,8,384]{2,1,0:T(8,128)(2,1)S(1)}, u32[]{:S(2)}, u32[]{:S(2)}) async-start(bf16[64,8,384]{2,1,0:T(8,128)(2,1)} %bitcast.14), calls=%async_computation | async-start | bytes 786432 | tf_op jit(solution)/shard_map/all_to_all | solution.py:585
  15.0 1.0 copy-start.5
  16.0 0.9 copy-start.8
  17.0 1.2 %copy-start.9 = (bf16[2048,256]{1,0:T(8,128)(2,1)S(1)}, bf16[2048,256]{1,0:T(8,128)(2,1)}, u32[]{:S(2)}) copy-start(bf16[2048,256]{1,0:T(8,128)(2,1)} %refs_3_.2) | copy-start | bytes 3145732
  18.2 0.7 copy-start.18
  18.9 0.6 copy-start.20
  21.3 3.7 %collective-permute-start = (f32[256,128]{1,0:T(8,128)S(1)}, f32[256,128]{1,0:T(8,128)S(1)}, u32[]{:S(2)}, u32[]{:S(2)}) collective-permute-start(f32[256,128]{1,0:T(8,128)S(1)} %get-tuple-element.43.refs_1_), channel_id=1, source_target_pairs={{0,64},{64,0},{1,65},{65,1},{2,66},{66,2},{3,67},{67,3},{4,68},{68... | collective-permute-start | bytes 393224 | tf_op jit(solution)/shard_map/ppermute | solution.py:26
  21.4 36.4 %collective-permute-start.5 = (bf16[272,1024]{1,0:T(8,128)(2,1)S(1)}, bf16[272,1024]{1,0:T(8,128)(2,1)S(1)}, u32[]{:S(2)}, u32[]{:S(2)}) collective-permute-start(bf16[272,1024]{1,0:T(8,128)(2,1)S(1)} %get-tuple-element.40.refs_0_.refs_4_.refs_1_), channel_id=1, source_target_pairs={{0,17},{1,16},{2,19},{3,18},{16,1},{17,0},{18,3},{19,2},{32,49},{3... | collective-permute-start | bytes 1671176 | tf_op jit(solution)/shard_map/ppermute | solution.py:41
  24.0 33.8 %collective-permute-start.4 = (bf16[272,1024]{1,0:T(8,128)(2,1)S(1)}, bf16[272,1024]{1,0:T(8,128)(2,1)S(1)}, u32[]{:S(2)}, u32[]{:S(2)}) collective-permute-start(bf16[272,1024]{1,0:T(8,128)(2,1)S(1)} %get-tuple-element.40.refs_0_.refs_4_.refs_1_), channel_id=1, source_target_pairs={{0,16},{1,17},{2,18},{3,19},{16,0},{17,1},{18,2},{19,3},{32,48},{3... | collective-permute-start | bytes 1671176 | tf_op jit(solution)/shard_map/ppermute | solution.py:41
  24.5 33.3 %collective-permute-start.3 = (bf16[272,1024]{1,0:T(8,128)(2,1)S(1)}, bf16[272,1024]{1,0:T(8,128)(2,1)S(1)}, u32[]{:S(2)}, u32[]{:S(2)}) collective-permute-start(bf16[272,1024]{1,0:T(8,128)(2,1)S(1)} %get-tuple-element.40.refs_0_.refs_4_.refs_1_), channel_id=1, source_target_pairs={{0,1},{1,0},{2,3},{3,2},{16,17},{17,16},{18,19},{19,18},{32,33},{3... | collective-permute-start | bytes 1671176 | tf_op jit(solution)/shard_map/ppermute | solution.py:41
  25.0 0.9 copy-start.16
  28.5 0.9 copy-start.11
  29.3 32.6 %collective-permute-start.2 = (bf16[256,1280]{1,0:T(8,128)(2,1)}, bf16[256,1280]{1,0:T(8,128)(2,1)}, u32[]{:S(2)}, u32[]{:S(2)}) collective-permute-start(bf16[256,1280]{1,0:T(8,128)(2,1)} %get-tuple-element.53), channel_id=1, source_target_pairs={{0,4},{4,0},{8,12},{12,8},{1,5},{5,1},{9,13},{13,9},{2,6},{6,2},{1... | collective-permute-start | bytes 1966088 | tf_op jit(solution)/shard_map/ppermute | solution.py:31
  30.9 7.6 %copy-start.7 = (bf16[64,8,384]{2,1,0:T(8,128)(2,1)}, bf16[64,8,384]{2,1,0:T(8,128)(2,1)S(1)}, u32[]{:S(2)}) copy-start(bf16[64,8,384]{2,1,0:T(8,128)(2,1)S(1)} %all-to-all-done) | copy-start | bytes 1179652
  38.5 1.6 %collective-permute-start.1 = (f32[512,128]{1,0:T(8,128)S(1)}, f32[512,128]{1,0:T(8,128)S(1)}, u32[]{:S(2)}, u32[]{:S(2)}) collective-permute-start(f32[512,128]{1,0:T(8,128)S(1)} %get-tuple-element.49.refs_2_), channel_id=1, source_target_pairs={{0,64},{64,0},{1,65},{65,1},{2,66},{66,2},{3,67},{67,3},{4,68},{68... | collective-permute-start | bytes 786440 | tf_op jit(solution)/shard_map/ppermute | solution.py:26
  46.4 0.7 copy-start.15
  47.2 21.1 %copy-start.21 = (s32[2,128]{1,0:T(2,128)S(1)}, s32[2,128]{1,0:T(2,128)}, u32[]{:S(2)}) copy-start(s32[2,128]{1,0:T(2,128)} %get-tuple-element.39.refs_4_.refs_0_) | copy-start | bytes 3076
  47.2 21.1 %all-to-all-start.1 = ((bf16[64,8,256]{2,1,0:T(8,128)(2,1)}), bf16[64,8,256]{2,1,0:T(8,128)(2,1)}, u32[]{:S(2)}, u32[]{:S(2)}) async-start(bf16[64,8,256]{2,1,0:T(8,128)(2,1)} %bitcast.3), calls=%async_computation.1 | async-start | bytes 524288 | tf_op jit(solution)/shard_map/all_to_all | solution.py:617
  57.5 12.2 %collective-permute-start.7 = (f32[256,256]{1,0:T(8,128)}, f32[256,256]{1,0:T(8,128)}, u32[]{:S(2)}, u32[]{:S(2)}) collective-permute-start(f32[256,256]{1,0:T(8,128)} %get-tuple-element.56), channel_id=1, source_target_pairs={{0,64},{64,0},{1,65},{65,1},{2,66},{66,2},{3,67},{67,3},{4,68},{68... | collective-permute-start | bytes 786440 | tf_op jit(solution)/shard_map/ppermute | solution.py:26
  61.9 18.1 %copy-start = (bf16[512,1024]{1,0:T(8,128)(2,1)S(1)}, bf16[512,1024]{1,0:T(8,128)(2,1)}, u32[]{:S(2)}) copy-start(bf16[512,1024]{1,0:T(8,128)(2,1)} %refs_4_.1) | copy-start | bytes 3145732
  61.9 1.2 copy-start.12
  63.1 0.7 copy-start.17
  65.4 0.8 copy-start.13
  68.3 11.8 %copy-start.3 = (bf16[1024,256]{1,0:T(8,128)(2,1)S(1)}, bf16[1024,256]{1,0:T(8,128)(2,1)}, u32[]{:S(2)}) copy-start(bf16[1024,256]{1,0:T(8,128)(2,1)} %refs_3_.3) | copy-start | bytes 1572868
  68.3 11.8 %copy-start.14 = (bf16[64,16,256]{2,1,0:T(8,128)(2,1)S(1)}, bf16[64,16,256]{2,1,0:T(8,128)(2,1)}, u32[]{:S(2)}) copy-start(bf16[64,16,256]{2,1,0:T(8,128)(2,1)} %copy-done.13) | copy-start | bytes 1572868
  69.6 1.6 %collective-permute-start.6 = (f32[256,256]{1,0:T(8,128)S(1)}, f32[256,256]{1,0:T(8,128)S(1)}, u32[]{:S(2)}, u32[]{:S(2)}) collective-permute-start(f32[256,256]{1,0:T(8,128)S(1)} %rows.1.refs_0_), channel_id=1, source_target_pairs={{0,64},{64,0},{1,65},{65,1},{2,66},{66,2},{3,67},{67,3},{4,68},{68... | collective-permute-start | bytes 786440 | tf_op jit(solution)/shard_map/ppermute | solution.py:26
  71.3 13.6 %copy-start.1 = (bf16[256,256]{1,0:T(8,128)(2,1)}, bf16[256,256]{1,0:T(8,128)(2,1)S(1)}, u32[]{:S(2)}) copy-start(bf16[256,256]{1,0:T(8,128)(2,1)S(1)} %row_grad.1.refs_5_.refs_0_.refs_2_) | copy-start | bytes 393220
  71.3 7.4 %collective-permute-start.8 = (bf16[256,256]{1,0:T(8,128)(2,1)S(1)}, bf16[256,256]{1,0:T(8,128)(2,1)S(1)}, u32[]{:S(2)}, u32[]{:S(2)}) collective-permute-start(bf16[256,256]{1,0:T(8,128)(2,1)S(1)} %row_grad.1.refs_5_.refs_0_.refs_2_), channel_id=1, source_target_pairs={{0,1},{1,0},{2,3},{3,2},{16,17},{17,16},{18,19},{19,18},{32,33},{3... | collective-permute-start | bytes 393224 | tf_op jit(solution)/shard_map/ppermute | solution.py:41
  72.0 8.1 %collective-permute-start.9 = (bf16[256,256]{1,0:T(8,128)(2,1)S(1)}, bf16[256,256]{1,0:T(8,128)(2,1)S(1)}, u32[]{:S(2)}, u32[]{:S(2)}) collective-permute-start(bf16[256,256]{1,0:T(8,128)(2,1)S(1)} %row_grad.1.refs_5_.refs_0_.refs_2_), channel_id=1, source_target_pairs={{0,16},{1,17},{2,18},{3,19},{16,0},{17,1},{18,2},{19,3},{32,48},{3... | collective-permute-start | bytes 393224 | tf_op jit(solution)/shard_map/ppermute | solution.py:41
  72.4 7.6 %collective-permute-start.10 = (bf16[256,256]{1,0:T(8,128)(2,1)S(1)}, bf16[256,256]{1,0:T(8,128)(2,1)S(1)}, u32[]{:S(2)}, u32[]{:S(2)}) collective-permute-start(bf16[256,256]{1,0:T(8,128)(2,1)S(1)} %row_grad.1.refs_5_.refs_0_.refs_2_), channel_id=1, source_target_pairs={{0,17},{1,16},{2,19},{3,18},{16,1},{17,0},{18,3},{19,2},{32,49},{3... | collective-permute-start | bytes 393224 | tf_op jit(solution)/shard_map/ppermute | solution.py:41
  74.9 1.2 %copy-start.10 = (bf16[1024,512]{1,0:T(8,128)(2,1)S(1)}, bf16[1024,512]{1,0:T(8,128)(2,1)}, u32[]{:S(2)}) copy-start(bf16[1024,512]{1,0:T(8,128)(2,1)} %get-tuple-element.57.refs_4_) | copy-start | bytes 3145732
  84.9 36.0 %all-to-all-start.2 = ((bf16[64,16,896]{2,1,0:T(8,128)(2,1)}), bf16[64,16,896]{2,1,0:T(8,128)(2,1)S(1)}, u32[]{:S(2)}, u32[]{:S(2)}) async-start(bf16[64,16,896]{2,1,0:T(8,128)(2,1)} %weight_parts.1.refs_6_.refs_2_), calls=%async_computation.2 | async-start | bytes 3670016 | tf_op jit(solution)/shard_map/all_to_all | solution.py:690
  94.2 3.1 %copy-start.2 = (bf16[256,256]{1,0:T(8,128)(2,1)S(1)}, bf16[256,256]{1,0:T(8,128)(2,1)}, u32[]{:S(2)}) copy-start(bf16[256,256]{1,0:T(8,128)(2,1)} %copy-done.1) | copy-start | bytes 393220
  94.2 3.1 %copy-start.4 = (bf16[1024,256]{1,0:T(8,128)(2,1)S(1)}, bf16[1024,256]{1,0:T(8,128)(2,1)}, u32[]{:S(2)}) copy-start(bf16[1024,256]{1,0:T(8,128)(2,1)} %refs_3_.3) | copy-start | bytes 1572868
  94.2 3.1 %copy-start.19 = (s32[2,1,4]{2,1,0:T(1,128)S(1)}, s32[2,1,4]{2,1,0:T(1,128)}, u32[]{:S(2)}) copy-start(s32[2,1,4]{2,1,0:T(1,128)} %refs_0_.8) | copy-start | bytes 100
  103.5 7.4 %collective-permute-start.11 = (f32[256,1024]{1,0:T(8,128)S(1)}, f32[256,1024]{1,0:T(8,128)S(1)}, u32[]{:S(2)}, u32[]{:S(2)}) collective-permute-start(f32[256,1024]{1,0:T(8,128)S(1)} %get-tuple-element.68.refs_2_), channel_id=1, source_target_pairs={{0,64},{64,0},{1,65},{65,1},{2,66},{66,2},{3,67},{67,3},{4,68},{68... | collective-permute-start | bytes 3145736 | tf_op jit(solution)/shard_map/ppermute | solution.py:26
  103.6 7.4 %copy-start.6 = (bf16[2,128,1024]{2,1,0:T(8,128)(2,1)S(1)}, bf16[2,128,1024]{2,1,0:T(8,128)(2,1)}, u32[]{:S(2)}) copy-start(bf16[2,128,1024]{2,1,0:T(8,128)(2,1)} %refs_0_.9) | copy-start | bytes 1572868

commit v7 on v6

--- a/solution.py
+++ b/solution.py
@@ -26,9 +26,9 @@
     return lax.ppermute(part, "section", [(0, 1), (1, 0)])
 
 
-def from_pair(part, axis):
+def from_pair(part, axis, other):
     count = lax.axis_size(axis)
-    return lax.ppermute(part, axis, [(i, i ^ 1) for i in range(count)])
+    return lax.ppermute(part, axis, [(i, i ^ other) for i in range(count)])
 
 
 def member():
@@ -208,11 +208,18 @@
 
 
 def table_kernel(owners, *refs):
-    *in_refs, out_ref = refs
-    width = out_ref.shape[2]
-    part = in_refs[0].shape[1] - width
+    *in_refs, keep_ref, send_ref = refs
+    lanes = keep_ref.shape[2]
+    part = in_refs[0].shape[1] - 2 * lanes
     total = sum(dot(r[:, :part], r[:, part:], TN) for r in in_refs)
-    out_ref[...] = total.reshape(owners, -1, width).astype(bf16)
+    halves = [total[:, i * lanes : (i + 1) * lanes].reshape(owners, -1, lanes).astype(bf16) for i in range(2)]
+    bit = lax.axis_index("z") // 2
+    for mine in range(2):
+
+        @pl.when(bit == mine)
+        def _(mine=mine):
+            keep_ref[...] = halves[mine]
+            send_ref[...] = halves[1 - mine]
 
 
 def masked_product(code_ref, left_ref, width, book_ref, out_ref, dims, group, ready):
@@ -257,11 +264,12 @@
 
     got_copy = pltpu.make_async_copy(got_in, got_ref, got_sem)
     got_copy.start()
-    for i in range(2):
-        for copy in copies(i):
-            copy.start()
+    for copy in copies(0):
+        copy.start()
     got_copy.wait()
     code_ref[...] = jnp.broadcast_to(got_ref[:, width : width + 1], code_ref.shape)
+    for copy in copies(1):
+        copy.start()
 
     def ready(i):
         for copy in copies(i):
@@ -509,7 +517,7 @@
 
 def weights_kernel(group, owners, *refs):
     row_refs, norm_refs = refs[:group], refs[group : 2 * group]
-    act_ref, slope_ref, att_ref, back_ref, out_ref, inverse_ref, prod_ref, proj_ref, mix_ref, table_ref, packed_ref = refs[2 * group :]
+    act_ref, slope_ref, att_ref, back_ref, out_ref, inverse_ref, prod_ref, proj_ref, mix_ref, *table_refs, packed_ref = refs[2 * group :]
     total = row_refs[0].shape[0]
     rows = att_ref.shape[1]
     cols = act_ref.shape[1]
@@ -525,7 +533,8 @@
             spans.append(pl.ds(s * total + m * rows, rows))
             incoming.append(grad_product[m * rows : (m + 1) * rows])
     packed_ref[:, :, cols : cols + HEAD_DIM] = mixing.reshape(owners, -1, HEAD_DIM).astype(bf16)
-    packed_ref[:, :, cols + HEAD_DIM :] = table_ref[...]
+    table = table_refs[0][...].astype(f32) + table_refs[1][...].astype(f32)
+    packed_ref[:, :, cols + HEAD_DIM :] = table.astype(bf16)
     acts = [[act_ref[lines, t * HEAD_DIM : (t + 1) * HEAD_DIM] for t in range(4)] for lines in spans]
     results = [(att_ref[lines, :], back_ref[lines, :], out_ref[lines, :], inverse_ref[lines, :]) for lines in spans]
     grads = attend_back_all(incoming, acts, results)
@@ -545,11 +554,11 @@
         for t in range(4):
             expand_ref[:, t, head] = total[:, t * HEAD_DIM : (t + 1) * HEAD_DIM]
         mixing_ref[:, head] = total[:, cols:]
-    lanes = pl.ds(cols + HEAD_DIM, table_ref.shape[1])
-    for q in range(PARTS):
-        sources = [(y * group + z) * group + x for y in side for z in side for x in side if z % PARTS == q]
-        total = sum(in_ref[i, :, lanes].astype(f32) for i in sources)
-        table_ref[q * total.shape[0] : (q + 1) * total.shape[0], :] = total
+    width = table_ref.shape[1] // 2
+    for z in side:
+        total = sum(in_ref[(y * group + z) * group + x, :, cols + HEAD_DIM :].astype(f32) for y in side for x in side)
+        part, half, count = z % PARTS, z // PARTS, total.shape[0]
+        table_ref[part * count : (part + 1) * count, half * width : (half + 1) * width] = total
 
 
 def body(
@@ -608,7 +617,7 @@
         limit=40,
         token=True,
     )
-    top_all = [top_grads[0], from_pair(top_grads[1], "z")]
+    top_all = [top_grads[0], from_pair(top_grads[1], "z", 1)]
 
     leaf, leaf_stats, got_held, book_held = leaf_scores(got, codebook, (top_token, normed[:8, :128]))
     back, leaf_grad = leaf_back(
@@ -632,16 +641,18 @@
         token=True,
     )
 
-    table_part, table_token = call(
+    table_keep, table_send, table_token = call(
         functools.partial(table_kernel, owners),
         "table_part",
-        [((owners, own // PARTS, width), bf16)],
+        [((owners, own // PARTS, width // 2), bf16)] * 2,
         top_all,
-        "V" * PARTS + " V",
+        "V" * PARTS + " VV",
         limit=16,
         after=(back, head_token),
         token=True,
     )
+
+    table_other = from_pair(table_send, "z", 2)
 
     (row_part,) = call(
         rows_kernel,
@@ -682,9 +693,9 @@
     (packed,) = call(
         functools.partial(weights_kernel, group, owners),
         "weight_parts",
-        [((owners, model_width // owners, cols + HEAD_DIM + width), bf16)],
-        (*row_all, *normed_all, *group_forward, projection, mixing_weight, table_part),
-        "V" * (2 * group + 10) + " H",
+        [((owners, model_width // owners, cols + HEAD_DIM + width // 2), bf16)],
+        (*row_all, *normed_all, *group_forward, projection, mixing_weight, table_keep, table_other),
+        "V" * (2 * group + 11) + " H",
         limit=28,
     )
     arrived = lax.all_to_all(packed, DEV, 0, 0, tiled=True)

time: 123 us -> 121 us (0.984)
  waiting for transfers between devices: 13.8 us -> 8.21 us
  local copies, waits for them, and re-layouts: 13.9 us -> 17.4 us
  starting transfers between devices: 40.5 us -> 42 us
    unnamed x44 -> x46, local copies, waits for them, and re-layouts: 10.8 us -> 14.3 us
    all_to_all x1, waiting for transfers between devices: 8.39 us -> 5.02 us  [body(): arrived = lax.all_to_all(packed, DEV, 0, 0, tiled=True)]
    ppermute x1 -> x2, starting transfers between devices: 1.58 us -> 4.32 us  [from_pair(): return lax.ppermute(part, axis, [(i, i ^ other) for i in range(count)])]
    all_to_all x1, waiting for transfers between devices: 2.11 us -> 0.8 us  [body(): lax.all_to_all(back.reshape(owners, slots // owners, width), DEV, 0, 0, t...]
  transfers between devices with their start and end apart: 15 -> 16, of which waited for: 5 -> 4; matrix products, arithmetic and copies ran while one was open for 4% -> 4% of each run, Pallas kernels for 35% -> 34%
where the time goes in v7:
time: 121 us; the launch traced here: 120 us
  Pallas kernels  49.9 us (41%)
  starting transfers between devices  42 us (35%)
  local copies, waits for them, and re-layouts  17.4 us (14%)
  waiting for transfers between devices  8.21 us (7%)
  other arithmetic  1.57 us (1%)
    pallas_call x15, Pallas kernels, call(): pl.pallas_call(run, in_specs=[pl.BlockSpec(memory_space=spaces[k]) for k...  49.9 us
    unnamed x46, local copies, waits for them, and re-layouts  14.3 us
    all_to_all x1, starting transfers between devices, body(): lax.all_to_all(sent.reshape(owners, slots // owners, -1), DEV, 0, 0, tile...  11.5 us
    all_to_all x1, starting transfers between devices, body(): lax.all_to_all(back.reshape(owners, slots // owners, width), DEV, 0, 0, t...  10.1 us
    all_to_all x1, starting transfers between devices, body(): arrived = lax.all_to_all(packed, DEV, 0, 0, tiled=True)  8.35 us
    ppermute x6, starting transfers between devices, from_member(): lax.ppermute(part, ('y', 'x'), [(i, i ^ flip) for i in range(lax.axis_siz...  7.14 us
    all_to_all x1, waiting for transfers between devices, body(): arrived = lax.all_to_all(packed, DEV, 0, 0, tiled=True)  5.02 us
    ppermute x2, starting transfers between devices, from_pair(): return lax.ppermute(part, axis, [(i, i ^ other) for i in range(count)])  4.32 us
  transfers between devices with their start and end apart: 16, of which 4 were waited for; matrix products, arithmetic and copies ran while one was open for 4% of the time, Pallas kernels for 34%

profile of v7, /device:TPU:0, one launch (start us, length us, event | category | flops | bytes accessed | tf_op | source)
XLA Modules:
  0.0 120.3 jit_solution(17926170806911665989)
XLA Ops:
  0.6 2.8 %dispatch.1 = (bf16[512,384]{1,0:T(8,128)(2,1)}, s32[2,128]{1,0:T(2,128)}, f32[256,128]{1,0:T(8,128)}) custom-call(s32[2,128]{1,0:T(2,128)} %refs_0_.5, s32[2,128]{1,0:T(2,128)} %refs_1_.3, bf16[2,128,256]{2,1,0:T(8,128)(2,1)} %refs_2_.1), custom_call_target="tpu_custom_call" | custom-call | tf_op jit(solution)/shard_map/dispatch/pallas_call | solution.py:106
  3.5 11.5 %all-to-all-start = ((bf16[64,8,384]{2,1,0:T(8,128)(2,1)}), bf16[64,8,384]{2,1,0:T(8,128)(2,1)S(1)}, u32[]{:S(2)}, u32[]{:S(2)}) async-start(bf16[64,8,384]{2,1,0:T(8,128)(2,1)} %bitcast.15), calls=%async_computation | async-start | bytes 786432 | tf_op jit(solution)/shard_map/all_to_all | solution.py:594
  15.0 1.0 copy-done.5
  16.0 0.9 copy-done.8
  16.9 1.2 %copy-done.9 = bf16[2048,256]{1,0:T(8,128)(2,1)S(1)} copy-done((bf16[2048,256]{1,0:T(8,128)(2,1)S(1)}, bf16[2048,256]{1,0:T(8,128)(2,1)}, u32[]{:S(2)}) %copy-start.9) | copy-done | bytes 1048600
  18.2 0.7 copy-done.18
  18.9 0.6 copy-done.20
  19.5 1.8 %norms_and_logits.1 = (bf16[272,1024]{1,0:T(8,128)(2,1)S(1)}, f32[256,2048]{1,0:T(8,128)S(1)}, f32[256,128]{1,0:T(8,128)S(1)}, bf16[2048,256]{1,0:T(8,128)(2,1)S(1)}) custom-call(s32[2,1,4]{2,1,0:T(1,128)S(1)} %copy-done.18, bf16[2,128,1024]{2,1,0:T(8,128)(2,1)S(1)} %copy-done.5, bf16[256,256]{1,0:T(8,128)(2,1)S(1)} %bitcast.12, ...), custom_call_target="tpu_custom_call" | custom-call | tf_op jit(solution)/shard_map/norms_and_logits/pallas_call | solution.py:106
  21.4 2.6 %collective-permute-start.5 = (bf16[272,1024]{1,0:T(8,128)(2,1)S(1)}, bf16[272,1024]{1,0:T(8,128)(2,1)S(1)}, u32[]{:S(2)}, u32[]{:S(2)}) collective-permute-start(bf16[272,1024]{1,0:T(8,128)(2,1)S(1)} %get-tuple-element.41.refs_0_.refs_4_.refs_1_), channel_id=1, source_target_pairs={{0,17},{1,16},{2,19},{3,18},{16,1},{17,0},{18,3},{19,2},{32,49},{3... | collective-permute-start | bytes 1671176 | tf_op jit(solution)/shard_map/ppermute | solution.py:41
  24.0 0.5 collective-permute-start.4
  24.5 0.4 collective-permute-start.3
  25.0 0.9 copy-done.16
  25.9 2.6 %top_grads.1 = (f32[256,256]{1,0:T(8,128)S(1)}, bf16[256,1280]{1,0:T(8,128)(2,1)S(1)}, bf16[256,1280]{1,0:T(8,128)(2,1)}, f32[8,128]{1,0:T(8,128)S(1)}) custom-call(f32[256,2048]{1,0:T(8,128)S(1)} %get-tuple-element.43.refs_0_, f32[256,128]{1,0:T(8,128)S(1)} %get-tuple-element.44.refs_1_, f32[256,128]{1,0:T(8,128)S(1)} %collective-permute-done.refs_2_, ...), custom_call_target="tpu_custom_call" | custom-call | tf_op jit(solution)/shard_map/top_grads/pallas_call | solution.py:106
  28.5 0.8 copy-done.11
  29.3 1.6 %collective-permute-start.2 = (bf16[256,1280]{1,0:T(8,128)(2,1)}, bf16[256,1280]{1,0:T(8,128)(2,1)}, u32[]{:S(2)}, u32[]{:S(2)}) collective-permute-start(bf16[256,1280]{1,0:T(8,128)(2,1)} %get-tuple-element.54), channel_id=1, source_target_pairs={{0,4},{4,0},{8,12},{12,8},{1,5},{5,1},{9,13},{13,9},{2,6},{6,2},{1... | collective-permute-start | bytes 1966088 | tf_op jit(solution)/shard_map/ppermute | solution.py:31
  30.9 7.5 %leaf_scores.1 = (f32[512,256]{1,0:T(8,128)S(1)}, f32[512,128]{1,0:T(8,128)S(1)}, bf16[512,384]{1,0:T(8,128)(2,1)S(1)}, bf16[64,256,256]{2,1,0:T(8,128)(2,1)S(1)}) custom-call(bf16[512,384]{1,0:T(8,128)(2,1)S(1)} %bitcast.10, bf16[64,256,256]{2,1,0:T(8,128)(2,1)} %refs_1_.5, f32[8,128]{1,0:T(8,128)S(1)} %get-tuple-element.47.refs_2_, ...), custom_call_target="tpu_custom_call" | custom-call | flops 4294967296 | tf_op jit(solution)/shard_map/leaf_scores/pallas_call | solution.py:106
  38.5 1.5 %collective-permute-done.1.refs_3_ = f32[512,128]{1,0:T(8,128)S(1)} collective-permute-done((f32[512,128]{1,0:T(8,128)S(1)}, f32[512,128]{1,0:T(8,128)S(1)}, u32[]{:S(2)}, u32[]{:S(2)}) %collective-permute-start.1) | collective-permute-done | bytes 262176 | tf_op jit(solution)/shard_map/ppermute | solution.py:26
  40.1 6.4 %leaf_back.1 = (bf16[512,256]{1,0:T(8,128)(2,1)}, bf16[512,256]{1,0:T(8,128)(2,1)S(1)}) custom-call(bf16[512,384]{1,0:T(8,128)(2,1)S(1)} %get-tuple-element.48.refs_0_, f32[512,256]{1,0:T(8,128)S(1)} %get-tuple-element.49.refs_1_, f32[512,128]{1,0:T(8,128)S(1)} %get-tuple-element.50.refs_2_, f32[512,128]{1,0:T(8,128)S(1)} %collective-permute-done.1.refs_3_, ...), custom_call_target="tpu_custom_call" | custom-call | tf_op jit(solution)/shard_map/leaf_back/pallas_call | solution.py:106
  46.5 0.7 copy-done.15
  47.1 10.1 %all-to-all-start.1 = ((bf16[64,8,256]{2,1,0:T(8,128)(2,1)}), bf16[64,8,256]{2,1,0:T(8,128)(2,1)S(1)}, u32[]{:S(2)}, u32[]{:S(2)}) async-start(bf16[64,8,256]{2,1,0:T(8,128)(2,1)} %bitcast.3), calls=%async_computation.1 | async-start | bytes 524288 | tf_op jit(solution)/shard_map/all_to_all | solution.py:626
  57.6 0.6 slice_add_fusion.refs_2_
  58.2 0.8 copy-done.1
  59.0 3.5 %head_weight.1 = (bf16[1024,512]{1,0:T(8,128)(2,1)}, f32[8,128]{1,0:T(8,128)}) custom-call(bf16[1024,4,512]{2,1,0:T(4,128)(2,1)} %refs_0_.7, bf16[512,256]{1,0:T(8,128)(2,1)} %get-tuple-element.52.refs_1_.refs_2_, bf16[8,128]{1,0:T(8,128)(2,1)} %slice_add_fusion.refs_2_), custom_call_target="tpu_custom_call" | custom-call | tf_op jit(solution)/shard_map/head_weight/pallas_call | solution.py:106
  62.5 1.2 copy-done.12
  63.7 0.7 copy-done.17
  64.3 1.6 %table_part.1 = (bf16[64,16,128]{2,1,0:T(8,128)(2,1)S(1)}, bf16[64,16,128]{2,1,0:T(8,128)(2,1)S(1)}, f32[8,128]{1,0:T(8,128)S(1)}) custom-call(bf16[256,1280]{1,0:T(8,128)(2,1)S(1)} %copy-done.12, bf16[256,1280]{1,0:T(8,128)(2,1)} %collective-permute-done.2.refs_1_, bf16[512,256]{1,0:T(8,128)(2,1)} %get-tuple-element.52.refs_1_.refs_2_, f32[8,128]{1,0:T(8,128)S(1)} %copy-done.17), custom_call_target="tpu_custom_call" | custom-call | tf_op jit(solution)/shard_map/table_part/pallas_call | solution.py:106
  66.0 0.7 copy-done.13
  66.7 0.7 copy-done.22
  67.4 0.8 all-to-all-done.1
  68.2 0.3 rows.1.refs_0_
  68.6 2.7 %collective-permute-start.11 = (bf16[64,16,128]{2,1,0:T(8,128)(2,1)}, bf16[64,16,128]{2,1,0:T(8,128)(2,1)S(1)}, u32[]{:S(2)}, u32[]{:S(2)}) collective-permute-start(bf16[64,16,128]{2,1,0:T(8,128)(2,1)} %copy-done.22), channel_id=1, source_target_pairs={{0,8},{4,12},{8,0},{12,4},{1,9},{5,13},{9,1},{13,5},{2,10},{6,14},... | collective-permute-start | bytes 786440 | tf_op jit(solution)/shard_map/ppermute | solution.py:31
  71.3 1.0 add.11.refs_2_
  72.4 1.5 %collective-permute-start.8 = (bf16[256,256]{1,0:T(8,128)(2,1)S(1)}, bf16[256,256]{1,0:T(8,128)(2,1)S(1)}, u32[]{:S(2)}, u32[]{:S(2)}) collective-permute-start(bf16[256,256]{1,0:T(8,128)(2,1)S(1)} %row_grad.1.refs_5_.refs_0_.refs_2_), channel_id=1, source_target_pairs={{0,1},{1,0},{2,3},{3,2},{16,17},{17,16},{18,19},{19,18},{32,33},{3... | collective-permute-start | bytes 393224 | tf_op jit(solution)/shard_map/ppermute | solution.py:41
  73.9 1.5 %collective-permute-start.9 = (bf16[256,256]{1,0:T(8,128)(2,1)S(1)}, bf16[256,256]{1,0:T(8,128)(2,1)S(1)}, u32[]{:S(2)}, u32[]{:S(2)}) collective-permute-start(bf16[256,256]{1,0:T(8,128)(2,1)S(1)} %row_grad.1.refs_5_.refs_0_.refs_2_), channel_id=1, source_target_pairs={{0,16},{1,17},{2,18},{3,19},{16,0},{17,1},{18,2},{19,3},{32,48},{3... | collective-permute-start | bytes 393224 | tf_op jit(solution)/shard_map/ppermute | solution.py:41
  75.4 0.5 collective-permute-start.10
  75.9 1.1 copy-done.2
  77.0 1.2 %copy-done.10 = bf16[1024,512]{1,0:T(8,128)(2,1)S(1)} copy-done((bf16[1024,512]{1,0:T(8,128)(2,1)S(1)}, bf16[1024,512]{1,0:T(8,128)(2,1)}, u32[]{:S(2)}) %copy-start.10) | copy-done | bytes 1048600
  78.2 2.6 %group_forward.1 = (bf16[1024,512]{1,0:T(8,128)(2,1)S(1)}, f32[1024,512]{1,0:T(8,128)S(1)}, bf16[1024,128]{1,0:T(8,128)(2,1)S(1)}, f32[1024,128]{1,0:T(8,128)S(1...) custom-call(bf16[272,1024]{1,0:T(8,128)(2,1)S(1)} %get-tuple-element.41.refs_0_.refs_4_.refs_1_, ...), custom_call_target="tpu_custom_call" | custom-call | tf_op jit(solution)/shard_map/group_forward/pallas_call | solution.py:106
  80.9 0.8 collective-permute-done.9.refs_2_
  81.7 1.0 copy-done.3
  82.8 4.7 %weight_parts.1.refs_6_.refs_2_ = bf16[64,16,768]{2,1,0:T(8,128)(2,1)} custom-call(bf16[256,256]{1,0:T(8,128)(2,1)S(1)} %row_grad.1.refs_5_.refs_0_.refs_2_, bf16[256,256]{1,0:T(8,128)(2,1)S(1)} %collective-permute-done.8.refs_1_, bf16[256,256]{1,0:T(8,128)(2,1)S(1)} %collective-permute-done.9.refs_2_, bf16[256,256]{1,0:T(8,128)(2,1)S(1)} %collective-permute-done.10.refs_3_, ...), custom_call_target="tpu_custom_call" | custom-call | tf_op jit(solution)/shard_map/weight_parts/pallas_call | solution.py:106
  87.5 8.3 %all-to-all-start.2 = ((bf16[64,16,768]{2,1,0:T(8,128)(2,1)}), bf16[64,16,768]{2,1,0:T(8,128)(2,1)S(1)}, u32[]{:S(2)}, u32[]{:S(2)}) async-start(bf16[64,16,768]{2,1,0:T(8,128)(2,1)} %weight_parts.1.refs_6_.refs_2_), calls=%async_computation.2 | async-start | bytes 3145728 | tf_op jit(solution)/shard_map/all_to_all | solution.py:701
  95.9 3.1 %copy.17 = bf16[1024,4,512]{2,0,1:T(8,128)(2,1)S(1)} copy(bf16[1024,4,512]{2,1,0:T(4,128)(2,1)} %refs_0_.7) | data formatting | bytes 8388608 | tf_op jit(solution)/shard_map/optimization_barrier | solution.py:703
  99.0 6.2 %trunk.1 = (bf16[256,1024]{1,0:T(8,128)(2,1)S(1)}, f32[256,1024]{1,0:T(8,128)S(1)}) custom-call(s32[2,1,4]{2,1,0:T(1,128)S(1)} %copy-done.19, bf16[272,1024]{1,0:T(8,128)(2,1)S(1)} %get-tuple-element.41.refs_0_.refs_4_.refs_1_, bf16[256,256]{1,0:T(8,128)(2,1)S(1)} %row_grad.1.refs_5_.refs_0_.refs_2_, bf16[1024,256]{1,0:T(8,128)(2,1)S(1)} %copy-done.4, ...), custom_call_target="tpu_custom_call" | custom-call | tf_op jit(solution)/shard_map/trunk/pallas_call | solution.py:106
  105.3 7.3 %leaf_book.1 = bf16[64,256,256]{2,1,0:T(8,128)(2,1)} custom-call(bf16[512,384]{1,0:T(8,128)(2,1)} %bitcast.11, bf16[512,256]{1,0:T(8,128)(2,1)} %copy-done.15, bf16[64,16,768]{2,1,0:T(8,128)(2,1)} %weight_parts.1.refs_6_.refs_2_), custom_call_target="tpu_custom_call" | custom-call | tf_op jit(solution)/shard_map/leaf_book/pallas_call | solution.py:106
  112.7 1.5 %input_grads.1 = bf16[2,128,1024]{2,1,0:T(8,128)(2,1)} custom-call(bf16[2,128,1024]{2,1,0:T(8,128)(2,1)S(1)} %copy-done.6, bf16[256,1024]{1,0:T(8,128)(2,1)S(1)} %get-tuple-element.69.refs_1_, f32[256,1024]{1,0:T(8,128)S(1)} %get-tuple-element.70.refs_2_, f32[256,1024]{1,0:T(8,128)S(1)} %collective-permute-done.12.refs_3_), custom_call_target="tpu_custom_call" | custom-call | tf_op jit(solution)/shard_map/input_grads/pallas_call | solution.py:106
  114.2 5.0 %all-to-all-done.2.refs_0_ = bf16[64,16,768]{2,1,0:T(8,128)(2,1)S(1)} async-done(((bf16[64,16,768]{2,1,0:T(8,128)(2,1)}), bf16[64,16,768]{2,1,0:T(8,128)(2,1)S(1)}, u32[]{:S(2)}, u32[]{:S(2)}) %all-to-all-start.2) | async-done | bytes 1572896 | tf_op jit(solution)/shard_map/all_to_all | solution.py:701
  119.2 0.9 weight_sums.1
  (49 shorter events, 0.7 us)
Async XLA Ops:
  3.5 27.4 %all-to-all-start = ((bf16[64,8,384]{2,1,0:T(8,128)(2,1)}), bf16[64,8,384]{2,1,0:T(8,128)(2,1)S(1)}, u32[]{:S(2)}, u32[]{:S(2)}) async-start(bf16[64,8,384]{2,1,0:T(8,128)(2,1)} %bitcast.15), calls=%async_computation | async-start | bytes 786432 | tf_op jit(solution)/shard_map/all_to_all | solution.py:594
  15.0 1.0 copy-start.5
  16.0 0.9 copy-start.8
  16.9 1.2 %copy-start.9 = (bf16[2048,256]{1,0:T(8,128)(2,1)S(1)}, bf16[2048,256]{1,0:T(8,128)(2,1)}, u32[]{:S(2)}) copy-start(bf16[2048,256]{1,0:T(8,128)(2,1)} %refs_3_.2) | copy-start | bytes 3145732
  18.2 0.7 copy-start.18
  18.9 0.6 copy-start.20
  21.3 3.7 %collective-permute-start = (f32[256,128]{1,0:T(8,128)S(1)}, f32[256,128]{1,0:T(8,128)S(1)}, u32[]{:S(2)}, u32[]{:S(2)}) collective-permute-start(f32[256,128]{1,0:T(8,128)S(1)} %get-tuple-element.44.refs_1_), channel_id=1, source_target_pairs={{0,64},{64,0},{1,65},{65,1},{2,66},{66,2},{3,67},{67,3},{4,68},{68... | collective-permute-start | bytes 393224 | tf_op jit(solution)/shard_map/ppermute | solution.py:26
  21.4 36.1 %collective-permute-start.5 = (bf16[272,1024]{1,0:T(8,128)(2,1)S(1)}, bf16[272,1024]{1,0:T(8,128)(2,1)S(1)}, u32[]{:S(2)}, u32[]{:S(2)}) collective-permute-start(bf16[272,1024]{1,0:T(8,128)(2,1)S(1)} %get-tuple-element.41.refs_0_.refs_4_.refs_1_), channel_id=1, source_target_pairs={{0,17},{1,16},{2,19},{3,18},{16,1},{17,0},{18,3},{19,2},{32,49},{3... | collective-permute-start | bytes 1671176 | tf_op jit(solution)/shard_map/ppermute | solution.py:41
  24.0 33.6 %collective-permute-start.4 = (bf16[272,1024]{1,0:T(8,128)(2,1)S(1)}, bf16[272,1024]{1,0:T(8,128)(2,1)S(1)}, u32[]{:S(2)}, u32[]{:S(2)}) collective-permute-start(bf16[272,1024]{1,0:T(8,128)(2,1)S(1)} %get-tuple-element.41.refs_0_.refs_4_.refs_1_), channel_id=1, source_target_pairs={{0,16},{1,17},{2,18},{3,19},{16,0},{17,1},{18,2},{19,3},{32,48},{3... | collective-permute-start | bytes 1671176 | tf_op jit(solution)/shard_map/ppermute | solution.py:41
  24.5 33.0 %collective-permute-start.3 = (bf16[272,1024]{1,0:T(8,128)(2,1)S(1)}, bf16[272,1024]{1,0:T(8,128)(2,1)S(1)}, u32[]{:S(2)}, u32[]{:S(2)}) collective-permute-start(bf16[272,1024]{1,0:T(8,128)(2,1)S(1)} %get-tuple-element.41.refs_0_.refs_4_.refs_1_), channel_id=1, source_target_pairs={{0,1},{1,0},{2,3},{3,2},{16,17},{17,16},{18,19},{19,18},{32,33},{3... | collective-permute-start | bytes 1671176 | tf_op jit(solution)/shard_map/ppermute | solution.py:41
  25.0 0.9 copy-start.16
  28.5 0.8 copy-start.11
  29.3 33.2 %collective-permute-start.2 = (bf16[256,1280]{1,0:T(8,128)(2,1)}, bf16[256,1280]{1,0:T(8,128)(2,1)}, u32[]{:S(2)}, u32[]{:S(2)}) collective-permute-start(bf16[256,1280]{1,0:T(8,128)(2,1)} %get-tuple-element.54), channel_id=1, source_target_pairs={{0,4},{4,0},{8,12},{12,8},{1,5},{5,1},{9,13},{13,9},{2,6},{6,2},{1... | collective-permute-start | bytes 1966088 | tf_op jit(solution)/shard_map/ppermute | solution.py:31
  30.9 7.6 %copy-start.7 = (bf16[64,8,384]{2,1,0:T(8,128)(2,1)}, bf16[64,8,384]{2,1,0:T(8,128)(2,1)S(1)}, u32[]{:S(2)}) copy-start(bf16[64,8,384]{2,1,0:T(8,128)(2,1)S(1)} %all-to-all-done) | copy-start | bytes 1179652
  38.4 1.6 %collective-permute-start.1 = (f32[512,128]{1,0:T(8,128)S(1)}, f32[512,128]{1,0:T(8,128)S(1)}, u32[]{:S(2)}, u32[]{:S(2)}) collective-permute-start(f32[512,128]{1,0:T(8,128)S(1)} %get-tuple-element.50.refs_2_), channel_id=1, source_target_pairs={{0,64},{64,0},{1,65},{65,1},{2,66},{66,2},{3,67},{67,3},{4,68},{68... | collective-permute-start | bytes 786440 | tf_op jit(solution)/shard_map/ppermute | solution.py:26
  46.4 0.7 copy-start.15
  47.1 21.0 %copy-start.21 = (s32[2,128]{1,0:T(2,128)S(1)}, s32[2,128]{1,0:T(2,128)}, u32[]{:S(2)}) copy-start(s32[2,128]{1,0:T(2,128)} %get-tuple-element.40.refs_4_.refs_0_) | copy-start | bytes 3076
  47.1 21.0 %all-to-all-start.1 = ((bf16[64,8,256]{2,1,0:T(8,128)(2,1)}), bf16[64,8,256]{2,1,0:T(8,128)(2,1)S(1)}, u32[]{:S(2)}, u32[]{:S(2)}) async-start(bf16[64,8,256]{2,1,0:T(8,128)(2,1)} %bitcast.3), calls=%async_computation.1 | async-start | bytes 524288 | tf_op jit(solution)/shard_map/all_to_all | solution.py:626
  57.3 14.1 %collective-permute-start.7 = (f32[256,256]{1,0:T(8,128)S(1)}, f32[256,256]{1,0:T(8,128)}, u32[]{:S(2)}, u32[]{:S(2)}) collective-permute-start(f32[256,256]{1,0:T(8,128)S(1)} %get-tuple-element.57), channel_id=1, source_target_pairs={{0,64},{64,0},{1,65},{65,1},{2,66},{66,2},{3,67},{67,3},{4,68},{68... | collective-permute-start | bytes 786440 | tf_op jit(solution)/shard_map/ppermute | solution.py:26
  58.2 0.8 copy-start.1
  62.5 19.2 %copy-start = (bf16[512,1024]{1,0:T(8,128)(2,1)S(1)}, bf16[512,1024]{1,0:T(8,128)(2,1)}, u32[]{:S(2)}) copy-start(bf16[512,1024]{1,0:T(8,128)(2,1)} %refs_4_.1) | copy-start | bytes 3145732
  62.5 1.2 copy-start.12
  63.7 0.7 copy-start.17
  66.0 0.7 copy-start.13
  66.7 0.7 copy-start.22
  68.2 13.5 %copy-start.14 = (bf16[64,16,128]{2,1,0:T(8,128)(2,1)S(1)}, bf16[64,16,128]{2,1,0:T(8,128)(2,1)}, u32[]{:S(2)}) copy-start(bf16[64,16,128]{2,1,0:T(8,128)(2,1)} %copy-done.13) | copy-start | bytes 786436
  68.5 3.8 %collective-permute-start.6 = (f32[256,256]{1,0:T(8,128)S(1)}, f32[256,256]{1,0:T(8,128)S(1)}, u32[]{:S(2)}, u32[]{:S(2)}) collective-permute-start(f32[256,256]{1,0:T(8,128)S(1)} %rows.1.refs_0_), channel_id=1, source_target_pairs={{0,64},{64,0},{1,65},{65,1},{2,66},{66,2},{3,67},{67,3},{4,68},{68... | collective-permute-start | bytes 786440 | tf_op jit(solution)/shard_map/ppermute | solution.py:26
  68.6 12.3 %collective-permute-start.11 = (bf16[64,16,128]{2,1,0:T(8,128)(2,1)}, bf16[64,16,128]{2,1,0:T(8,128)(2,1)S(1)}, u32[]{:S(2)}, u32[]{:S(2)}) collective-permute-start(bf16[64,16,128]{2,1,0:T(8,128)(2,1)} %copy-done.22), channel_id=1, source_target_pairs={{0,8},{4,12},{8,0},{12,4},{1,9},{5,13},{9,1},{13,5},{2,10},{6,14},... | collective-permute-start | bytes 786440 | tf_op jit(solution)/shard_map/ppermute | solution.py:31
  72.4 8.5 %collective-permute-start.8 = (bf16[256,256]{1,0:T(8,128)(2,1)S(1)}, bf16[256,256]{1,0:T(8,128)(2,1)S(1)}, u32[]{:S(2)}, u32[]{:S(2)}) collective-permute-start(bf16[256,256]{1,0:T(8,128)(2,1)S(1)} %row_grad.1.refs_5_.refs_0_.refs_2_), channel_id=1, source_target_pairs={{0,1},{1,0},{2,3},{3,2},{16,17},{17,16},{18,19},{19,18},{32,33},{3... | collective-permute-start | bytes 393224 | tf_op jit(solution)/shard_map/ppermute | solution.py:41
  73.9 7.8 %collective-permute-start.9 = (bf16[256,256]{1,0:T(8,128)(2,1)S(1)}, bf16[256,256]{1,0:T(8,128)(2,1)S(1)}, u32[]{:S(2)}, u32[]{:S(2)}) collective-permute-start(bf16[256,256]{1,0:T(8,128)(2,1)S(1)} %row_grad.1.refs_5_.refs_0_.refs_2_), channel_id=1, source_target_pairs={{0,16},{1,17},{2,18},{3,19},{16,0},{17,1},{18,2},{19,3},{32,48},{3... | collective-permute-start | bytes 393224 | tf_op jit(solution)/shard_map/ppermute | solution.py:41
  75.4 6.3 %collective-permute-start.10 = (bf16[256,256]{1,0:T(8,128)(2,1)S(1)}, bf16[256,256]{1,0:T(8,128)(2,1)S(1)}, u32[]{:S(2)}, u32[]{:S(2)}) collective-permute-start(bf16[256,256]{1,0:T(8,128)(2,1)S(1)} %row_grad.1.refs_5_.refs_0_.refs_2_), channel_id=1, source_target_pairs={{0,17},{1,16},{2,19},{3,18},{16,1},{17,0},{18,3},{19,2},{32,49},{3... | collective-permute-start | bytes 393224 | tf_op jit(solution)/shard_map/ppermute | solution.py:41
  75.9 1.1 copy-start.2
  77.0 1.2 %copy-start.10 = (bf16[1024,512]{1,0:T(8,128)(2,1)S(1)}, bf16[1024,512]{1,0:T(8,128)(2,1)}, u32[]{:S(2)}) copy-start(bf16[1024,512]{1,0:T(8,128)(2,1)} %get-tuple-element.58.refs_4_) | copy-start | bytes 3145732
  81.7 1.0 copy-start.3
  87.5 31.7 %all-to-all-start.2 = ((bf16[64,16,768]{2,1,0:T(8,128)(2,1)}), bf16[64,16,768]{2,1,0:T(8,128)(2,1)S(1)}, u32[]{:S(2)}, u32[]{:S(2)}) async-start(bf16[64,16,768]{2,1,0:T(8,128)(2,1)} %weight_parts.1.refs_6_.refs_2_), calls=%async_computation.2 | async-start | bytes 3145728 | tf_op jit(solution)/shard_map/all_to_all | solution.py:701
  95.9 3.1 %copy-start.4 = (bf16[1024,256]{1,0:T(8,128)(2,1)S(1)}, bf16[1024,256]{1,0:T(8,128)(2,1)}, u32[]{:S(2)}) copy-start(bf16[1024,256]{1,0:T(8,128)(2,1)} %refs_3_.3) | copy-start | bytes 1572868
  95.9 3.1 %copy-start.19 = (s32[2,1,4]{2,1,0:T(1,128)S(1)}, s32[2,1,4]{2,1,0:T(1,128)}, u32[]{:S(2)}) copy-start(s32[2,1,4]{2,1,0:T(1,128)} %refs_0_.8) | copy-start | bytes 100
  105.2 7.4 %collective-permute-start.12 = (f32[256,1024]{1,0:T(8,128)S(1)}, f32[256,1024]{1,0:T(8,128)S(1)}, u32[]{:S(2)}, u32[]{:S(2)}) collective-permute-start(f32[256,1024]{1,0:T(8,128)S(1)} %get-tuple-element.70.refs_2_), channel_id=1, source_target_pairs={{0,64},{64,0},{1,65},{65,1},{2,66},{66,2},{3,67},{67,3},{4,68},{68... | collective-permute-start | bytes 3145736 | tf_op jit(solution)/shard_map/ppermute | solution.py:26
  105.3 7.4 %copy-start.6 = (bf16[2,128,1024]{2,1,0:T(8,128)(2,1)S(1)}, bf16[2,128,1024]{2,1,0:T(8,128)(2,1)}, u32[]{:S(2)}) copy-start(bf16[2,128,1024]{2,1,0:T(8,128)(2,1)} %refs_0_.9) | copy-start | bytes 1572868

commit v8 on v7

--- a/solution.py
+++ b/solution.py
@@ -593,6 +593,7 @@
     )
     got = lax.all_to_all(sent.reshape(owners, slots // owners, -1), DEV, 0, 0, tiled=True).reshape(slots, -1)
 
+    late_inputs, late_saved, _ = lax.optimization_barrier((inputs, saved, slot_ids))
     normed, logits, stats, table = call(
         functools.partial(first_kernel, PARTS, owners),
         "norms_and_logits",
@@ -602,10 +603,9 @@
             ((total, 128), f32),
             (top_table.shape, bf16),
         ],
-        (lengths, inputs, saved, top_table),
+        (lengths, late_inputs, late_saved, top_table),
         "SHHH VVVV",
         limit=FIRST_LIMIT,
-        after=(slot_ids,),
     )
     normed_all = [normed] + [from_member(normed, s) for s in range(1, group)]
     row_top, *top_grads, top_token = call(

time: 121 us -> 121 us (level)
    unnamed x46 -> x44, local copies, waits for them, and re-layouts: 14.3 us -> 13.7 us
  transfers between devices with their start and end apart: 16 -> 16, of which waited for: 4 -> 4; matrix products, arithmetic and copies ran while one was open for 4% -> 4% of each run, Pallas kernels for 34% -> 35%
where the time goes in v8:
time: 121 us; the launch traced here: 120 us
  Pallas kernels  50 us (41%)
  starting transfers between devices  42 us (35%)
  local copies, waits for them, and re-layouts  16.8 us (14%)
  waiting for transfers between devices  8.2 us (7%)
  other arithmetic  1.57 us (1%)
    pallas_call x15, Pallas kernels, call(): pl.pallas_call(run, in_specs=[pl.BlockSpec(memory_space=spaces[k]) for k...  50 us
    unnamed x44, local copies, waits for them, and re-layouts  13.7 us
    all_to_all x1, starting transfers between devices, body(): lax.all_to_all(sent.reshape(owners, slots // owners, -1), DEV, 0, 0, tile...  11.5 us
    all_to_all x1, starting transfers between devices, body(): lax.all_to_all(back.reshape(owners, slots // owners, width), DEV, 0, 0, t...  10.1 us
    all_to_all x1, starting transfers between devices, body(): arrived = lax.all_to_all(packed, DEV, 0, 0, tiled=True)  8.34 us
    ppermute x6, starting transfers between devices, from_member(): lax.ppermute(part, ('y', 'x'), [(i, i ^ flip) for i in range(lax.axis_siz...  7.14 us
    all_to_all x1, waiting for transfers between devices, body(): arrived = lax.all_to_all(packed, DEV, 0, 0, tiled=True)  5.03 us
    ppermute x2, starting transfers between devices, from_pair(): return lax.ppermute(part, axis, [(i, i ^ other) for i in range(count)])  4.36 us
  transfers between devices with their start and end apart: 16, of which 4 were waited for; matrix products, arithmetic and copies ran while one was open for 4% of the time, Pallas kernels for 35%

profile of v8, /device:TPU:0, one launch (start us, length us, event | category | flops | bytes accessed | tf_op | source)
XLA Modules:
  0.0 119.8 jit_solution(1874577685495806446)
XLA Ops:
  0.6 2.9 %dispatch.1 = (bf16[512,384]{1,0:T(8,128)(2,1)}, s32[2,128]{1,0:T(2,128)}, f32[256,128]{1,0:T(8,128)}) custom-call(s32[2,128]{1,0:T(2,128)} %refs_0_.5, s32[2,128]{1,0:T(2,128)} %refs_1_.2, bf16[2,128,256]{2,1,0:T(8,128)(2,1)} %refs_2_.1), custom_call_target="tpu_custom_call" | custom-call | tf_op jit(solution)/shard_map/dispatch/pallas_call | solution.py:106
  3.5 11.5 %all-to-all-start = ((bf16[64,8,384]{2,1,0:T(8,128)(2,1)}), bf16[64,8,384]{2,1,0:T(8,128)(2,1)S(1)}, u32[]{:S(2)}, u32[]{:S(2)}) async-start(bf16[64,8,384]{2,1,0:T(8,128)(2,1)} %bitcast.15), calls=%async_computation | async-start | bytes 786432 | tf_op jit(solution)/shard_map/all_to_all | solution.py:594
  15.1 1.0 copy-done.5
  16.1 0.9 copy-done.8
  17.0 1.2 %copy-done.9 = bf16[2048,256]{1,0:T(8,128)(2,1)S(1)} copy-done((bf16[2048,256]{1,0:T(8,128)(2,1)S(1)}, bf16[2048,256]{1,0:T(8,128)(2,1)}, u32[]{:S(2)}) %copy-start.9) | copy-done | bytes 1048600
  18.2 0.7 copy-done.18
  18.9 1.8 %norms_and_logits.1 = (bf16[272,1024]{1,0:T(8,128)(2,1)S(1)}, f32[256,2048]{1,0:T(8,128)S(1)}, f32[256,128]{1,0:T(8,128)S(1)}, bf16[2048,256]{1,0:T(8,128)(2,1)S(1)}) custom-call(s32[2,1,4]{2,1,0:T(1,128)S(1)} %copy-done.18, bf16[2,128,1024]{2,1,0:T(8,128)(2,1)S(1)} %copy-done.5, bf16[256,256]{1,0:T(8,128)(2,1)S(1)} %bitcast.12, bf16[2048,256]{1,0:T(8,128)(2,1)S(1)} %copy-done.9), custom_call_target="tpu_custom_call" | custom-call | tf_op jit(solution)/shard_map/norms_and_logits/pallas_call | solution.py:106
  20.8 2.6 %collective-permute-start.5 = (bf16[272,1024]{1,0:T(8,128)(2,1)S(1)}, bf16[272,1024]{1,0:T(8,128)(2,1)S(1)}, u32[]{:S(2)}, u32[]{:S(2)}) collective-permute-start(bf16[272,1024]{1,0:T(8,128)(2,1)S(1)} %get-tuple-element.45.refs_0_.refs_4_.refs_1_), channel_id=1, source_target_pairs={{0,17},{1,16},{2,19},{3,18},{16,1},{17,0},{18,3},{19,2},{32,49},{3... | collective-permute-start | bytes 1671176 | tf_op jit(solution)/shard_map/ppermute | solution.py:41
  23.4 0.6 collective-permute-start.4
  24.0 0.4 collective-permute-start.3
  24.4 0.9 copy-done.16
  25.3 2.6 %top_grads.1 = (f32[256,256]{1,0:T(8,128)S(1)}, bf16[256,1280]{1,0:T(8,128)(2,1)S(1)}, bf16[256,1280]{1,0:T(8,128)(2,1)}, f32[8,128]{1,0:T(8,128)S(1)}) custom-call(f32[256,2048]{1,0:T(8,128)S(1)} %get-tuple-element.47.refs_0_, f32[256,128]{1,0:T(8,128)S(1)} %get-tuple-element.48.refs_1_, f32[256,128]{1,0:T(8,128)S(1)} %collective-permute-done.refs_2_, ...), custom_call_target="tpu_custom_call" | custom-call | tf_op jit(solution)/shard_map/top_grads/pallas_call | solution.py:106
  27.9 0.8 copy-done.11
  28.8 1.6 %collective-permute-start.2 = (bf16[256,1280]{1,0:T(8,128)(2,1)}, bf16[256,1280]{1,0:T(8,128)(2,1)}, u32[]{:S(2)}, u32[]{:S(2)}) collective-permute-start(bf16[256,1280]{1,0:T(8,128)(2,1)} %get-tuple-element.58), channel_id=1, source_target_pairs={{0,4},{4,0},{8,12},{12,8},{1,5},{5,1},{9,13},{13,9},{2,6},{6,2},{1... | collective-permute-start | bytes 1966088 | tf_op jit(solution)/shard_map/ppermute | solution.py:31
  30.4 7.5 %leaf_scores.1 = (f32[512,256]{1,0:T(8,128)S(1)}, f32[512,128]{1,0:T(8,128)S(1)}, bf16[512,384]{1,0:T(8,128)(2,1)S(1)}, bf16[64,256,256]{2,1,0:T(8,128)(2,1)S(1)}) custom-call(bf16[512,384]{1,0:T(8,128)(2,1)S(1)} %bitcast.10, bf16[64,256,256]{2,1,0:T(8,128)(2,1)} %refs_1_.4, f32[8,128]{1,0:T(8,128)S(1)} %get-tuple-element.51.refs_2_, ...), custom_call_target="tpu_custom_call" | custom-call | flops 4294967296 | tf_op jit(solution)/shard_map/leaf_scores/pallas_call | solution.py:106
  38.0 1.5 %collective-permute-done.1.refs_3_ = f32[512,128]{1,0:T(8,128)S(1)} collective-permute-done((f32[512,128]{1,0:T(8,128)S(1)}, f32[512,128]{1,0:T(8,128)S(1)}, u32[]{:S(2)}, u32[]{:S(2)}) %collective-permute-start.1) | collective-permute-done | bytes 262176 | tf_op jit(solution)/shard_map/ppermute | solution.py:26
  39.6 6.4 %leaf_back.1 = (bf16[512,256]{1,0:T(8,128)(2,1)}, bf16[512,256]{1,0:T(8,128)(2,1)S(1)}) custom-call(bf16[512,384]{1,0:T(8,128)(2,1)S(1)} %get-tuple-element.52.refs_0_, f32[512,256]{1,0:T(8,128)S(1)} %get-tuple-element.53.refs_1_, f32[512,128]{1,0:T(8,128)S(1)} %get-tuple-element.54.refs_2_, f32[512,128]{1,0:T(8,128)S(1)} %collective-permute-done.1.refs_3_, ...), custom_call_target="tpu_custom_call" | custom-call | tf_op jit(solution)/shard_map/leaf_back/pallas_call | solution.py:106
  46.0 0.7 copy-done.15
  46.7 10.1 %all-to-all-start.1 = ((bf16[64,8,256]{2,1,0:T(8,128)(2,1)}), bf16[64,8,256]{2,1,0:T(8,128)(2,1)S(1)}, u32[]{:S(2)}, u32[]{:S(2)}) async-start(bf16[64,8,256]{2,1,0:T(8,128)(2,1)} %bitcast.3), calls=%async_computation.1 | async-start | bytes 524288 | tf_op jit(solution)/shard_map/all_to_all | solution.py:626
  56.7 0.3 collective-permute-start.7
  57.0 0.6 slice_add_fusion.refs_2_
  57.6 0.8 copy-done.1
  58.4 3.5 %head_weight.1 = (bf16[1024,512]{1,0:T(8,128)(2,1)}, f32[8,128]{1,0:T(8,128)}) custom-call(bf16[1024,4,512]{2,1,0:T(4,128)(2,1)} %refs_0_.7, bf16[512,256]{1,0:T(8,128)(2,1)} %get-tuple-element.56.refs_1_.refs_2_, bf16[8,128]{1,0:T(8,128)(2,1)} %slice_add_fusion.refs_2_), custom_call_target="tpu_custom_call" | custom-call | tf_op jit(solution)/shard_map/head_weight/pallas_call | solution.py:106
  61.9 1.2 copy-done.12
  63.1 0.7 copy-done.17
  63.8 1.6 %table_part.1 = (bf16[64,16,128]{2,1,0:T(8,128)(2,1)S(1)}, bf16[64,16,128]{2,1,0:T(8,128)(2,1)S(1)}, f32[8,128]{1,0:T(8,128)S(1)}) custom-call(bf16[256,1280]{1,0:T(8,128)(2,1)S(1)} %copy-done.12, bf16[256,1280]{1,0:T(8,128)(2,1)} %collective-permute-done.2.refs_1_, bf16[512,256]{1,0:T(8,128)(2,1)} %get-tuple-element.56.refs_1_.refs_2_, f32[8,128]{1,0:T(8,128)S(1)} %copy-done.17), custom_call_target="tpu_custom_call" | custom-call | tf_op jit(solution)/shard_map/table_part/pallas_call | solution.py:106
  65.4 0.7 copy-done.13
  66.1 0.7 copy-done.21
  66.8 0.8 all-to-all-done.1
  67.6 0.3 rows.1.refs_0_
  68.0 2.8 %collective-permute-start.11 = (bf16[64,16,128]{2,1,0:T(8,128)(2,1)}, bf16[64,16,128]{2,1,0:T(8,128)(2,1)S(1)}, u32[]{:S(2)}, u32[]{:S(2)}) collective-permute-start(bf16[64,16,128]{2,1,0:T(8,128)(2,1)} %copy-done.21), channel_id=1, source_target_pairs={{0,8},{4,12},{8,0},{12,4},{1,9},{5,13},{9,1},{13,5},{2,10},{6,14},... | collective-permute-start | bytes 786440 | tf_op jit(solution)/shard_map/ppermute | solution.py:31
  70.8 1.0 add.11.refs_2_
  71.8 1.5 %collective-permute-start.8 = (bf16[256,256]{1,0:T(8,128)(2,1)S(1)}, bf16[256,256]{1,0:T(8,128)(2,1)S(1)}, u32[]{:S(2)}, u32[]{:S(2)}) collective-permute-start(bf16[256,256]{1,0:T(8,128)(2,1)S(1)} %row_grad.1.refs_5_.refs_0_.refs_2_), channel_id=1, source_target_pairs={{0,1},{1,0},{2,3},{3,2},{16,17},{17,16},{18,19},{19,18},{32,33},{3... | collective-permute-start | bytes 393224 | tf_op jit(solution)/shard_map/ppermute | solution.py:41
  73.4 1.5 %collective-permute-start.9 = (bf16[256,256]{1,0:T(8,128)(2,1)S(1)}, bf16[256,256]{1,0:T(8,128)(2,1)S(1)}, u32[]{:S(2)}, u32[]{:S(2)}) collective-permute-start(bf16[256,256]{1,0:T(8,128)(2,1)S(1)} %row_grad.1.refs_5_.refs_0_.refs_2_), channel_id=1, source_target_pairs={{0,16},{1,17},{2,18},{3,19},{16,0},{17,1},{18,2},{19,3},{32,48},{3... | collective-permute-start | bytes 393224 | tf_op jit(solution)/shard_map/ppermute | solution.py:41
  74.9 0.5 collective-permute-start.10
  75.4 1.1 copy-done.2
  76.5 1.2 %copy-done.10 = bf16[1024,512]{1,0:T(8,128)(2,1)S(1)} copy-done((bf16[1024,512]{1,0:T(8,128)(2,1)S(1)}, bf16[1024,512]{1,0:T(8,128)(2,1)}, u32[]{:S(2)}) %copy-start.10) | copy-done | bytes 1048600
  77.7 2.6 %group_forward.1 = (bf16[1024,512]{1,0:T(8,128)(2,1)S(1)}, f32[1024,512]{1,0:T(8,128)S(1)}, bf16[1024,128]{1,0:T(8,128)(2,1)S(1)}, f32[1024,128]{1,0:T(8,128)S(1...) custom-call(bf16[272,1024]{1,0:T(8,128)(2,1)S(1)} %get-tuple-element.45.refs_0_.refs_4_.refs_1_, ...), custom_call_target="tpu_custom_call" | custom-call | tf_op jit(solution)/shard_map/group_forward/pallas_call | solution.py:106
  80.3 0.8 collective-permute-done.9.refs_2_
  81.2 1.0 copy-done.3
  82.2 4.8 %weight_parts.1.refs_6_.refs_2_ = bf16[64,16,768]{2,1,0:T(8,128)(2,1)} custom-call(bf16[256,256]{1,0:T(8,128)(2,1)S(1)} %row_grad.1.refs_5_.refs_0_.refs_2_, bf16[256,256]{1,0:T(8,128)(2,1)S(1)} %collective-permute-done.8.refs_1_, bf16[256,256]{1,0:T(8,128)(2,1)S(1)} %collective-permute-done.9.refs_2_, bf16[256,256]{1,0:T(8,128)(2,1)S(1)} %collective-permute-done.10.refs_3_, ...), custom_call_target="tpu_custom_call" | custom-call | tf_op jit(solution)/shard_map/weight_parts/pallas_call | solution.py:106
  87.0 8.3 %all-to-all-start.2 = ((bf16[64,16,768]{2,1,0:T(8,128)(2,1)}), bf16[64,16,768]{2,1,0:T(8,128)(2,1)S(1)}, u32[]{:S(2)}, u32[]{:S(2)}) async-start(bf16[64,16,768]{2,1,0:T(8,128)(2,1)} %weight_parts.1.refs_6_.refs_2_), calls=%async_computation.2 | async-start | bytes 3145728 | tf_op jit(solution)/shard_map/all_to_all | solution.py:701
  95.4 3.1 %copy.17 = bf16[1024,4,512]{2,0,1:T(8,128)(2,1)S(1)} copy(bf16[1024,4,512]{2,1,0:T(4,128)(2,1)} %refs_0_.7) | data formatting | bytes 8388608 | tf_op jit(solution)/shard_map/optimization_barrier | solution.py:703
  98.5 6.2 %trunk.1 = (bf16[256,1024]{1,0:T(8,128)(2,1)S(1)}, f32[256,1024]{1,0:T(8,128)S(1)}) custom-call(s32[2,1,4]{2,1,0:T(1,128)S(1)} %copy-done.19, bf16[272,1024]{1,0:T(8,128)(2,1)S(1)} %get-tuple-element.45.refs_0_.refs_4_.refs_1_, bf16[256,256]{1,0:T(8,128)(2,1)S(1)} %row_grad.1.refs_5_.refs_0_.refs_2_, bf16[1024,256]{1,0:T(8,128)(2,1)S(1)} %copy-done.4, ...), custom_call_target="tpu_custom_call" | custom-call | tf_op jit(solution)/shard_map/trunk/pallas_call | solution.py:106
  104.8 7.3 %leaf_book.1 = bf16[64,256,256]{2,1,0:T(8,128)(2,1)} custom-call(bf16[512,384]{1,0:T(8,128)(2,1)} %bitcast.11, bf16[512,256]{1,0:T(8,128)(2,1)} %copy-done.15, bf16[64,16,768]{2,1,0:T(8,128)(2,1)} %weight_parts.1.refs_6_.refs_2_), custom_call_target="tpu_custom_call" | custom-call | tf_op jit(solution)/shard_map/leaf_book/pallas_call | solution.py:106
  112.1 1.5 %input_grads.1 = bf16[2,128,1024]{2,1,0:T(8,128)(2,1)} custom-call(bf16[2,128,1024]{2,1,0:T(8,128)(2,1)S(1)} %copy-done.6, bf16[256,1024]{1,0:T(8,128)(2,1)S(1)} %get-tuple-element.73.refs_1_, f32[256,1024]{1,0:T(8,128)S(1)} %get-tuple-element.74.refs_2_, f32[256,1024]{1,0:T(8,128)S(1)} %collective-permute-done.12.refs_3_), custom_call_target="tpu_custom_call" | custom-call | tf_op jit(solution)/shard_map/input_grads/pallas_call | solution.py:106
  113.6 5.0 %all-to-all-done.2.refs_0_ = bf16[64,16,768]{2,1,0:T(8,128)(2,1)S(1)} async-done(((bf16[64,16,768]{2,1,0:T(8,128)(2,1)}), bf16[64,16,768]{2,1,0:T(8,128)(2,1)S(1)}, u32[]{:S(2)}, u32[]{:S(2)}) %all-to-all-start.2) | async-done | bytes 1572896 | tf_op jit(solution)/shard_map/all_to_all | solution.py:701
  118.7 0.9 weight_sums.1
  (47 shorter events, 0.5 us)
Async XLA Ops:
  3.5 26.9 %all-to-all-start = ((bf16[64,8,384]{2,1,0:T(8,128)(2,1)}), bf16[64,8,384]{2,1,0:T(8,128)(2,1)S(1)}, u32[]{:S(2)}, u32[]{:S(2)}) async-start(bf16[64,8,384]{2,1,0:T(8,128)(2,1)} %bitcast.15), calls=%async_computation | async-start | bytes 786432 | tf_op jit(solution)/shard_map/all_to_all | solution.py:594
  15.0 1.0 copy-start.5
  16.1 0.9 copy-start.8
  17.0 1.2 %copy-start.9 = (bf16[2048,256]{1,0:T(8,128)(2,1)S(1)}, bf16[2048,256]{1,0:T(8,128)(2,1)}, u32[]{:S(2)}) copy-start(bf16[2048,256]{1,0:T(8,128)(2,1)} %refs_3_.2) | copy-start | bytes 3145732
  18.2 0.7 copy-start.18
  20.7 3.7 %collective-permute-start = (f32[256,128]{1,0:T(8,128)S(1)}, f32[256,128]{1,0:T(8,128)S(1)}, u32[]{:S(2)}, u32[]{:S(2)}) collective-permute-start(f32[256,128]{1,0:T(8,128)S(1)} %get-tuple-element.48.refs_1_), channel_id=1, source_target_pairs={{0,64},{64,0},{1,65},{65,1},{2,66},{66,2},{3,67},{67,3},{4,68},{68... | collective-permute-start | bytes 393224 | tf_op jit(solution)/shard_map/ppermute | solution.py:26
  20.8 36.2 %collective-permute-start.5 = (bf16[272,1024]{1,0:T(8,128)(2,1)S(1)}, bf16[272,1024]{1,0:T(8,128)(2,1)S(1)}, u32[]{:S(2)}, u32[]{:S(2)}) collective-permute-start(bf16[272,1024]{1,0:T(8,128)(2,1)S(1)} %get-tuple-element.45.refs_0_.refs_4_.refs_1_), channel_id=1, source_target_pairs={{0,17},{1,16},{2,19},{3,18},{16,1},{17,0},{18,3},{19,2},{32,49},{3... | collective-permute-start | bytes 1671176 | tf_op jit(solution)/shard_map/ppermute | solution.py:41
  23.4 33.6 %collective-permute-start.4 = (bf16[272,1024]{1,0:T(8,128)(2,1)S(1)}, bf16[272,1024]{1,0:T(8,128)(2,1)S(1)}, u32[]{:S(2)}, u32[]{:S(2)}) collective-permute-start(bf16[272,1024]{1,0:T(8,128)(2,1)S(1)} %get-tuple-element.45.refs_0_.refs_4_.refs_1_), channel_id=1, source_target_pairs={{0,16},{1,17},{2,18},{3,19},{16,0},{17,1},{18,2},{19,3},{32,48},{3... | collective-permute-start | bytes 1671176 | tf_op jit(solution)/shard_map/ppermute | solution.py:41
  24.0 33.0 %collective-permute-start.3 = (bf16[272,1024]{1,0:T(8,128)(2,1)S(1)}, bf16[272,1024]{1,0:T(8,128)(2,1)S(1)}, u32[]{:S(2)}, u32[]{:S(2)}) collective-permute-start(bf16[272,1024]{1,0:T(8,128)(2,1)S(1)} %get-tuple-element.45.refs_0_.refs_4_.refs_1_), channel_id=1, source_target_pairs={{0,1},{1,0},{2,3},{3,2},{16,17},{17,16},{18,19},{19,18},{32,33},{3... | collective-permute-start | bytes 1671176 | tf_op jit(solution)/shard_map/ppermute | solution.py:41
  24.4 0.9 copy-start.16
  27.9 0.9 copy-start.11
  28.8 33.2 %collective-permute-start.2 = (bf16[256,1280]{1,0:T(8,128)(2,1)}, bf16[256,1280]{1,0:T(8,128)(2,1)}, u32[]{:S(2)}, u32[]{:S(2)}) collective-permute-start(bf16[256,1280]{1,0:T(8,128)(2,1)} %get-tuple-element.58), channel_id=1, source_target_pairs={{0,4},{4,0},{8,12},{12,8},{1,5},{5,1},{9,13},{13,9},{2,6},{6,2},{1... | collective-permute-start | bytes 1966088 | tf_op jit(solution)/shard_map/ppermute | solution.py:31
  30.4 7.6 %copy-start.7 = (bf16[64,8,384]{2,1,0:T(8,128)(2,1)}, bf16[64,8,384]{2,1,0:T(8,128)(2,1)S(1)}, u32[]{:S(2)}) copy-start(bf16[64,8,384]{2,1,0:T(8,128)(2,1)S(1)} %all-to-all-done) | copy-start | bytes 1179652
  37.9 1.6 %collective-permute-start.1 = (f32[512,128]{1,0:T(8,128)S(1)}, f32[512,128]{1,0:T(8,128)S(1)}, u32[]{:S(2)}, u32[]{:S(2)}) collective-permute-start(f32[512,128]{1,0:T(8,128)S(1)} %get-tuple-element.54.refs_2_), channel_id=1, source_target_pairs={{0,64},{64,0},{1,65},{65,1},{2,66},{66,2},{3,67},{67,3},{4,68},{68... | collective-permute-start | bytes 786440 | tf_op jit(solution)/shard_map/ppermute | solution.py:26
  45.9 0.7 copy-start.15
  46.7 21.0 %copy-start.20 = (s32[2,128]{1,0:T(2,128)S(1)}, s32[2,128]{1,0:T(2,128)}, u32[]{:S(2)}) copy-start(s32[2,128]{1,0:T(2,128)} %get-tuple-element.42.refs_0_) | copy-start | bytes 3076
  46.7 21.0 %all-to-all-start.1 = ((bf16[64,8,256]{2,1,0:T(8,128)(2,1)}), bf16[64,8,256]{2,1,0:T(8,128)(2,1)S(1)}, u32[]{:S(2)}, u32[]{:S(2)}) async-start(bf16[64,8,256]{2,1,0:T(8,128)(2,1)} %bitcast.3), calls=%async_computation.1 | async-start | bytes 524288 | tf_op jit(solution)/shard_map/all_to_all | solution.py:626
  56.7 14.1 %collective-permute-start.7 = (f32[256,256]{1,0:T(8,128)S(1)}, f32[256,256]{1,0:T(8,128)}, u32[]{:S(2)}, u32[]{:S(2)}) collective-permute-start(f32[256,256]{1,0:T(8,128)S(1)} %get-tuple-element.61), channel_id=1, source_target_pairs={{0,64},{64,0},{1,65},{65,1},{2,66},{66,2},{3,67},{67,3},{4,68},{68... | collective-permute-start | bytes 786440 | tf_op jit(solution)/shard_map/ppermute | solution.py:26
  57.6 0.8 copy-start.1
  61.9 19.3 %copy-start = (bf16[512,1024]{1,0:T(8,128)(2,1)S(1)}, bf16[512,1024]{1,0:T(8,128)(2,1)}, u32[]{:S(2)}) copy-start(bf16[512,1024]{1,0:T(8,128)(2,1)} %refs_4_.1) | copy-start | bytes 3145732
  61.9 1.2 copy-start.12
  63.1 0.7 copy-start.17
  65.4 0.7 copy-start.13
  66.1 0.7 copy-start.21
  67.6 13.5 %copy-start.14 = (bf16[64,16,128]{2,1,0:T(8,128)(2,1)S(1)}, bf16[64,16,128]{2,1,0:T(8,128)(2,1)}, u32[]{:S(2)}) copy-start(bf16[64,16,128]{2,1,0:T(8,128)(2,1)} %copy-done.13) | copy-start | bytes 786436
  67.9 3.8 %collective-permute-start.6 = (f32[256,256]{1,0:T(8,128)S(1)}, f32[256,256]{1,0:T(8,128)S(1)}, u32[]{:S(2)}, u32[]{:S(2)}) collective-permute-start(f32[256,256]{1,0:T(8,128)S(1)} %rows.1.refs_0_), channel_id=1, source_target_pairs={{0,64},{64,0},{1,65},{65,1},{2,66},{66,2},{3,67},{67,3},{4,68},{68... | collective-permute-start | bytes 786440 | tf_op jit(solution)/shard_map/ppermute | solution.py:26
  68.0 12.3 %collective-permute-start.11 = (bf16[64,16,128]{2,1,0:T(8,128)(2,1)}, bf16[64,16,128]{2,1,0:T(8,128)(2,1)S(1)}, u32[]{:S(2)}, u32[]{:S(2)}) collective-permute-start(bf16[64,16,128]{2,1,0:T(8,128)(2,1)} %copy-done.21), channel_id=1, source_target_pairs={{0,8},{4,12},{8,0},{12,4},{1,9},{5,13},{9,1},{13,5},{2,10},{6,14},... | collective-permute-start | bytes 786440 | tf_op jit(solution)/shard_map/ppermute | solution.py:31
  71.8 8.5 %collective-permute-start.8 = (bf16[256,256]{1,0:T(8,128)(2,1)S(1)}, bf16[256,256]{1,0:T(8,128)(2,1)S(1)}, u32[]{:S(2)}, u32[]{:S(2)}) collective-permute-start(bf16[256,256]{1,0:T(8,128)(2,1)S(1)} %row_grad.1.refs_5_.refs_0_.refs_2_), channel_id=1, source_target_pairs={{0,1},{1,0},{2,3},{3,2},{16,17},{17,16},{18,19},{19,18},{32,33},{3... | collective-permute-start | bytes 393224 | tf_op jit(solution)/shard_map/ppermute | solution.py:41
  73.4 7.8 %collective-permute-start.9 = (bf16[256,256]{1,0:T(8,128)(2,1)S(1)}, bf16[256,256]{1,0:T(8,128)(2,1)S(1)}, u32[]{:S(2)}, u32[]{:S(2)}) collective-permute-start(bf16[256,256]{1,0:T(8,128)(2,1)S(1)} %row_grad.1.refs_5_.refs_0_.refs_2_), channel_id=1, source_target_pairs={{0,16},{1,17},{2,18},{3,19},{16,0},{17,1},{18,2},{19,3},{32,48},{3... | collective-permute-start | bytes 393224 | tf_op jit(solution)/shard_map/ppermute | solution.py:41
  74.9 6.3 %collective-permute-start.10 = (bf16[256,256]{1,0:T(8,128)(2,1)S(1)}, bf16[256,256]{1,0:T(8,128)(2,1)S(1)}, u32[]{:S(2)}, u32[]{:S(2)}) collective-permute-start(bf16[256,256]{1,0:T(8,128)(2,1)S(1)} %row_grad.1.refs_5_.refs_0_.refs_2_), channel_id=1, source_target_pairs={{0,17},{1,16},{2,19},{3,18},{16,1},{17,0},{18,3},{19,2},{32,49},{3... | collective-permute-start | bytes 393224 | tf_op jit(solution)/shard_map/ppermute | solution.py:41
  75.4 1.1 copy-start.2
  76.5 1.2 %copy-start.10 = (bf16[1024,512]{1,0:T(8,128)(2,1)S(1)}, bf16[1024,512]{1,0:T(8,128)(2,1)}, u32[]{:S(2)}) copy-start(bf16[1024,512]{1,0:T(8,128)(2,1)} %get-tuple-element.62.refs_4_) | copy-start | bytes 3145732
  81.2 1.0 copy-start.3
  87.0 31.7 %all-to-all-start.2 = ((bf16[64,16,768]{2,1,0:T(8,128)(2,1)}), bf16[64,16,768]{2,1,0:T(8,128)(2,1)S(1)}, u32[]{:S(2)}, u32[]{:S(2)}) async-start(bf16[64,16,768]{2,1,0:T(8,128)(2,1)} %weight_parts.1.refs_6_.refs_2_), calls=%async_computation.2 | async-start | bytes 3145728 | tf_op jit(solution)/shard_map/all_to_all | solution.py:701
  95.3 3.1 %copy-start.4 = (bf16[1024,256]{1,0:T(8,128)(2,1)S(1)}, bf16[1024,256]{1,0:T(8,128)(2,1)}, u32[]{:S(2)}) copy-start(bf16[1024,256]{1,0:T(8,128)(2,1)} %refs_3_.3) | copy-start | bytes 1572868
  95.3 3.1 %copy-start.19 = (s32[2,1,4]{2,1,0:T(1,128)S(1)}, s32[2,1,4]{2,1,0:T(1,128)}, u32[]{:S(2)}) copy-start(s32[2,1,4]{2,1,0:T(1,128)} %refs_0_.8) | copy-start | bytes 100
  104.7 7.4 %collective-permute-start.12 = (f32[256,1024]{1,0:T(8,128)S(1)}, f32[256,1024]{1,0:T(8,128)S(1)}, u32[]{:S(2)}, u32[]{:S(2)}) collective-permute-start(f32[256,1024]{1,0:T(8,128)S(1)} %get-tuple-element.74.refs_2_), channel_id=1, source_target_pairs={{0,64},{64,0},{1,65},{65,1},{2,66},{66,2},{3,67},{67,3},{4,68},{68... | collective-permute-start | bytes 3145736 | tf_op jit(solution)/shard_map/ppermute | solution.py:26
  104.7 7.4 %copy-start.6 = (bf16[2,128,1024]{2,1,0:T(8,128)(2,1)S(1)}, bf16[2,128,1024]{2,1,0:T(8,128)(2,1)}, u32[]{:S(2)}) copy-start(bf16[2,128,1024]{2,1,0:T(8,128)(2,1)} %refs_0_.9) | copy-start | bytes 1572868
